TPU v7x, 128 devices: a whole 4x4x4 slice. The times are simulated.
128 devices in a mesh: replica: 8 (over x, core), expert: 16 (over z, y).
Axes of the slice: x: 4, y: 4, z: 4, core: 2. Of those that a mesh axis runs over, the one named last changes fastest.
Arguments:
- tokens: bfloat16 [1024, 3584], P(('replica', 'expert')), may hold values from -6 to 6
- queries: bfloat16 [1024, 36864], P(('replica', 'expert')), may hold values from -360 to 360
- latent_cache: bfloat16 [1024, 128, 576], P(('replica', 'expert')), may hold values from -6 to 6
- new_latent: bfloat16 [1024, 576], P(('replica', 'expert')), may hold values from -6 to 6
- lengths: int32 [1024], P(('replica', 'expert')), may hold values from 1 to 128
- finished: int32 [1024], P(('replica', 'expert')), may hold values 0 or 1
- migrate: int32 [128, 8, 1], P(('replica', 'expert')), may hold values from -1 to 7, as said below
- routes: int32 [2048, 8], P(('replica', 'expert')), may hold values from 0 to 127, all different within a row; in each aligned block of 16 rows (0 to 15, 16 to 31, ...) at most 2 rows name the same one
- route_score: float32 [2048, 8], P(('replica', 'expert')), may hold values from 0.05 to 1
- w_gate: bfloat16 [128, 3584, 1024], P(('replica', 'expert')), may hold values from -0.09375 to 0.09375
- w_up: bfloat16 [128, 3584, 1024], P(('replica', 'expert')), may hold values from -0.09375 to 0.09375
- w_down: bfloat16 [128, 1024, 3584], P(('replica', 'expert')), may hold values from -0.1875 to 0.1875
Outputs:
- attended: bfloat16 [2048, 32768], P(('replica', 'expert'))
- expert_out: bfloat16 [2048, 3584], P(('replica', 'expert'))
Inputs may be any that keep to these rules, and one draw needn't show every extreme that they name: migrate[v, d, m] is a row of device v sent to the device of replica d with v's expert index, or -1 for none; a device names none of its rows twice and sends nothing to its own replica. `routes`: among the 16 work slots of one device no expert is named more than 2 times.
All inputs are finite; a program needn't handle non-finite values. No bound on the sum of `finished` on one device may be relied on, other than what follows from the above.
Results may differ from a plain program's by a relative error of at most 0.007.
Values may be sent and summed in bfloat16 or wider, within the bound.
No kernel may reach another device: no remote copies, remote signals or barrier semaphores. Data moves between devices by JAX's collectives and lax.ppermute only.
A program may use at most 128 MiB of HBM per device.

v0:
```python
import jax
import jax.numpy as jnp
from jax import lax
from jax.sharding import PartitionSpec as P

HEADS = 64
VDIM = 512
LAT = 576


score_scale = 192.0 ** (-0.5)


def attend(query_rows, latent_rows, own_latent, live_length):
    row_count = query_rows.shape[0]
    per_head = query_rows.reshape(row_count, HEADS, LAT)
    scores = (
        jnp.einsum("nhl,ntl->nht", per_head, latent_rows, preferred_element_type=jnp.float32)
        * score_scale
    )
    own_score = (
        jnp.einsum("nhl,nl->nh", per_head, own_latent, preferred_element_type=jnp.float32)
        * score_scale
    )
    visible = (
        lax.broadcasted_iota(jnp.int32, (1, 1, latent_rows.shape[1]), 2)
        < live_length[:, None, None]
    )
    scores = jnp.where(visible, scores, -jnp.inf)
    largest = jnp.maximum(jnp.max(scores, axis=2), own_score)
    weights = jnp.exp(scores - largest[:, :, None])
    own_weight = jnp.exp(own_score - largest)
    denominator = jnp.sum(weights, axis=2) + own_weight
    context = jnp.einsum(
        "nht,ntv->nhv",
        weights.astype(jnp.bfloat16),
        latent_rows[:, :, :VDIM],
        preferred_element_type=jnp.float32,
    )
    own_rounded = lax.optimization_barrier(own_weight.astype(jnp.bfloat16)).astype(jnp.float32)
    context = context + own_rounded[:, :, None] * own_latent[:, None, :VDIM].astype(jnp.float32)
    normalized = (
        context / denominator[:, :, None] * (live_length > 0).astype(jnp.float32)[:, None, None]
    )
    return normalized.astype(jnp.bfloat16).reshape(row_count, HEADS * VDIM)


def to_buffer(values, replicas):
    return values.reshape((replicas, -1) + values.shape[1:])


def from_buffer(values):
    return values.reshape((-1,) + values.shape[2:])


def expert_rows(arrived_rows, w_gate, w_up, w_down):
    flat_rows = arrived_rows.reshape(-1, arrived_rows.shape[-1])
    gate_value = jnp.dot(flat_rows, w_gate[0], preferred_element_type=jnp.float32)
    up_value = jnp.dot(flat_rows, w_up[0], preferred_element_type=jnp.float32)
    hidden = (jax.nn.silu(gate_value) * up_value).astype(jnp.bfloat16)
    output = jnp.dot(hidden, w_down[0], preferred_element_type=jnp.float32).astype(jnp.bfloat16)
    return output.reshape(arrived_rows.shape)


def on_device(
    tokens,
    queries,
    latent_cache,
    new_latent,
    lengths,
    finished,
    migrate,
    routes,
    route_score,
    w_gate,
    w_up,
    w_down,
):
    local_count = tokens.shape[0]
    replicas = lax.axis_size("replica")
    columns = lax.axis_size("expert")
    plan_rows = migrate[0].reshape(-1)
    sending = plan_rows >= 0
    picked = jnp.maximum(plan_rows, 0)
    moved_out = jnp.any(
        (plan_rows[:, None] == jnp.arange(local_count)[None, :]) & sending[:, None], axis=0
    )
    own_length = jnp.where(finished == 0, lengths, 0)
    local_length = jnp.where(moved_out, 0, own_length)
    send_length = jnp.where(sending, own_length[picked], 0).astype(jnp.bfloat16)
    send_tokens = jnp.where(sending[:, None], tokens[picked], jnp.zeros_like(tokens[:1]))
    send_cache = jnp.where(
        sending[:, None, None], latent_cache[picked], jnp.zeros_like(latent_cache[:1])
    )
    send_query = jnp.where(sending[:, None], queries[picked], jnp.zeros_like(queries[:1]))
    send_new = jnp.where(sending[:, None], new_latent[picked], jnp.zeros_like(new_latent[:1]))
    arrived = (
        lax.all_to_all(
            to_buffer(send_cache, replicas), "replica", split_axis=0, concat_axis=0, tiled=True
        ),
        lax.all_to_all(
            to_buffer(send_query, replicas), "replica", split_axis=0, concat_axis=0, tiled=True
        ),
        lax.all_to_all(
            to_buffer(send_new, replicas), "replica", split_axis=0, concat_axis=0, tiled=True
        ),
        lax.all_to_all(
            to_buffer(send_tokens, replicas), "replica", split_axis=0, concat_axis=0, tiled=True
        ),
        lax.all_to_all(
            to_buffer(send_length, replicas), "replica", split_axis=0, concat_axis=0, tiled=True
        ),
    )
    in_cache = from_buffer(arrived[0])
    in_query = from_buffer(arrived[1])
    in_new = from_buffer(arrived[2])
    in_tokens = from_buffer(arrived[3])
    in_length = from_buffer(arrived[4]).astype(jnp.int32)
    local_result = attend(queries, latent_cache, new_latent, local_length)
    in_result = attend(in_query, in_cache, in_new, in_length)
    attended = jnp.concatenate([local_result, in_result], axis=0)
    living = jnp.concatenate([local_length > 0, in_length > 0], axis=0)
    work_tokens = jnp.concatenate([tokens, in_tokens], axis=0)
    work_tokens = jnp.where(living[:, None], work_tokens, jnp.zeros_like(work_tokens[:1]))
    work_count, top_count = routes.shape
    expert_count = replicas * columns
    capacity = (work_count * top_count + expert_count - 1) // expert_count + 1
    combine = (
        2.5
        * route_score
        / jnp.sum(route_score, axis=1, keepdims=True)
        * living[:, None].astype(jnp.float32)
    )
    chosen_expert = routes.reshape(-1)
    pair_alive = jnp.repeat(living, top_count)
    matches = (
        (chosen_expert[:, None] == jnp.arange(expert_count)[None, :]) & pair_alive[:, None]
    ).astype(jnp.int32)
    position = jnp.sum((jnp.cumsum(matches, axis=0) - 1) * matches, axis=1)
    slot_index = chosen_expert * capacity + position
    slot_match = (slot_index[:, None] == jnp.arange(expert_count * capacity)[None, :]) & pair_alive[
        :, None
    ]
    scatter_matrix = jnp.sum(
        slot_match.reshape(work_count, top_count, -1).astype(jnp.int32), axis=1
    ).astype(jnp.bfloat16)
    outgoing = jnp.dot(scatter_matrix.T, work_tokens, preferred_element_type=jnp.float32).astype(
        jnp.bfloat16
    )
    outgoing = outgoing.reshape(expert_count, capacity, -1)
    returned = lax.all_to_all(
        expert_rows(
            lax.all_to_all(
                outgoing, ("replica", "expert"), split_axis=0, concat_axis=0, tiled=True
            ),
            w_gate,
            w_up,
            w_down,
        ),
        ("replica", "expert"),
        split_axis=0,
        concat_axis=0,
        tiled=True,
    )
    returned_flat = returned.reshape(expert_count * capacity, -1)
    gathered = returned_flat[jnp.clip(slot_index, 0, expert_count * capacity - 1)].astype(
        jnp.float32
    )
    expert_out = jnp.sum(
        gathered.reshape(work_count, top_count, -1) * combine[:, :, None], axis=1
    ).astype(jnp.bfloat16)
    return (attended, expert_out)


def solution(mesh):
    placed = (
        P(("replica", "expert"), None),
        P(("replica", "expert"), None),
        P(("replica", "expert"), None, None),
        P(("replica", "expert"), None),
        P(("replica", "expert")),
        P(("replica", "expert")),
        P(("replica", "expert"), None, None),
        P(("replica", "expert"), None),
        P(("replica", "expert"), None),
        P(("replica", "expert"), None, None),
        P(("replica", "expert"), None, None),
        P(("replica", "expert"), None, None),
    )
    return jax.shard_map(
        on_device,
        mesh=mesh,
        in_specs=placed,
        out_specs=(P(("replica", "expert"), None), P(("replica", "expert"), None)),
        check_vma=False,
    )
```

profile of v0, /device:TPU:0, one launch (start us, length us, event | category | flops | bytes accessed | tf_op | source)
XLA Modules:
  0.0 179.9 jit_solution(12008865204245623414)
XLA Ops:
  5.4 4.4 %all-to-all-start = ((bf16[8,1,1]{2,1,0:T(2,128)(2,1)}), bf16[8,1,1]{2,1,0:T(2,128)(2,1)S(1)}, u32[]{:S(2)}, u32[]{:S(2)}) async-start(bf16[8,1,1]{2,1,0:T(2,128)(2,1)} %copy.45), calls=%async_computation | async-start | bytes 8192 | tf_op jit(solution)/shard_map/all_to_all | solution.py:110
  9.8 2.6 %gather_fusion.1 = bf16[8,36864]{1,0:T(8,128)(2,1)S(1)} fusion(bf16[8,36864]{1,0:T(8,128)(2,1)} %param.13, s32[1024]{0:T(1024)S(1)} %pad_clamp_fusion.1), kind=kCustom, calls=%fused_computation.1 | custom fusion | bytes 1179680 | tf_op jit(solution)/shard_map/gather | solution.py:95
  16.7 1.1 reduce.1
  17.8 1.3 reshape.387
  19.8 1.2 bitcast_select_fusion
  24.0 1.1 copy.62
  25.1 4.8 %all-to-all-start.3 = ((bf16[8,2,288]{2,1,0:T(2,128)(2,1)}), bf16[8,2,288]{2,1,0:T(2,128)(2,1)S(1)}, u32[]{:S(2)}, u32[]{:S(2)}) async-start(bf16[8,2,288]{2,1,0:T(2,128)(2,1)} %reshape.389), calls=%async_computation.3 | async-start | bytes 24576 | tf_op jit(solution)/shard_map/all_to_all | solution.py:104
  30.1 5.2 %all-to-all-done.3 = bf16[8,2,288]{2,1,0:T(2,128)(2,1)S(1)} async-done(((bf16[8,2,288]{2,1,0:T(2,128)(2,1)}), bf16[8,2,288]{2,1,0:T(2,128)(2,1)S(1)}, u32[]{:S(2)}, u32[]{:S(2)}) %all-to-all-start.3) | async-done | bytes 9248 | tf_op jit(solution)/shard_map/all_to_all | solution.py:104
  35.3 3.3 %all-to-all-start.4 = ((bf16[8,2,1792]{2,1,0:T(2,128)(2,1)}), bf16[8,2,1792]{2,1,0:T(2,128)(2,1)S(1)}, u32[]{:S(2)}, u32[]{:S(2)}) async-start(bf16[8,2,1792]{2,1,0:T(2,128)(2,1)} %reshape.391), calls=%async_computation.4 | async-start | bytes 114688 | tf_op jit(solution)/shard_map/all_to_all | solution.py:107
  38.9 5.2 %all-to-all-done.4 = bf16[8,2,1792]{2,1,0:T(2,128)(2,1)S(1)} async-done(((bf16[8,2,1792]{2,1,0:T(2,128)(2,1)}), bf16[8,2,1792]{2,1,0:T(2,128)(2,1)S(1)}, u32[]{:S(2)}, u32[]{:S(2)}) %all-to-all-start.4) | async-done | bytes 57376 | tf_op jit(solution)/shard_map/all_to_all | solution.py:107
  44.2 3.5 %all-to-all-start.1 = ((bf16[8,2,18432]{2,1,0:T(2,128)(2,1)}), bf16[8,2,18432]{2,1,0:T(2,128)(2,1)S(1)}, u32[]{:S(2)}, u32[]{:S(2)}) async-start(bf16[8,2,18432]{2,1,0:T(2,128)(2,1)} %reshape.387), calls=%async_computation.1 | async-start | bytes 1179648 | tf_op jit(solution)/shard_map/all_to_all | solution.py:101
  48.3 10.4 %all-to-all-done.1 = bf16[8,2,18432]{2,1,0:T(2,128)(2,1)S(1)} async-done(((bf16[8,2,18432]{2,1,0:T(2,128)(2,1)}), bf16[8,2,18432]{2,1,0:T(2,128)(2,1)S(1)}, u32[]{:S(2)}, u32[]{:S(2)}) %all-to-all-start.1) | async-done | bytes 589856 | tf_op jit(solution)/shard_map/all_to_all | solution.py:101
  58.7 3.6 %all-to-all-start.2 = ((bf16[8,1,128,576]{2,3,1,0:T(8,128)(2,1)}), bf16[8,1,128,576]{2,3,1,0:T(8,128)(2,1)S(1)}, u32[]{:S(2)}, u32[]{:S(2)}) async-start(bf16[8,1,128,576]{2,3,1,0:T(8,128)(2,1)} %bitcast_select_fusion), calls=%async_computation.2 | async-start | bytes 2359296 | tf_op jit(solution)/shard_map/all_to_all | solution.py:98
  63.3 1.7 reshape.323
  65.0 14.5 %all-to-all-done.2 = bf16[8,1,128,576]{2,3,1,0:T(8,128)(2,1)S(1)} async-done(((bf16[8,1,128,576]{2,3,1,0:T(8,128)(2,1)}), bf16[8,1,128,576]{2,3,1,0:T(8,128)(2,1)S(1)}, u32[]{:S(2)}, u32[]{:S(2)}) %all-to-all-start.2) | async-done | bytes 1179680 | tf_op jit(solution)/shard_map/all_to_all | solution.py:98
  80.5 9.4 %all-to-all-start.5 = ((bf16[128,2,3584]{2,1,0:T(2,128)(2,1)}), bf16[128,2,3584]{2,1,0:T(2,128)(2,1)S(1)}, u32[]{:S(2)}, u32[]{:S(2)}) async-start(bf16[128,2,3584]{2,1,0:T(2,128)(2,1)} %reshape.323), calls=%async_computation.5 | async-start | bytes 3670016 | tf_op jit(solution)/shard_map/all_to_all | solution.py:153
  90.1 2.3 %reshape.388 = bf16[8,1,36864]{2,1,0:T(2,128)(2,1)S(1)} reshape(bf16[8,2,18432]{2,1,0:T(2,128)(2,1)} %copy-done.5) | data formatting | bytes 1179648
  92.4 4.4 %reduce = bf16[8,36864]{1,0:T(8,128)(2,1)} reduce(bf16[8,1,36864]{2,1,0:T(2,128)(2,1)S(1)} %reshape.388, bf16[]{:T(256)} %constant.50), dimensions={1}, to_apply=%all_to_all.23.reduce_sub_computation | reduce | bytes 1179650 | tf_op jit(solution)/shard_map/all_to_all | solution.py:101
  96.8 2.8 %reshape_reshape.3 = bf16[8,64,576]{2,1,0:T(8,128)(2,1)} reshape(bf16[8,36864]{1,0:T(8,128)(2,1)} %reduce) | data formatting | bytes 1179648 | tf_op jit(solution)/shard_map/reshape;reshape | solution.py:16
  99.6 1.4 fusion.46
  101.0 1.6 fusion.68
  103.7 13.1 %all-to-all-done.5 = bf16[128,2,3584]{2,1,0:T(2,128)(2,1)S(1)} async-done(((bf16[128,2,3584]{2,1,0:T(2,128)(2,1)}), bf16[128,2,3584]{2,1,0:T(2,128)(2,1)S(1)}, u32[]{:S(2)}, u32[]{:S(2)}) %all-to-all-start.5) | async-done | bytes 1835040 | tf_op jit(solution)/shard_map/all_to_all | solution.py:153
  116.8 1.7 reshape.324
  118.5 6.8 %fusion.4 = f32[256,1024]{1,0:T(8,128)} fusion(bf16[256,3584]{1,0:T(8,128)(2,1)} %reshape.324, bf16[1,3584,1024]{2,1,0:T(8,128)(2,1)} %param.21), kind=kOutput, calls=%fused_computation.10 | convolution fusion | flops 1879048192 | bytes 10223616 | tf_op jit(solution)/shard_map/dot_general | solution.py:58
  125.3 10.8 %fusion.6 = bf16[256,3584]{1,0:T(8,128)(2,1)} fusion(bf16[1,1024,3584]{2,1,0:T(8,128)(2,1)} %param.23, bf16[256,3584]{1,0:T(8,128)(2,1)S(1)} %copy-done.7, bf16[1,3584,1024]{2,1,0:T(8,128)(2,1)} %param.22, f32[256,1024]{1,0:T(8,128)} %fusion.4), kind=kOutput, calls=%fused_computation.12 | convolution fusion | flops 3760586752 | bytes 19398656 | tf_op jit(solution)/shard_map/dot_general | solution.py:61
  136.1 4.8 %reshape.325 = bf16[128,2,3584]{2,1,0:T(2,128)(2,1)} reshape(bf16[256,3584]{1,0:T(8,128)(2,1)} %fusion.6) | data formatting | bytes 3670016 | tf_op jit(solution)/shard_map/reshape | solution.py:62
  140.8 5.8 %all-to-all-start.6 = ((bf16[128,2,3584]{2,1,0:T(2,128)(2,1)}), bf16[128,2,3584]{2,1,0:T(2,128)(2,1)}, u32[]{:S(2)}, u32[]{:S(2)}) async-start(bf16[128,2,3584]{2,1,0:T(2,128)(2,1)} %reshape.325), calls=%async_computation.6 | async-start | bytes 3670016 | tf_op jit(solution)/shard_map/all_to_all | solution.py:151
  146.7 1.0 pad_maximum_fusion
  147.7 25.7 %all-to-all-done.6 = bf16[128,2,3584]{2,1,0:T(2,128)(2,1)} async-done(((bf16[128,2,3584]{2,1,0:T(2,128)(2,1)}), bf16[128,2,3584]{2,1,0:T(2,128)(2,1)}, u32[]{:S(2)}, u32[]{:S(2)}) %all-to-all-start.6) | async-done | bytes 1835040 | tf_op jit(solution)/shard_map/all_to_all | solution.py:151
  173.4 4.1 %reshape.326 = bf16[256,3584]{1,0:T(8,128)(2,1)S(1)} reshape(bf16[128,2,3584]{2,1,0:T(2,128)(2,1)} %all-to-all-done.6) | data formatting | bytes 3670016 | tf_op jit(solution)/shard_map/reshape | solution.py:165
  177.5 1.1 gather_fusion.5
  178.6 1.3 fusion.9
  (86 shorter events, 17.0 us)
Async XLA Ops:
  5.4 19.8 %all-to-all-start = ((bf16[8,1,1]{2,1,0:T(2,128)(2,1)}), bf16[8,1,1]{2,1,0:T(2,128)(2,1)S(1)}, u32[]{:S(2)}, u32[]{:S(2)}) async-start(bf16[8,1,1]{2,1,0:T(2,128)(2,1)} %copy.45), calls=%async_computation | async-start | bytes 8192 | tf_op jit(solution)/shard_map/all_to_all | solution.py:110
  9.8 2.7 %copy-start = (bf16[8,36864]{1,0:T(8,128)(2,1)S(1)}, bf16[8,36864]{1,0:T(8,128)(2,1)}, u32[]{:S(2)}) copy-start(bf16[8,36864]{1,0:T(8,128)(2,1)} %param.13) | copy-start | bytes 1769476
  9.8 3.6 %copy-start.8 = (bf16[8,576]{1,0:T(8,128)(2,1)S(1)}, bf16[8,576]{1,0:T(8,128)(2,1)}, u32[]{:S(2)}) copy-start(bf16[8,576]{1,0:T(8,128)(2,1)} %param.15) | copy-start | bytes 27652
  9.8 4.1 %copy-start.10 = (s32[16,8]{0,1:T(8,128)S(1)}, s32[16,8]{0,1:T(8,128)}, u32[]{:S(2)}) copy-start(s32[16,8]{0,1:T(8,128)} %param.19) | copy-start | bytes 1540
  9.8 4.3 %copy-start.4 = (bf16[8,3584]{1,0:T(8,128)(2,1)S(1)}, bf16[8,3584]{1,0:T(8,128)(2,1)}, u32[]{:S(2)}) copy-start(bf16[8,3584]{1,0:T(8,128)(2,1)} %param.12) | copy-start | bytes 172036
  16.0 3.1 %copy-start.1 = (bf16[8,128,576]{1,2,0:T(8,128)(2,1)S(1)}, bf16[8,128,576]{1,2,0:T(8,128)(2,1)}, u32[]{:S(2)}) copy-start(bf16[8,128,576]{1,2,0:T(8,128)(2,1)} %param.14) | copy-start | bytes 3538948
  23.5 1.7 copy-start.9
  25.1 10.1 %all-to-all-start.3 = ((bf16[8,2,288]{2,1,0:T(2,128)(2,1)}), bf16[8,2,288]{2,1,0:T(2,128)(2,1)S(1)}, u32[]{:S(2)}, u32[]{:S(2)}) async-start(bf16[8,2,288]{2,1,0:T(2,128)(2,1)} %reshape.389), calls=%async_computation.3 | async-start | bytes 24576 | tf_op jit(solution)/shard_map/all_to_all | solution.py:104
  35.3 8.9 %all-to-all-start.4 = ((bf16[8,2,1792]{2,1,0:T(2,128)(2,1)}), bf16[8,2,1792]{2,1,0:T(2,128)(2,1)S(1)}, u32[]{:S(2)}, u32[]{:S(2)}) async-start(bf16[8,2,1792]{2,1,0:T(2,128)(2,1)} %reshape.391), calls=%async_computation.4 | async-start | bytes 114688 | tf_op jit(solution)/shard_map/all_to_all | solution.py:107
  44.2 14.5 %all-to-all-start.1 = ((bf16[8,2,18432]{2,1,0:T(2,128)(2,1)}), bf16[8,2,18432]{2,1,0:T(2,128)(2,1)S(1)}, u32[]{:S(2)}, u32[]{:S(2)}) async-start(bf16[8,2,18432]{2,1,0:T(2,128)(2,1)} %reshape.387), calls=%async_computation.1 | async-start | bytes 1179648 | tf_op jit(solution)/shard_map/all_to_all | solution.py:101
  58.7 4.0 %copy-start.5 = (bf16[8,2,18432]{2,1,0:T(2,128)(2,1)}, bf16[8,2,18432]{2,1,0:T(2,128)(2,1)S(1)}, u32[]{:S(2)}) copy-start(bf16[8,2,18432]{2,1,0:T(2,128)(2,1)S(1)} %all-to-all-done.1) | copy-start | bytes 1769476
  58.7 20.9 %all-to-all-start.2 = ((bf16[8,1,128,576]{2,3,1,0:T(8,128)(2,1)}), bf16[8,1,128,576]{2,3,1,0:T(8,128)(2,1)S(1)}, u32[]{:S(2)}, u32[]{:S(2)}) async-start(bf16[8,1,128,576]{2,3,1,0:T(8,128)(2,1)} %bitcast_select_fusion), calls=%async_computation.2 | async-start | bytes 2359296 | tf_op jit(solution)/shard_map/all_to_all | solution.py:98
  79.5 1.0 copy-start.2
  80.5 36.3 %all-to-all-start.5 = ((bf16[128,2,3584]{2,1,0:T(2,128)(2,1)}), bf16[128,2,3584]{2,1,0:T(2,128)(2,1)S(1)}, u32[]{:S(2)}, u32[]{:S(2)}) async-start(bf16[128,2,3584]{2,1,0:T(2,128)(2,1)} %reshape.323), calls=%async_computation.5 | async-start | bytes 3670016 | tf_op jit(solution)/shard_map/all_to_all | solution.py:153
  96.8 4.2 %copy-start.3 = (bf16[8,1,128,576]{2,3,1,0:T(8,128)(2,1)S(1)}, bf16[8,1,128,576]{2,3,1,0:T(8,128)(2,1)}, u32[]{:S(2)}) copy-start(bf16[8,1,128,576]{2,3,1,0:T(8,128)(2,1)} %copy-done.2) | copy-start | bytes 3538948
  118.5 6.8 %copy-start.7 = (bf16[256,3584]{1,0:T(8,128)(2,1)S(1)}, bf16[256,3584]{1,0:T(8,128)(2,1)}, u32[]{:S(2)}) copy-start(bf16[256,3584]{1,0:T(8,128)(2,1)} %reshape.324) | copy-start | bytes 5505028
  140.8 5.9 %copy-start.6 = (bf16[1,8,64,512]{3,1,2,0:T(8,128)(2,1)S(1)}, bf16[1,8,64,512]{3,1,2,0:T(8,128)(2,1)}, u32[]{:S(2)}) copy-start(bf16[1,8,64,512]{3,1,2,0:T(8,128)(2,1)} %copy.62) | copy-start | bytes 1572868
  140.8 32.6 %all-to-all-start.6 = ((bf16[128,2,3584]{2,1,0:T(2,128)(2,1)}), bf16[128,2,3584]{2,1,0:T(2,128)(2,1)}, u32[]{:S(2)}, u32[]{:S(2)}) async-start(bf16[128,2,3584]{2,1,0:T(2,128)(2,1)} %reshape.325), calls=%async_computation.6 | async-start | bytes 3670016 | tf_op jit(solution)/shard_map/all_to_all | solution.py:151
where the time goes:
time: 181 us; the launch traced here: 180 us
  waiting for transfers between devices  74.2 us (41%)
  starting transfers between devices  34.9 us (19%)
  local copies, waits for them, and re-layouts  31.5 us (17%)
  matrix products  23 us (13%)
  other arithmetic  15.4 us (9%)
    all_to_all x1, waiting for transfers between devices, on_device(): lax.all_to_all(expert_rows(lax.all_to_all(outgoing, ('replica', 'expert')...  25.7 us
    all_to_all x1, waiting for transfers between devices, on_device(): lax.all_to_all(to_buffer(send_cache, replicas), 'replica', split_axis=0,...  14.5 us
    all_to_all x1, waiting for transfers between devices, on_device(): lax.all_to_all(outgoing, ('replica', 'expert'), split_axis=0, concat_axis...  13.1 us
    dot_general x1, matrix products, expert_rows(): jnp.dot(hidden, w_down[0], preferred_element_type=jnp.float32)  10.8 us
    all_to_all x1, waiting for transfers between devices, on_device(): lax.all_to_all(to_buffer(send_query, replicas), 'replica', split_axis=0,...  10.4 us
    all_to_all x1, starting transfers between devices, on_device(): lax.all_to_all(outgoing, ('replica', 'expert'), split_axis=0, concat_axis...  9.37 us
    unnamed x33, local copies, waits for them, and re-layouts  7.54 us
    dot_general x1, matrix products, expert_rows(): jnp.dot(flat_rows, w_gate[0], preferred_element_type=jnp.float32)  6.8 us
  transfers between devices with their start and end apart: 7, of which 6 were waited for; matrix products, arithmetic and copies ran while one was open for 19% of the time, Pallas kernels for 0%

commit v1 on v0

v1 whole, which is shorter than its diff:
```python
import jax
import jax.numpy as jnp
from jax import lax
from jax.experimental import pallas as pl
from jax.experimental.pallas import tpu as pltpu
from jax.sharding import PartitionSpec as P

HEADS = 64
VDIM = 512
LAT = 576
BOTH = ("replica", "expert")
F32 = jnp.float32
BF16 = jnp.bfloat16

PARTS = 4
CAP = 2

DEVICE_ORDER = (
    23, 44, 105, 64, 100, 28, 5, 34, 111, 118, 84, 50, 77, 79, 37, 43,
    15, 120, 74, 83, 125, 69, 8, 19, 41, 88, 47, 102, 115, 17, 101, 127,
    55, 81, 78, 122, 13, 57, 65, 0, 126, 117, 40, 112, 1, 61, 66, 22,
    107, 76, 62, 89, 116, 103, 110, 36, 82, 30, 85, 9, 3, 95, 6, 51,
    16, 124, 75, 104, 121, 45, 38, 114, 26, 99, 72, 27, 42, 53, 97, 60,
    54, 87, 94, 73, 113, 7, 31, 52, 59, 29, 90, 4, 98, 49, 92, 11,
    21, 39, 48, 93, 10, 67, 123, 24, 32, 108, 63, 119, 12, 71, 14, 20,
    80, 33, 70, 58, 109, 68, 25, 86, 35, 96, 91, 56, 18, 106, 2, 46,
)

score_scale = 192.0 ** (-0.5)

VMEM = pl.BlockSpec(memory_space=pltpu.VMEM)
SMEM = pl.BlockSpec(memory_space=pltpu.SMEM)
HBM = pl.BlockSpec(memory_space=pltpu.HBM)


def iota(shape, dim):
    return lax.broadcasted_iota(jnp.int32, shape, dim)


def attend(query_rows, latent_rows, own_latent, live_length):
    row_count = query_rows.shape[0]
    per_head = query_rows.reshape(row_count, HEADS, LAT)
    scores = (
        jnp.einsum("nhl,ntl->nht", per_head, latent_rows, preferred_element_type=F32) * score_scale
    )
    own_score = jnp.einsum("nhl,nl->nh", per_head, own_latent, preferred_element_type=F32)
    own_score = own_score * score_scale
    visible = iota((1, 1, latent_rows.shape[1]), 2) < live_length[:, None, None]
    scores = jnp.where(visible, scores, -jnp.inf)
    largest = jnp.maximum(jnp.max(scores, axis=2), own_score)
    weights = jnp.exp(scores - largest[:, :, None])
    own_weight = jnp.exp(own_score - largest)
    denominator = jnp.sum(weights, axis=2) + own_weight
    context = jnp.einsum(
        "nht,ntv->nhv",
        weights.astype(BF16),
        latent_rows[:, :, :VDIM],
        preferred_element_type=F32,
    )
    own_rounded = lax.optimization_barrier(own_weight.astype(BF16)).astype(F32)
    context = context + own_rounded[:, :, None] * own_latent[:, None, :VDIM].astype(F32)
    normalized = context / denominator[:, :, None] * (live_length > 0).astype(F32)[:, None, None]
    return normalized.astype(BF16)


def by_index(index, count, value_of):
    spread = jnp.zeros(index.shape, jnp.int32)
    for i in range(count):
        spread = jnp.where(index == i, value_of(i), spread)
    return spread


def alive_of(length, finished):
    return lambda s: jnp.where(finished[s] == 0, length[s], 0)


def start_all(copies):
    for copy in copies:
        copy.start()
    return copies


def wait_all(copies):
    for copy in copies:
        copy.wait()


def sub_rows(rows, width):
    pieces = [rows[:, q * width : (q + 1) * width].astype(F32) for q in range(PARTS)]
    return jnp.concatenate(pieces, axis=0).astype(BF16)


def pick_kernel(plan_hbm, length_hbm, finished_hbm, tokens_hbm, out, *scratch):
    plan, length, finished, tokens, send, sems = scratch
    pairs = [
        (plan_hbm, plan),
        (length_hbm, length),
        (finished_hbm, finished),
        (tokens_hbm, tokens),
    ]
    wait_all(start_all([pltpu.make_async_copy(*pair, sems.at[n]) for n, pair in enumerate(pairs)]))
    count = tokens.shape[0]
    shape = (send.shape[0], PARTS * count)
    row, col = iota(shape, 0), iota(shape, 1)
    source = col & (count - 1)
    wanted = by_index(row >> 3, send.shape[0] // 8, lambda d: plan[d])
    alive = by_index(source, count, alive_of(length, finished))
    chosen = (wanted == source) & ((row & 7) == (col >> 3)) & (alive > 0)
    chosen = jnp.where(chosen, 1.0, 0.0).astype(BF16)
    flat = sub_rows(tokens[...], send.shape[1])
    send[...] = jnp.dot(chosen, flat, preferred_element_type=F32).astype(BF16)
    wait_all(start_all([pltpu.make_async_copy(send, out, sems.at[0])]))


def routing_kernel(plan, length, finished, routes, score, order, scatter, gather):
    slots, top = routes.shape
    lanes = scatter.shape[0]
    experts = lanes // 8
    count = slots // 2
    names = routes[...]
    scores = score[...]
    named = jnp.zeros((slots, experts), F32)
    weight = jnp.zeros((slots, experts), F32)
    for k in range(top):
        hit = names[:, k : k + 1] == order[...]
        named = jnp.where(hit, 1.0, named)
        weight = jnp.where(hit, scores[:, k : k + 1], weight)
    weight = 2.5 * weight / jnp.sum(scores, axis=1, keepdims=True)
    lower = jnp.where(iota((slots, slots), 1) < iota((slots, slots), 0), 1.0, 0.0).astype(BF16)
    position = jnp.dot(lower, named.astype(BF16), preferred_element_type=F32)
    high = weight.astype(BF16).astype(F32)
    low = weight - high
    stacked = jnp.concatenate([named, position, high, low], axis=0).astype(BF16)
    widen = iota((experts, lanes), 0) == (iota((experts, lanes), 1) >> 3)
    wide = jnp.dot(stacked, jnp.where(widen, 1.0, 0.0).astype(BF16), preferred_element_type=F32)
    lane = iota((slots, lanes), 1)
    part = lane & (PARTS - 1)
    place = ((lane >> 2) & 1).astype(F32)
    taken = (wide[:slots] > 0.5) & (wide[slots : 2 * slots] == place)
    taken = jnp.where(taken, 1.0, 0.0)

    row = iota((count, lanes), 0)
    alive = by_index(row, count, alive_of(length, finished))
    moved = jnp.zeros((count, lanes), jnp.int32)
    for d in range(count):
        moved = jnp.where(row == plan[d], 1, moved)
    stays = (alive > 0) & (moved == 0)
    half = part[:count]
    pieces = [jnp.where(stays & (half == q), taken[:count], 0.0) for q in range(PARTS)]
    for i in range(count):
        pieces.append(jnp.where(half == row, taken[count + i : count + i + 1], 0.0))
    used = len(pieces) * count
    pieces.append(jnp.zeros((scatter.shape[1] - used, lanes), F32))
    scatter[...] = jnp.transpose(jnp.concatenate(pieces, axis=0)).astype(BF16)

    pieces = []
    for start in (2 * slots, 3 * slots):
        wanted = wide[start : start + slots] * taken
        pieces += [jnp.where(part == q, wanted, 0.0) for q in range(PARTS)]
    gather[...] = jnp.concatenate(pieces, axis=0).astype(BF16)


def dispatch_kernel(scatter, tokens, arrived, out, block, sems):
    lanes, width = out.shape
    pad = scatter.shape[1] - PARTS * tokens.shape[0] - arrived.shape[0]
    pieces = [tokens[:, q * width : (q + 1) * width].astype(F32) for q in range(PARTS)]
    pieces += [arrived[...].astype(F32), jnp.zeros((pad, width), F32)]
    flat = jnp.concatenate(pieces, axis=0).astype(BF16)
    copies = []
    for b in range(lanes // 256):
        part = pl.ds(b * 256, 256)
        rows = jnp.dot(scatter[part, :], flat, preferred_element_type=F32)
        block[part, :] = rows.astype(BF16)
        copies += start_all([pltpu.make_async_copy(block.at[part], out.at[part], sems.at[b])])
    wait_all(copies)


def expert_kernel(recv, w_gate, w_up, w_down, out, rows, hidden, results, sent, sems):
    width = recv.shape[1]
    blocks = recv.shape[0] // 256
    one, two = iota((256, 256), 0), iota((256, 256), 1)
    apart = ((one & 63) * PARTS + (one >> 6)) == two
    together = ((two & 63) * PARTS + (two >> 6)) == one
    apart = jnp.where(apart, 1.0, 0.0).astype(BF16)
    together = jnp.where(together, 1.0, 0.0).astype(BF16)
    for b in range(blocks):
        got = jnp.dot(apart, recv[b * 256 : (b + 1) * 256, :], preferred_element_type=F32)
        got = got.astype(BF16)
        for q in range(PARTS):
            rows[q, b * 64 : (b + 1) * 64, :] = got[q * 64 : (q + 1) * 64, :]

    gate = up = None
    for q in range(PARTS):
        part = slice(q * width, (q + 1) * width)
        more = jnp.dot(rows[q], w_gate[0, part, :], preferred_element_type=F32)
        gate = more if gate is None else gate + more
        more = jnp.dot(rows[q], w_up[0, part, :], preferred_element_type=F32)
        up = more if up is None else up + more
    hidden[...] = (gate / (1.0 + jnp.exp(-gate)) * up).astype(BF16)
    for q in range(PARTS):
        part = slice(q * width, (q + 1) * width)
        result = jnp.dot(hidden[...], w_down[0, :, part], preferred_element_type=F32).astype(BF16)
        for b in range(blocks):
            results[b, q * 64 : (q + 1) * 64, :] = result[b * 64 : (b + 1) * 64, :]
    copies = []
    for b in range(blocks):
        part = pl.ds(b * 256, 256)
        value = jnp.dot(together, results[b], preferred_element_type=F32).astype(BF16)
        sent[part, :] = value
        copies += start_all([pltpu.make_async_copy(sent.at[part], out.at[part], sems.at[b])])
    wait_all(copies)


def combine_kernel(gather, recv, out):
    slots = out.shape[0]
    width = recv.shape[1]
    summed = jnp.dot(gather[...], recv[...], preferred_element_type=F32)
    half = summed.shape[0] // 2
    summed = summed[:half] + summed[half:]
    for q in range(PARTS):
        out[:, q * width : (q + 1) * width] = summed[q * slots : (q + 1) * slots].astype(BF16)


def call(kernel, outs, in_specs, cost, scratch=(), limit=32, in_hbm=False):
    shape_of = pltpu.HBM if in_hbm else jax.ShapeDtypeStruct
    shapes = [shape_of(shape, BF16) for shape in outs]
    specs = [HBM if in_hbm else VMEM] * len(outs)
    return pl.pallas_call(
        kernel,
        out_shape=shapes if len(shapes) > 1 else shapes[0],
        in_specs=in_specs,
        out_specs=specs if len(specs) > 1 else specs[0],
        scratch_shapes=list(scratch),
        compiler_params=pltpu.CompilerParams(vmem_limit_bytes=limit * 2**20),
        cost_estimate=pl.CostEstimate(flops=cost[0], bytes_accessed=cost[1], transcendentals=0),
    )


def on_device(
    tokens,
    queries,
    latent_cache,
    new_latent,
    lengths,
    finished,
    migrate,
    routes,
    route_score,
    w_gate,
    w_up,
    w_down,
):
    count, model = tokens.shape
    slots = routes.shape[0]
    replicas = lax.axis_size("replica")
    devices = replicas * lax.axis_size("expert")
    width = model // PARTS
    lanes = devices * CAP * PARTS
    hidden = w_gate.shape[2]
    plan = migrate.reshape(replicas)

    order = [list(DEVICE_ORDER)] if devices == len(DEVICE_ORDER) else [list(range(devices))]
    spread = jnp.broadcast_to(jnp.asarray(order, jnp.int32), (slots, devices))

    def exchange(values):
        values = values.reshape(devices, 8, width)
        values = lax.all_to_all(values, BOTH, 0, 0, axis_index_groups=order, tiled=True)
        return values.reshape(lanes, width)

    send = call(
        pick_kernel,
        [(replicas * 8, width)],
        [HBM] * 4,
        (10**6, 10**5),
        [
            pltpu.SMEM((replicas,), jnp.int32),
            pltpu.SMEM((count,), jnp.int32),
            pltpu.SMEM((count,), jnp.int32),
            pltpu.VMEM((count, model), BF16),
            pltpu.VMEM((replicas * 8, width), BF16),
            pltpu.SemaphoreType.DMA((4,)),
        ],
        in_hbm=True,
    )(*[pltpu.with_memory_space_constraint(x, pltpu.HBM) for x in (plan, lengths, finished, tokens)])
    arrived = lax.all_to_all(
        send.reshape(replicas, 8, width), "replica", split_axis=0, concat_axis=0, tiled=True
    ).reshape(replicas * 8, width)
    scatter, gather = call(
        routing_kernel,
        [(lanes, 128), (2 * PARTS * slots, lanes)],
        [SMEM] * 3 + [VMEM] * 3,
        (10**7, 10**6),
    )(plan, lengths, finished, routes, route_score, spread)
    outgoing = call(
        dispatch_kernel,
        [(lanes, width)],
        [VMEM] * 3,
        (2 * 10**8, 2 * 10**6),
        [pltpu.VMEM((lanes, width), BF16), pltpu.SemaphoreType.DMA((lanes // 256,))],
        in_hbm=True,
    )(scatter, tokens, arrived)
    incoming = exchange(outgoing)

    own_length = jnp.where(finished == 0, lengths, 0)
    attended = attend(queries, latent_cache, new_latent, own_length)
    sending = plan >= 0
    moved_out = jnp.any((plan[:, None] == jnp.arange(count)[None, :]), axis=0)
    leave = jnp.where(sending[:, None, None], attended[jnp.maximum(plan, 0)], jnp.zeros((), BF16))
    leave, incoming = lax.optimization_barrier((leave, incoming))
    landed = lax.all_to_all(leave, "replica", split_axis=0, concat_axis=0, tiled=True)
    stay = jnp.where(moved_out[:, None, None], jnp.zeros((), BF16), attended)
    attended_out = jnp.concatenate([stay, landed], axis=0).reshape(slots, HEADS * VDIM)

    results = call(
        expert_kernel,
        [(lanes, width)],
        [VMEM] * 4,
        (6 * devices * CAP * model * hidden, 6 * 10**6),
        [
            pltpu.VMEM((PARTS, devices * CAP, width), BF16),
            pltpu.VMEM((devices * CAP, hidden), BF16),
            pltpu.VMEM((lanes // 256, 256, width), BF16),
            pltpu.VMEM((lanes, width), BF16),
            pltpu.SemaphoreType.DMA((lanes // 256,)),
        ],
        24,
        True,
    )(incoming, *[pltpu.with_memory_space_constraint(w, pltpu.VMEM) for w in (w_gate, w_up, w_down)])
    returned = exchange(results)
    expert_out = call(combine_kernel, [(slots, model)], [VMEM] * 2, (2 * 10**8, 2 * 10**6))(
        gather, returned
    )
    return (attended_out, expert_out)


def solution(mesh):
    rows = P(BOTH, None)
    blocks = P(BOTH, None, None)
    flat = P(BOTH)
    return jax.shard_map(
        on_device,
        mesh=mesh,
        in_specs=(rows, rows, blocks, rows, flat, flat, blocks, rows, rows, blocks, blocks, blocks),
        out_specs=(rows, rows),
        check_vma=False,
    )
```

time: 181 us -> 109 us (0.60)
  waiting for transfers between devices: 74.2 us -> 48.6 us
  matrix products: 23 us -> 2.25 us
  local copies, waits for them, and re-layouts: 31.5 us -> 14.5 us
  Pallas kernels: 0 us -> 14.2 us
  other arithmetic: 15.4 us -> 2.83 us
  starting transfers between devices: 34.9 us -> 24.9 us
    all_to_all x7 -> x4, waiting for transfers between devices: 74.2 us -> 48.6 us  [the longest x2 47.4 us: exchange(): lax.all_to_all(values, BOTH, 0, 0, axis_index_groups=order, tiled=True)]
    dot_general x7 -> x2, matrix products: 21 us -> 1.81 us  [the longest x1 1.51 us: attend(): jnp.einsum('nht,ntv->nhv', weights.astype(BF16), latent_rows[:, :, :VDIM]...]
    pallas_call x0 -> x5, Pallas kernels: none -> 14.2 us  [the longest x1 8.67 us: on_device(): call(expert_kernel, [(lanes, width)], [VMEM] * 4, (6 * devices * CAP * mo...]
    reshape x4 -> x0, local copies, waits for them, and re-layouts: 12.2 us -> none  [the longest x1 4.79 us: expert_rows(): return output.reshape(arrived_rows.shape)]
    all_to_all x7 -> x4, starting transfers between devices: 34.9 us -> 24.9 us  [the longest x2 17 us: exchange(): lax.all_to_all(values, BOTH, 0, 0, axis_index_groups=order, tiled=True)]
    gather x6 -> x1, local copies, waits for them, and re-layouts: 6.31 us -> 1.62 us  [on_device(): attended[jnp.maximum(plan, 0)]]
    all_to_all x1 -> x0, other arithmetic: 4.39 us -> none  [on_device(): lax.all_to_all(to_buffer(send_query, replicas), 'replica', split_axis=0,...]
    unnamed x33 -> x29, local copies, waits for them, and re-layouts: 7.54 us -> 11 us
  transfers between devices with their start and end apart: 7 -> 4, of which waited for: 6 -> 3; matrix products, arithmetic and copies ran while one was open for 19% -> 10% of each run, Pallas kernels for 0% -> 9%
where the time goes in v1:
time: 109 us; the launch traced here: 108 us
  waiting for transfers between devices  48.6 us (45%)
  starting transfers between devices  24.9 us (23%)
  local copies, waits for them, and re-layouts  14.5 us (13%)
  Pallas kernels  14.2 us (13%)
  other arithmetic  2.83 us (3%)
  matrix products  2.25 us (2%)
    all_to_all x2, waiting for transfers between devices, exchange(): lax.all_to_all(values, BOTH, 0, 0, axis_index_groups=order, tiled=True)  47.4 us
    all_to_all x2, starting transfers between devices, exchange(): lax.all_to_all(values, BOTH, 0, 0, axis_index_groups=order, tiled=True)  17 us
    unnamed x29, local copies, waits for them, and re-layouts  11 us
    pallas_call x1, Pallas kernels, on_device(): call(expert_kernel, [(lanes, width)], [VMEM] * 4, (6 * devices * CAP * mo...  8.67 us
    all_to_all x1, starting transfers between devices, on_device(): lax.all_to_all(send.reshape(replicas, 8, width), 'replica', split_axis=0,...  4.4 us
    all_to_all x1, starting transfers between devices, on_device(): lax.all_to_all(leave, 'replica', split_axis=0, concat_axis=0, tiled=True)  3.49 us
  transfers between devices with their start and end apart: 4, of which 3 were waited for; matrix products, arithmetic and copies ran while one was open for 10% of the time, Pallas kernels for 9%

profile of v1, /device:TPU:0, one launch (start us, length us, event | category | flops | bytes accessed | tf_op | source)
XLA Modules:
  0.0 108.1 jit_solution(8295947446425754651)
XLA Ops:
  0.6 1.8 %shard_map.141 = bf16[64,896]{1,0:T(8,128)(2,1)} custom-call(s32[8]{0:T(128)} %bitcast.21, s32[8]{0:T(128)} %length_hbm.1, s32[8]{0:T(128)} %finished_hbm.1, bf16[8,3584]{1,0:T(8,128)(2,1)} %tokens.1), custom_call_target="tpu_custom_call" | custom-call | flops 1000000 | bytes 100000 | tf_op jit(solution)/shard_map/pallas_call | solution.py:270
  2.4 4.4 %all-to-all-start = ((bf16[8,8,896]{2,1,0:T(8,128)(2,1)}), bf16[8,8,896]{2,1,0:T(8,128)(2,1)S(1)}, u32[]{:S(2)}, u32[]{:S(2)}) async-start(bf16[8,8,896]{2,1,0:T(8,128)(2,1)} %bitcast.28), calls=%async_computation | async-start | bytes 229376 | tf_op jit(solution)/shard_map/all_to_all | solution.py:285
  6.8 0.7 compare_convert_fusion
  7.5 0.1 iota_compare_fusion
  7.6 0.0 copy-start.3
  7.6 1.9 %reshape.75 = bf16[8,64,576]{2,1,0:T(8,128)(2,1)S(1)} reshape(bf16[8,36864]{1,0:T(8,128)(2,1)} %param.14) | data formatting | bytes 1179648 | tf_op jit(solution)/shard_map/reshape | solution.py:42
  9.6 0.4 fusion.14
  10.0 0.3 fusion.9
  10.3 0.1 copy.19.routes
  10.4 0.1 copy.20.score
  10.5 1.1 shard_map.140
  11.6 1.2 %all-to-all-done = bf16[8,8,896]{2,1,0:T(8,128)(2,1)S(1)} async-done(((bf16[8,8,896]{2,1,0:T(8,128)(2,1)}), bf16[8,8,896]{2,1,0:T(8,128)(2,1)S(1)}, u32[]{:S(2)}, u32[]{:S(2)}) %all-to-all-start) | async-done | bytes 114720 | tf_op jit(solution)/shard_map/all_to_all | solution.py:285
  12.8 1.6 %shard_map.142 = bf16[1024,896]{1,0:T(8,128)(2,1)} custom-call(bf16[1024,128]{1,0:T(8,128)(2,1)S(1)} %get-tuple-element.6.scatter, bf16[8,3584]{1,0:T(8,128)(2,1)S(1)} %copy-done.3, bf16[64,896]{1,0:T(8,128)(2,1)S(1)} %bitcast.20), custom_call_target="tpu_custom_call" | custom-call | flops 200000000 | bytes 2000000 | tf_op jit(solution)/shard_map/pallas_call | solution.py:294
  14.4 10.4 %all-to-all-start.1 = ((bf16[128,8,896]{2,1,0:T(8,128)(2,1)}), bf16[128,8,896]{2,1,0:T(8,128)(2,1)S(1)}, u32[]{:S(2)}, u32[]{:S(2)}) async-start(bf16[128,8,896]{2,1,0:T(8,128)(2,1)} %bitcast.25), calls=%async_computation.1 | async-start | bytes 3670016 | tf_op jit(solution)/shard_map/all_to_all | solution.py:267
  24.8 0.3 fusion.5
  25.1 0.1 fusion.11
  25.2 0.7 slice_convert_fusion
  25.9 1.5 %broadcast_select_fusion.1 = (bf16[8,64,512]{2,1,0:T(8,128)(2,1)}, bf16[8,64,512]{2,1,0:T(8,128)(2,1)}) fusion(pred[8]{0:T(512)(128)(4,1)S(1)} %fusion.11, f32[8]{0:T(128)S(1)} %get-tuple-element.10, f32[8,64]{1,0:T(8,128)S(1)} %get-tuple-element.13, f32[8,512]{1,0:T(8,128)S(1)} %slice_convert_fusion, f32[8,64]{1,0:T(8,128)S(1)} %convert_element_type.21, ...), kind=kOutput, calls=%fused_computation.10 | convolution fusion | flops 68812800 | bytes 2388992 | tf_op jit(solution)/shard_map/nht,ntv->nhv/dot_general | solution.py:54
  27.4 1.6 %gather_fusion = bf16[8,64,512]{2,1,0:T(8,128)(2,1)S(1)} fusion(bf16[8,64,512]{2,1,0:T(8,128)(2,1)} %get-tuple-element.17, s32[1024]{0:T(1024)S(1)} %pad_clamp_fusion), kind=kCustom, calls=%fused_computation | custom fusion | bytes 1048608 | tf_op jit(solution)/shard_map/gather | solution.py:308
  29.0 0.9 broadcast_select_fusion
  29.9 21.9 %all-to-all-done.1 = bf16[128,8,896]{2,1,0:T(8,128)(2,1)S(1)} async-done(((bf16[128,8,896]{2,1,0:T(8,128)(2,1)}), bf16[128,8,896]{2,1,0:T(8,128)(2,1)S(1)}, u32[]{:S(2)}, u32[]{:S(2)}) %all-to-all-start.1) | async-done | bytes 1835040 | tf_op jit(solution)/shard_map/all_to_all | solution.py:267
  51.9 3.5 %all-to-all-start.2 = ((bf16[8,64,512]{2,1,0:T(8,128)(2,1)}), bf16[8,64,512]{2,1,0:T(8,128)(2,1)S(1)}, u32[]{:S(2)}, u32[]{:S(2)}) async-start(bf16[8,64,512]{2,1,0:T(8,128)(2,1)} %broadcast_select_fusion), calls=%async_computation.2 | async-start | bytes 1048576 | tf_op jit(solution)/shard_map/all_to_all | solution.py:310
  55.4 0.0 copy-start
  55.4 3.1 %copy-done = bf16[1,3584,1024]{2,1,0:T(8,128)(2,1)S(1)} copy-done((bf16[1,3584,1024]{2,1,0:T(8,128)(2,1)S(1)}, bf16[1,3584,1024]{2,1,0:T(8,128)(2,1)}, u32[]{:S(2)}) %copy-start) | copy-done | bytes 7340056
  58.4 3.1 %copy-done.1 = bf16[1,3584,1024]{2,1,0:T(8,128)(2,1)S(1)} copy-done((bf16[1,3584,1024]{2,1,0:T(8,128)(2,1)S(1)}, bf16[1,3584,1024]{2,1,0:T(8,128)(2,1)}, u32[]{:S(2)}) %copy-start.1) | copy-done | bytes 7340056
  61.5 3.1 %copy-done.2 = bf16[1,1024,3584]{2,1,0:T(8,128)(2,1)S(1)} copy-done((bf16[1,1024,3584]{2,1,0:T(8,128)(2,1)S(1)}, bf16[1,1024,3584]{2,1,0:T(8,128)(2,1)}, u32[]{:S(2)}) %copy-start.2) | copy-done | bytes 7340056
  64.6 8.7 %shard_map.143 = bf16[1024,896]{1,0:T(8,128)(2,1)} custom-call(bf16[1024,896]{1,0:T(8,128)(2,1)S(1)} %bitcast.18, bf16[1,3584,1024]{2,1,0:T(8,128)(2,1)S(1)} %copy-done, bf16[1,3584,1024]{2,1,0:T(8,128)(2,1)S(1)} %copy-done.1, bf16[1,1024,3584]{2,1,0:T(8,128)(2,1)S(1)} %copy-done.2), custom_call_target="tpu_custom_call" | custom-call | flops 5637144576 | bytes 6000000 | tf_op jit(solution)/shard_map/pallas_call | solution.py:314
  73.3 6.6 %all-to-all-start.3 = ((bf16[128,8,896]{2,1,0:T(8,128)(2,1)}), bf16[128,8,896]{2,1,0:T(8,128)(2,1)S(1)}, u32[]{:S(2)}, u32[]{:S(2)}) async-start(bf16[128,8,896]{2,1,0:T(8,128)(2,1)} %bitcast.24), calls=%async_computation.3 | async-start | bytes 3670016 | tf_op jit(solution)/shard_map/all_to_all | solution.py:267
  80.0 0.1 pad_maximum_fusion
  80.1 1.5 %copy.24 = bf16[2,8,64,512]{3,1,2,0:T(8,128)(2,1)} copy(bf16[2,8,64,512]{3,2,1,0:T(8,128)(2,1)S(1)} %bitcast.26) | data formatting | bytes 2097152
  81.6 25.4 %all-to-all-done.3 = bf16[128,8,896]{2,1,0:T(8,128)(2,1)S(1)} async-done(((bf16[128,8,896]{2,1,0:T(8,128)(2,1)}), bf16[128,8,896]{2,1,0:T(8,128)(2,1)S(1)}, u32[]{:S(2)}, u32[]{:S(2)}) %all-to-all-start.3) | async-done | bytes 1835040 | tf_op jit(solution)/shard_map/all_to_all | solution.py:267
  107.0 1.1 %shard_map.144 = bf16[16,3584]{1,0:T(8,128)(2,1)} custom-call(bf16[128,1024]{1,0:T(8,128)(2,1)S(1)} %get-tuple-element.8.gather, bf16[1024,896]{1,0:T(8,128)(2,1)S(1)} %bitcast.19), custom_call_target="tpu_custom_call" | custom-call | flops 200000000 | bytes 2000000 | tf_op jit(solution)/shard_map/pallas_call | solution.py:330
  (29 shorter events, 0.1 us)
Async XLA Ops:
  0.6 8.9 %copy-start.7 = (bf16[8,128,576]{1,2,0:T(8,128)(2,1)S(1)}, bf16[8,128,576]{1,2,0:T(8,128)(2,1)}, u32[]{:S(2)}) copy-start(bf16[8,128,576]{1,2,0:T(8,128)(2,1)} %param.15) | copy-start | bytes 3538948
  2.4 7.6 %copy-start.9 = (bf16[8,576]{1,0:T(8,128)(2,1)S(1)}, bf16[8,576]{1,0:T(8,128)(2,1)}, u32[]{:S(2)}) copy-start(bf16[8,576]{1,0:T(8,128)(2,1)} %param.16) | copy-start | bytes 27652
  2.4 10.4 %all-to-all-start = ((bf16[8,8,896]{2,1,0:T(8,128)(2,1)}), bf16[8,8,896]{2,1,0:T(8,128)(2,1)S(1)}, u32[]{:S(2)}, u32[]{:S(2)}) async-start(bf16[8,8,896]{2,1,0:T(8,128)(2,1)} %bitcast.28), calls=%async_computation | async-start | bytes 229376 | tf_op jit(solution)/shard_map/all_to_all | solution.py:285
  7.6 2.7 %copy-start.10 = (s32[16,8]{0,1:T(8,128)S(1)}, s32[16,8]{0,1:T(8,128)}, u32[]{:S(2)}) copy-start(s32[16,8]{0,1:T(8,128)} %param.20) | copy-start | bytes 1540
  7.6 2.8 %copy-start.11 = (f32[16,8]{0,1:T(8,128)S(1)}, f32[16,8]{0,1:T(8,128)}, u32[]{:S(2)}) copy-start(f32[16,8]{0,1:T(8,128)} %param.21) | copy-start | bytes 1540
  7.6 2.9 %copy-start.12 = (s32[128]{0:T(128)S(1)}, s32[128]{0:T(128)}, u32[]{:S(2)}) copy-start(s32[128]{0:T(128)} %constant.31) | copy-start | bytes 1540
  7.6 2.9 %copy-start.4 = (s32[8]{0:T(128)S(1)}, s32[8]{0:T(128)}, u32[]{:S(2)}) copy-start(s32[8]{0:T(128)} %length_hbm.1) | copy-start | bytes 100
  7.6 2.9 %copy-start.5 = (s32[8]{0:T(128)S(1)}, s32[8]{0:T(128)}, u32[]{:S(2)}) copy-start(s32[8]{0:T(128)} %finished_hbm.1) | copy-start | bytes 100
  7.6 2.9 %copy-start.6 = (s32[1,8,1]{1,2,0:T(1,128)S(1)}, s32[1,8,1]{1,2,0:T(1,128)}, u32[]{:S(2)}) copy-start(s32[1,8,1]{1,2,0:T(1,128)} %param.19) | copy-start | bytes 100
  7.6 5.2 %copy-start.3 = (bf16[8,3584]{1,0:T(8,128)(2,1)S(1)}, bf16[8,3584]{1,0:T(8,128)(2,1)}, u32[]{:S(2)}) copy-start(bf16[8,3584]{1,0:T(8,128)(2,1)} %tokens.1) | copy-start | bytes 172036
  14.4 37.5 %all-to-all-start.1 = ((bf16[128,8,896]{2,1,0:T(8,128)(2,1)}), bf16[128,8,896]{2,1,0:T(8,128)(2,1)S(1)}, u32[]{:S(2)}, u32[]{:S(2)}) async-start(bf16[128,8,896]{2,1,0:T(8,128)(2,1)} %bitcast.25), calls=%async_computation.1 | async-start | bytes 3670016 | tf_op jit(solution)/shard_map/all_to_all | solution.py:267
  51.9 21.4 %all-to-all-start.2 = ((bf16[8,64,512]{2,1,0:T(8,128)(2,1)}), bf16[8,64,512]{2,1,0:T(8,128)(2,1)S(1)}, u32[]{:S(2)}, u32[]{:S(2)}) async-start(bf16[8,64,512]{2,1,0:T(8,128)(2,1)} %broadcast_select_fusion), calls=%async_computation.2 | async-start | bytes 1048576 | tf_op jit(solution)/shard_map/all_to_all | solution.py:310
  55.4 3.1 %copy-start = (bf16[1,3584,1024]{2,1,0:T(8,128)(2,1)S(1)}, bf16[1,3584,1024]{2,1,0:T(8,128)(2,1)}, u32[]{:S(2)}) copy-start(bf16[1,3584,1024]{2,1,0:T(8,128)(2,1)} %w_gate.1) | copy-start | bytes 22020100
  58.4 3.1 %copy-start.1 = (bf16[1,3584,1024]{2,1,0:T(8,128)(2,1)S(1)}, bf16[1,3584,1024]{2,1,0:T(8,128)(2,1)}, u32[]{:S(2)}) copy-start(bf16[1,3584,1024]{2,1,0:T(8,128)(2,1)} %w_up.1) | copy-start | bytes 22020100
  61.5 3.1 %copy-start.2 = (bf16[1,1024,3584]{2,1,0:T(8,128)(2,1)S(1)}, bf16[1,1024,3584]{2,1,0:T(8,128)(2,1)}, u32[]{:S(2)}) copy-start(bf16[1,1024,3584]{2,1,0:T(8,128)(2,1)} %w_down.1) | copy-start | bytes 22020100
  73.3 6.6 %copy-start.8 = (bf16[8,64,512]{2,1,0:T(8,128)(2,1)S(1)}, bf16[8,64,512]{2,1,0:T(8,128)(2,1)}, u32[]{:S(2)}) copy-start(bf16[8,64,512]{2,1,0:T(8,128)(2,1)} %get-tuple-element.16) | copy-start | bytes 1572868
  73.3 33.7 %all-to-all-start.3 = ((bf16[128,8,896]{2,1,0:T(8,128)(2,1)}), bf16[128,8,896]{2,1,0:T(8,128)(2,1)S(1)}, u32[]{:S(2)}, u32[]{:S(2)}) async-start(bf16[128,8,896]{2,1,0:T(8,128)(2,1)} %bitcast.24), calls=%async_computation.3 | async-start | bytes 3670016 | tf_op jit(solution)/shard_map/all_to_all | solution.py:267

commit v2 on v1

--- a/solution.py
+++ b/solution.py
@@ -14,17 +14,6 @@
 
 PARTS = 4
 CAP = 2
-
-DEVICE_ORDER = (
-    23, 44, 105, 64, 100, 28, 5, 34, 111, 118, 84, 50, 77, 79, 37, 43,
-    15, 120, 74, 83, 125, 69, 8, 19, 41, 88, 47, 102, 115, 17, 101, 127,
-    55, 81, 78, 122, 13, 57, 65, 0, 126, 117, 40, 112, 1, 61, 66, 22,
-    107, 76, 62, 89, 116, 103, 110, 36, 82, 30, 85, 9, 3, 95, 6, 51,
-    16, 124, 75, 104, 121, 45, 38, 114, 26, 99, 72, 27, 42, 53, 97, 60,
-    54, 87, 94, 73, 113, 7, 31, 52, 59, 29, 90, 4, 98, 49, 92, 11,
-    21, 39, 48, 93, 10, 67, 123, 24, 32, 108, 63, 119, 12, 71, 14, 20,
-    80, 33, 70, 58, 109, 68, 25, 86, 35, 96, 91, 56, 18, 106, 2, 46,
-)
 
 score_scale = 192.0 ** (-0.5)
 
@@ -112,17 +101,27 @@
     wait_all(start_all([pltpu.make_async_copy(send, out, sems.at[0])]))
 
 
-def routing_kernel(plan, length, finished, routes, score, order, scatter, gather):
-    slots, top = routes.shape
+def routing_kernel(plan_hbm, length_hbm, finished_hbm, routes_hbm, score_hbm, *rest):
+    scatter, gather, plan, length, finished, routes, score, sems = rest
+    pairs = [
+        (plan_hbm, plan),
+        (length_hbm, length),
+        (finished_hbm, finished),
+        (routes_hbm, routes),
+        (score_hbm, score),
+    ]
+    wait_all(start_all([pltpu.make_async_copy(*pair, sems.at[n]) for n, pair in enumerate(pairs)]))
+    top, slots = routes.shape
     lanes = scatter.shape[0]
     experts = lanes // 8
     count = slots // 2
-    names = routes[...]
-    scores = score[...]
+    names = jnp.transpose(routes[...].astype(F32))
+    scores = jnp.transpose(score[...])
+    expert = iota((slots, experts), 1).astype(F32)
     named = jnp.zeros((slots, experts), F32)
     weight = jnp.zeros((slots, experts), F32)
     for k in range(top):
-        hit = names[:, k : k + 1] == order[...]
+        hit = names[:, k : k + 1] == expert
         named = jnp.where(hit, 1.0, named)
         weight = jnp.where(hit, scores[:, k : k + 1], weight)
     weight = 2.5 * weight / jnp.sum(scores, axis=1, keepdims=True)
@@ -175,9 +174,28 @@
     wait_all(copies)
 
 
-def expert_kernel(recv, w_gate, w_up, w_down, out, rows, hidden, results, sent, sems):
+def expert_kernel(recv, w_gate, w_up, w_down, out, *scratch):
+    gates, ups, downs, rows, hidden, results, sent, sems = scratch
     width = recv.shape[1]
     blocks = recv.shape[0] // 256
+    chunk = gates.shape[2]
+    wide = [pl.ds(n * chunk, chunk) for n in range(gates.shape[0])]
+    gate_copies = [
+        pltpu.make_async_copy(w_gate.at[0, :, part], gates.at[n], sems.at[0, n])
+        for n, part in enumerate(wide)
+    ]
+    up_copies = [
+        pltpu.make_async_copy(w_up.at[0, :, part], ups.at[n], sems.at[1, n])
+        for n, part in enumerate(wide)
+    ]
+    down_copies = [
+        pltpu.make_async_copy(w_down.at[0, :, pl.ds(q * width, width)], downs.at[q], sems.at[2, q])
+        for q in range(PARTS)
+    ]
+    for n in range(len(wide)):
+        start_all([gate_copies[n], up_copies[n]])
+    start_all(down_copies)
+
     one, two = iota((256, 256), 0), iota((256, 256), 1)
     apart = ((one & 63) * PARTS + (one >> 6)) == two
     together = ((two & 63) * PARTS + (two >> 6)) == one
@@ -187,19 +205,19 @@
         got = jnp.dot(apart, recv[b * 256 : (b + 1) * 256, :], preferred_element_type=F32)
         got = got.astype(BF16)
         for q in range(PARTS):
-            rows[q, b * 64 : (b + 1) * 64, :] = got[q * 64 : (q + 1) * 64, :]
-
-    gate = up = None
+            part = slice(q * width, (q + 1) * width)
+            rows[b * 64 : (b + 1) * 64, part] = got[q * 64 : (q + 1) * 64, :]
+
+    for n in range(len(wide)):
+        gate_copies[n].wait()
+        gate = jnp.dot(rows[...], gates[n], preferred_element_type=F32)
+        up_copies[n].wait()
+        up = jnp.dot(rows[...], ups[n], preferred_element_type=F32)
+        value = gate / (1.0 + jnp.exp(-gate)) * up
+        hidden[:, n * chunk : (n + 1) * chunk] = value.astype(BF16)
     for q in range(PARTS):
-        part = slice(q * width, (q + 1) * width)
-        more = jnp.dot(rows[q], w_gate[0, part, :], preferred_element_type=F32)
-        gate = more if gate is None else gate + more
-        more = jnp.dot(rows[q], w_up[0, part, :], preferred_element_type=F32)
-        up = more if up is None else up + more
-    hidden[...] = (gate / (1.0 + jnp.exp(-gate)) * up).astype(BF16)
-    for q in range(PARTS):
-        part = slice(q * width, (q + 1) * width)
-        result = jnp.dot(hidden[...], w_down[0, :, part], preferred_element_type=F32).astype(BF16)
+        down_copies[q].wait()
+        result = jnp.dot(hidden[...], downs[q], preferred_element_type=F32).astype(BF16)
         for b in range(blocks):
             results[b, q * 64 : (q + 1) * 64, :] = result[b * 64 : (b + 1) * 64, :]
     copies = []
@@ -207,7 +225,7 @@
         part = pl.ds(b * 256, 256)
         value = jnp.dot(together, results[b], preferred_element_type=F32).astype(BF16)
         sent[part, :] = value
-        copies += start_all([pltpu.make_async_copy(sent.at[part], out.at[part], sems.at[b])])
+        copies += start_all([pltpu.make_async_copy(sent.at[part], out.at[part], sems.at[0, b])])
     wait_all(copies)
 
 
@@ -259,38 +277,47 @@
     hidden = w_gate.shape[2]
     plan = migrate.reshape(replicas)
 
-    order = [list(DEVICE_ORDER)] if devices == len(DEVICE_ORDER) else [list(range(devices))]
-    spread = jnp.broadcast_to(jnp.asarray(order, jnp.int32), (slots, devices))
-
     def exchange(values):
         values = values.reshape(devices, 8, width)
-        values = lax.all_to_all(values, BOTH, 0, 0, axis_index_groups=order, tiled=True)
+        values = lax.all_to_all(values, BOTH, split_axis=0, concat_axis=0, tiled=True)
         return values.reshape(lanes, width)
 
+    def in_hbm(*values):
+        return [pltpu.with_memory_space_constraint(value, pltpu.HBM) for value in values]
+
+    integers = [
+        pltpu.SMEM((replicas,), jnp.int32),
+        pltpu.SMEM((count,), jnp.int32),
+        pltpu.SMEM((count,), jnp.int32),
+    ]
     send = call(
         pick_kernel,
         [(replicas * 8, width)],
         [HBM] * 4,
         (10**6, 10**5),
-        [
-            pltpu.SMEM((replicas,), jnp.int32),
-            pltpu.SMEM((count,), jnp.int32),
-            pltpu.SMEM((count,), jnp.int32),
+        integers
+        + [
             pltpu.VMEM((count, model), BF16),
             pltpu.VMEM((replicas * 8, width), BF16),
             pltpu.SemaphoreType.DMA((4,)),
         ],
         in_hbm=True,
-    )(*[pltpu.with_memory_space_constraint(x, pltpu.HBM) for x in (plan, lengths, finished, tokens)])
+    )(*in_hbm(plan, lengths, finished, tokens))
     arrived = lax.all_to_all(
         send.reshape(replicas, 8, width), "replica", split_axis=0, concat_axis=0, tiled=True
     ).reshape(replicas * 8, width)
     scatter, gather = call(
         routing_kernel,
         [(lanes, 128), (2 * PARTS * slots, lanes)],
-        [SMEM] * 3 + [VMEM] * 3,
+        [HBM] * 5,
         (10**7, 10**6),
-    )(plan, lengths, finished, routes, route_score, spread)
+        integers
+        + [
+            pltpu.VMEM((routes.shape[1], slots), jnp.int32),
+            pltpu.VMEM((routes.shape[1], slots), F32),
+            pltpu.SemaphoreType.DMA((5,)),
+        ],
+    )(*in_hbm(plan, lengths, finished, routes.T, route_score.T))
     outgoing = call(
         dispatch_kernel,
         [(lanes, width)],
@@ -299,6 +326,7 @@
         [pltpu.VMEM((lanes, width), BF16), pltpu.SemaphoreType.DMA((lanes // 256,))],
         in_hbm=True,
     )(scatter, tokens, arrived)
+    queries, outgoing = lax.optimization_barrier((queries, outgoing))
     incoming = exchange(outgoing)
 
     own_length = jnp.where(finished == 0, lengths, 0)
@@ -314,18 +342,21 @@
     results = call(
         expert_kernel,
         [(lanes, width)],
-        [VMEM] * 4,
-        (6 * devices * CAP * model * hidden, 6 * 10**6),
+        [VMEM] + [HBM] * 3,
+        (6 * devices * CAP * model * hidden, 6 * model * hidden),
         [
-            pltpu.VMEM((PARTS, devices * CAP, width), BF16),
+            pltpu.VMEM((4, model, hidden // 4), BF16),
+            pltpu.VMEM((4, model, hidden // 4), BF16),
+            pltpu.VMEM((PARTS, hidden, width), BF16),
+            pltpu.VMEM((devices * CAP, model), BF16),
             pltpu.VMEM((devices * CAP, hidden), BF16),
             pltpu.VMEM((lanes // 256, 256, width), BF16),
             pltpu.VMEM((lanes, width), BF16),
-            pltpu.SemaphoreType.DMA((lanes // 256,)),
+            pltpu.SemaphoreType.DMA((3, 4)),
         ],
-        24,
+        46,
         True,
-    )(incoming, *[pltpu.with_memory_space_constraint(w, pltpu.VMEM) for w in (w_gate, w_up, w_down)])
+    )(incoming, *in_hbm(w_gate, w_up, w_down))
     returned = exchange(results)
     expert_out = call(combine_kernel, [(slots, model)], [VMEM] * 2, (2 * 10**8, 2 * 10**6))(
         gather, returned

time: 109 us -> 106 us (0.972)
  local copies, waits for them, and re-layouts: 14.5 us -> 3.78 us
  Pallas kernels: 14.2 us -> 20.8 us
  other arithmetic: 2.83 us -> 4.14 us
  matrix products: 2.25 us -> 3.41 us
    unnamed x29 -> x13, local copies, waits for them, and re-layouts: 11 us -> 2.4 us
    pallas_call x2, Pallas kernels: 9.73 us -> 16.5 us  [the longest x1 15.1 us: on_device(): call(expert_kernel, [(lanes, width)], [VMEM] + [HBM] * 3, (6 * devices *...]
    dot_general x1, matrix products: 0.45 us -> 1.76 us  [attend(): jnp.einsum('nhl,ntl->nht', per_head, latent_rows, preferred_element_type=...]
    reshape x1, local copies, waits for them, and re-layouts: 1.91 us -> 0.8 us  [attend(): per_head = query_rows.reshape(row_count, HEADS, LAT)]
  transfers between devices with their start and end apart: 4 -> 4, of which waited for: 3 -> 3; matrix products, arithmetic and copies ran while one was open for 10% -> 10% of each run, Pallas kernels for 9% -> 16%
where the time goes in v2:
time: 106 us; the launch traced here: 105 us
  waiting for transfers between devices  48.1 us (45%)
  starting transfers between devices  24.3 us (23%)
  Pallas kernels  20.8 us (20%)
  other arithmetic  4.14 us (4%)
  local copies, waits for them, and re-layouts  3.78 us (4%)
  matrix products  3.41 us (3%)
    all_to_all x2, waiting for transfers between devices, exchange(): lax.all_to_all(values, BOTH, split_axis=0, concat_axis=0, tiled=True)  46.4 us
    all_to_all x2, starting transfers between devices, exchange(): lax.all_to_all(values, BOTH, split_axis=0, concat_axis=0, tiled=True)  16.4 us
    pallas_call x1, Pallas kernels, on_device(): call(expert_kernel, [(lanes, width)], [VMEM] + [HBM] * 3, (6 * devices *...  15.1 us
    all_to_all x1, starting transfers between devices, on_device(): lax.all_to_all(send.reshape(replicas, 8, width), 'replica', split_axis=0,...  4.4 us
    all_to_all x1, starting transfers between devices, on_device(): lax.all_to_all(leave, 'replica', split_axis=0, concat_axis=0, tiled=True)  3.49 us
    unnamed x13, local copies, waits for them, and re-layouts  2.4 us
  transfers between devices with their start and end apart: 4, of which 3 were waited for; matrix products, arithmetic and copies ran while one was open for 10% of the time, Pallas kernels for 16%

profile of v2, /device:TPU:0, one launch (start us, length us, event | category | flops | bytes accessed | tf_op | source)
XLA Modules:
  0.0 105.4 jit_solution(6512183354170390166)
XLA Ops:
  0.6 1.7 %shard_map.132 = bf16[64,896]{1,0:T(8,128)(2,1)} custom-call(s32[8]{0:T(128)} %bitcast.31, s32[8]{0:T(128)} %length_hbm.3, s32[8]{0:T(128)} %finished_hbm.3, bf16[8,3584]{1,0:T(8,128)(2,1)} %tokens.1), custom_call_target="tpu_custom_call" | custom-call | flops 1000000 | bytes 100000 | tf_op jit(solution)/shard_map/pallas_call | solution.py:293
  2.3 4.4 %all-to-all-start = ((bf16[8,8,896]{2,1,0:T(8,128)(2,1)}), bf16[8,8,896]{2,1,0:T(8,128)(2,1)S(1)}, u32[]{:S(2)}, u32[]{:S(2)}) async-start(bf16[8,8,896]{2,1,0:T(8,128)(2,1)} %bitcast.27), calls=%async_computation | async-start | bytes 229376 | tf_op jit(solution)/shard_map/all_to_all | solution.py:306
  6.7 0.7 fusion.11
  7.5 0.7 maximum_bitcast_fusion
  8.1 0.7 compare_convert_fusion
  8.8 0.1 iota_compare_fusion
  8.9 0.7 slice_convert_fusion
  9.6 1.4 %shard_map.131 = (bf16[1024,128]{1,0:T(8,128)(2,1)S(1)}, bf16[128,1024]{1,0:T(8,128)(2,1)S(1)}) custom-call(s32[8]{0:T(128)} %bitcast.33, s32[8]{0:T(128)} %length_hbm.3, s32[8]{0:T(128)} %finished_hbm.3, s32[8,16]{1,0:T(8,128)} %bitcast.34, f32[8,16]{1,0:T(8,128)} %bitcast.35), custom_call_target="tpu_custom_call" | custom-call | flops 10000000 | bytes 1000000 | tf_op jit(solution)/shard_map/pallas_call | solution.py:309
  10.9 1.7 %all-to-all-done = bf16[8,8,896]{2,1,0:T(8,128)(2,1)S(1)} async-done(((bf16[8,8,896]{2,1,0:T(8,128)(2,1)}), bf16[8,8,896]{2,1,0:T(8,128)(2,1)S(1)}, u32[]{:S(2)}, u32[]{:S(2)}) %all-to-all-start) | async-done | bytes 114720 | tf_op jit(solution)/shard_map/all_to_all | solution.py:306
  12.7 0.8 copy-done
  13.5 1.6 %shard_map.133 = bf16[1024,896]{1,0:T(8,128)(2,1)} custom-call(bf16[1024,128]{1,0:T(8,128)(2,1)S(1)} %get-tuple-element.8.scatter, bf16[8,3584]{1,0:T(8,128)(2,1)S(1)} %copy-done, bf16[64,896]{1,0:T(8,128)(2,1)S(1)} %bitcast.22), custom_call_target="tpu_custom_call" | custom-call | flops 200000000 | bytes 2000000 | tf_op jit(solution)/shard_map/pallas_call | solution.py:321
  15.1 0.0 copy-start.5
  15.1 0.0 copy-start.2
  15.1 0.0 copy-start.4
  15.1 9.8 %all-to-all-start.1 = ((bf16[128,8,896]{2,1,0:T(8,128)(2,1)}), bf16[128,8,896]{2,1,0:T(8,128)(2,1)S(1)}, u32[]{:S(2)}, u32[]{:S(2)}) async-start(bf16[128,8,896]{2,1,0:T(8,128)(2,1)} %bitcast.24), calls=%async_computation.1 | async-start | bytes 3670016 | tf_op jit(solution)/shard_map/all_to_all | solution.py:282
  25.0 0.8 reshape.77
  25.8 0.0 copy-start.1
  25.8 0.3 fusion.9
  26.1 1.8 %fusion.14 = (f32[8,64]{1,0:T(8,128)S(1)}, f32[8,64,128]{2,1,0:T(8,128)S(1)}) fusion(bf16[8,64,576]{2,1,0:T(8,128)(2,1)S(1)} %reshape.77, bf16[8,128,576]{1,2,0:T(8,128)(2,1)} %param.14, pred[8,128]{1,0:T(8,128)(4,1)S(1)} %iota_compare_fusion), kind=kOutput, calls=%fused_computation.30 | convolution fusion | flops 75693568 | bytes 2034688 | tf_op jit(solution)/shard_map/nhl,ntl->nht/dot_general | solution.py:33
  27.9 0.3 fusion.5
  28.2 1.3 %broadcast_select_fusion.1 = (bf16[8,64,512]{2,1,0:T(8,128)(2,1)}, bf16[8,64,512]{2,1,0:T(8,128)(2,1)S(1)}) fusion(pred[8]{0:T(512)(128)(4,1)S(1)} %fusion.11, f32[8]{0:T(128)S(1)} %get-tuple-element.14, f32[8,64]{1,0:T(8,128)S(1)} %get-tuple-element.17, f32[8,512]{1,0:T(8,128)S(1)} %slice_convert_fusion, f32[8,64]{1,0:T(8,128)S(1)} %convert_element_type.21, ...), kind=kOutput, calls=%fused_computation.10 | convolution fusion | flops 68812800 | bytes 2388992 | tf_op jit(solution)/shard_map/nht,ntv->nhv/dot_general | solution.py:43
  29.6 0.6 gather_fusion
  30.1 0.9 broadcast_select_fusion
  31.0 21.0 %all-to-all-done.1 = bf16[128,8,896]{2,1,0:T(8,128)(2,1)S(1)} async-done(((bf16[128,8,896]{2,1,0:T(8,128)(2,1)}), bf16[128,8,896]{2,1,0:T(8,128)(2,1)S(1)}, u32[]{:S(2)}, u32[]{:S(2)}) %all-to-all-start.1) | async-done | bytes 1835040 | tf_op jit(solution)/shard_map/all_to_all | solution.py:282
  52.0 3.5 %all-to-all-start.2 = ((bf16[8,64,512]{2,1,0:T(8,128)(2,1)}), bf16[8,64,512]{2,1,0:T(8,128)(2,1)S(1)}, u32[]{:S(2)}, u32[]{:S(2)}) async-start(bf16[8,64,512]{2,1,0:T(8,128)(2,1)} %broadcast_select_fusion), calls=%async_computation.2 | async-start | bytes 1048576 | tf_op jit(solution)/shard_map/all_to_all | solution.py:338
  55.5 15.1 %shard_map.134 = bf16[1024,896]{1,0:T(8,128)(2,1)} custom-call(bf16[1024,896]{1,0:T(8,128)(2,1)S(1)} %bitcast.20, bf16[1,3584,1024]{2,1,0:T(8,128)(2,1)} %w_gate.1, bf16[1,3584,1024]{2,1,0:T(8,128)(2,1)} %w_up.1, bf16[1,1024,3584]{2,1,0:T(8,128)(2,1)} %w_down.1), custom_call_target="tpu_custom_call" | custom-call | flops 5637144576 | bytes 22020096 | tf_op jit(solution)/shard_map/pallas_call | solution.py:342
  70.7 0.0 copy-start.3
  70.7 6.6 %all-to-all-start.3 = ((bf16[128,8,896]{2,1,0:T(8,128)(2,1)}), bf16[128,8,896]{2,1,0:T(8,128)(2,1)S(1)}, u32[]{:S(2)}, u32[]{:S(2)}) async-start(bf16[128,8,896]{2,1,0:T(8,128)(2,1)} %bitcast.23), calls=%async_computation.3 | async-start | bytes 3670016 | tf_op jit(solution)/shard_map/all_to_all | solution.py:282
  77.3 0.1 pad_maximum_fusion
  77.4 1.5 %copy.19 = bf16[2,8,64,512]{3,1,2,0:T(8,128)(2,1)} copy(bf16[2,8,64,512]{3,2,1,0:T(8,128)(2,1)S(1)} %bitcast.25) | data formatting | bytes 2097152
  78.9 25.4 %all-to-all-done.3 = bf16[128,8,896]{2,1,0:T(8,128)(2,1)S(1)} async-done(((bf16[128,8,896]{2,1,0:T(8,128)(2,1)}), bf16[128,8,896]{2,1,0:T(8,128)(2,1)S(1)}, u32[]{:S(2)}, u32[]{:S(2)}) %all-to-all-start.3) | async-done | bytes 1835040 | tf_op jit(solution)/shard_map/all_to_all | solution.py:282
  104.3 1.1 %shard_map.135 = bf16[16,3584]{1,0:T(8,128)(2,1)} custom-call(bf16[128,1024]{1,0:T(8,128)(2,1)S(1)} %get-tuple-element.12.gather, bf16[1024,896]{1,0:T(8,128)(2,1)S(1)} %bitcast.21), custom_call_target="tpu_custom_call" | custom-call | flops 200000000 | bytes 2000000 | tf_op jit(solution)/shard_map/pallas_call | solution.py:361
  (12 shorter events, 0.0 us)
Async XLA Ops:
  2.3 10.4 %all-to-all-start = ((bf16[8,8,896]{2,1,0:T(8,128)(2,1)}), bf16[8,8,896]{2,1,0:T(8,128)(2,1)S(1)}, u32[]{:S(2)}, u32[]{:S(2)}) async-start(bf16[8,8,896]{2,1,0:T(8,128)(2,1)} %bitcast.27), calls=%async_computation | async-start | bytes 229376 | tf_op jit(solution)/shard_map/all_to_all | solution.py:306
  12.7 0.8 copy-start
  15.1 9.9 %copy-start.5 = (s32[1,8,1]{1,2,0:T(1,128)S(1)}, s32[1,8,1]{1,2,0:T(1,128)}, u32[]{:S(2)}) copy-start(s32[1,8,1]{1,2,0:T(1,128)} %param.18) | copy-start | bytes 100
  15.1 9.9 %copy-start.2 = (bf16[8,36864]{1,0:T(8,128)(2,1)S(1)}, bf16[8,36864]{1,0:T(8,128)(2,1)}, u32[]{:S(2)}) copy-start(bf16[8,36864]{1,0:T(8,128)(2,1)} %param.13) | copy-start | bytes 1769476
  15.1 10.7 %copy-start.4 = (bf16[8,576]{1,0:T(8,128)(2,1)S(1)}, bf16[8,576]{1,0:T(8,128)(2,1)}, u32[]{:S(2)}) copy-start(bf16[8,576]{1,0:T(8,128)(2,1)} %param.15) | copy-start | bytes 27652
  15.1 36.9 %all-to-all-start.1 = ((bf16[128,8,896]{2,1,0:T(8,128)(2,1)}), bf16[128,8,896]{2,1,0:T(8,128)(2,1)S(1)}, u32[]{:S(2)}, u32[]{:S(2)}) async-start(bf16[128,8,896]{2,1,0:T(8,128)(2,1)} %bitcast.24), calls=%async_computation.1 | async-start | bytes 3670016 | tf_op jit(solution)/shard_map/all_to_all | solution.py:282
  25.8 2.4 %copy-start.1 = (bf16[8,128,576]{1,2,0:T(8,128)(2,1)S(1)}, bf16[8,128,576]{1,2,0:T(8,128)(2,1)}, u32[]{:S(2)}) copy-start(bf16[8,128,576]{1,2,0:T(8,128)(2,1)} %param.14) | copy-start | bytes 3538948
  52.0 18.6 %all-to-all-start.2 = ((bf16[8,64,512]{2,1,0:T(8,128)(2,1)}), bf16[8,64,512]{2,1,0:T(8,128)(2,1)S(1)}, u32[]{:S(2)}, u32[]{:S(2)}) async-start(bf16[8,64,512]{2,1,0:T(8,128)(2,1)} %broadcast_select_fusion), calls=%async_computation.2 | async-start | bytes 1048576 | tf_op jit(solution)/shard_map/all_to_all | solution.py:338
  70.7 6.6 %copy-start.3 = (bf16[8,64,512]{2,1,0:T(8,128)(2,1)S(1)}, bf16[8,64,512]{2,1,0:T(8,128)(2,1)}, u32[]{:S(2)}) copy-start(bf16[8,64,512]{2,1,0:T(8,128)(2,1)} %get-tuple-element.20) | copy-start | bytes 1572868
  70.7 33.6 %all-to-all-start.3 = ((bf16[128,8,896]{2,1,0:T(8,128)(2,1)}), bf16[128,8,896]{2,1,0:T(8,128)(2,1)S(1)}, u32[]{:S(2)}, u32[]{:S(2)}) async-start(bf16[128,8,896]{2,1,0:T(8,128)(2,1)} %bitcast.23), calls=%async_computation.3 | async-start | bytes 3670016 | tf_op jit(solution)/shard_map/all_to_all | solution.py:282

commit v3 on v2

--- a/solution.py
+++ b/solution.py
@@ -101,16 +101,18 @@
     wait_all(start_all([pltpu.make_async_copy(send, out, sems.at[0])]))
 
 
-def routing_kernel(plan_hbm, length_hbm, finished_hbm, routes_hbm, score_hbm, *rest):
-    scatter, gather, plan, length, finished, routes, score, sems = rest
+def routing_kernel(plan_hbm, length_hbm, finished_hbm, routes_hbm, score_hbm, tokens_hbm, *rest):
+    scatter, gather, flat, plan, length, finished, routes, score, tokens, sems = rest
     pairs = [
         (plan_hbm, plan),
         (length_hbm, length),
         (finished_hbm, finished),
         (routes_hbm, routes),
         (score_hbm, score),
+        (tokens_hbm, tokens),
     ]
     wait_all(start_all([pltpu.make_async_copy(*pair, sems.at[n]) for n, pair in enumerate(pairs)]))
+    flat[...] = sub_rows(tokens[...], flat.shape[1])
     top, slots = routes.shape
     lanes = scatter.shape[0]
     experts = lanes // 8
@@ -161,10 +163,8 @@
 
 def dispatch_kernel(scatter, tokens, arrived, out, block, sems):
     lanes, width = out.shape
-    pad = scatter.shape[1] - PARTS * tokens.shape[0] - arrived.shape[0]
-    pieces = [tokens[:, q * width : (q + 1) * width].astype(F32) for q in range(PARTS)]
-    pieces += [arrived[...].astype(F32), jnp.zeros((pad, width), F32)]
-    flat = jnp.concatenate(pieces, axis=0).astype(BF16)
+    pad = scatter.shape[1] - tokens.shape[0] - arrived.shape[0]
+    flat = jnp.concatenate([tokens[...], arrived[...], jnp.zeros((pad, width), BF16)], axis=0)
     copies = []
     for b in range(lanes // 256):
         part = pl.ds(b * 256, 256)
@@ -175,25 +175,19 @@
 
 
 def expert_kernel(recv, w_gate, w_up, w_down, out, *scratch):
-    gates, ups, downs, rows, hidden, results, sent, sems = scratch
+    gates, ups, downs, rows, hidden, partial, results, sent, sems = scratch
     width = recv.shape[1]
     blocks = recv.shape[0] // 256
-    chunk = gates.shape[2]
-    wide = [pl.ds(n * chunk, chunk) for n in range(gates.shape[0])]
-    gate_copies = [
-        pltpu.make_async_copy(w_gate.at[0, :, part], gates.at[n], sems.at[0, n])
-        for n, part in enumerate(wide)
-    ]
-    up_copies = [
-        pltpu.make_async_copy(w_up.at[0, :, part], ups.at[n], sems.at[1, n])
-        for n, part in enumerate(wide)
-    ]
-    down_copies = [
-        pltpu.make_async_copy(w_down.at[0, :, pl.ds(q * width, width)], downs.at[q], sems.at[2, q])
-        for q in range(PARTS)
-    ]
-    for n in range(len(wide)):
-        start_all([gate_copies[n], up_copies[n]])
+    half = downs.shape[1]
+    gate_copies, up_copies, down_copies = [], [], []
+    for q in range(PARTS):
+        part = pl.ds(q * width, width)
+        gate_copies.append(pltpu.make_async_copy(w_gate.at[0, part, :], gates.at[q], sems.at[0, q]))
+        up_copies.append(pltpu.make_async_copy(w_up.at[0, part, :], ups.at[q], sems.at[1, q]))
+        start_all([gate_copies[q], up_copies[q]])
+    for n in range(downs.shape[0]):
+        part = pl.ds(n * half, half)
+        down_copies.append(pltpu.make_async_copy(w_down.at[0, part, :], downs.at[n], sems.at[2, n]))
     start_all(down_copies)
 
     one, two = iota((256, 256), 0), iota((256, 256), 1)
@@ -205,19 +199,26 @@
         got = jnp.dot(apart, recv[b * 256 : (b + 1) * 256, :], preferred_element_type=F32)
         got = got.astype(BF16)
         for q in range(PARTS):
-            part = slice(q * width, (q + 1) * width)
-            rows[b * 64 : (b + 1) * 64, part] = got[q * 64 : (q + 1) * 64, :]
-
-    for n in range(len(wide)):
-        gate_copies[n].wait()
-        gate = jnp.dot(rows[...], gates[n], preferred_element_type=F32)
-        up_copies[n].wait()
-        up = jnp.dot(rows[...], ups[n], preferred_element_type=F32)
-        value = gate / (1.0 + jnp.exp(-gate)) * up
-        hidden[:, n * chunk : (n + 1) * chunk] = value.astype(BF16)
-    for q in range(PARTS):
-        down_copies[q].wait()
-        result = jnp.dot(hidden[...], downs[q], preferred_element_type=F32).astype(BF16)
+            rows[q, b * 64 : (b + 1) * 64, :] = got[q * 64 : (q + 1) * 64, :]
+
+    gate = up = None
+    for q in range(PARTS):
+        gate_copies[q].wait()
+        more = jnp.dot(rows[q], gates[q], preferred_element_type=F32)
+        gate = more if gate is None else gate + more
+        up_copies[q].wait()
+        more = jnp.dot(rows[q], ups[q], preferred_element_type=F32)
+        up = more if up is None else up + more
+    hidden[...] = (gate / (1.0 + jnp.exp(-gate)) * up).astype(BF16)
+    down_copies[0].wait()
+    for q in range(PARTS):
+        part = slice(q * width, (q + 1) * width)
+        partial[q] = jnp.dot(hidden[:, :half], downs[0, :, part], preferred_element_type=F32)
+    down_copies[1].wait()
+    for q in range(PARTS):
+        part = slice(q * width, (q + 1) * width)
+        result = jnp.dot(hidden[:, half:], downs[1, :, part], preferred_element_type=F32)
+        result = (partial[q] + result).astype(BF16)
         for b in range(blocks):
             results[b, q * 64 : (q + 1) * 64, :] = result[b * 64 : (b + 1) * 64, :]
     copies = []
@@ -306,18 +307,19 @@
     arrived = lax.all_to_all(
         send.reshape(replicas, 8, width), "replica", split_axis=0, concat_axis=0, tiled=True
     ).reshape(replicas * 8, width)
-    scatter, gather = call(
+    scatter, gather, flat = call(
         routing_kernel,
-        [(lanes, 128), (2 * PARTS * slots, lanes)],
-        [HBM] * 5,
+        [(lanes, 128), (2 * PARTS * slots, lanes), (PARTS * count, width)],
+        [HBM] * 6,
         (10**7, 10**6),
         integers
         + [
             pltpu.VMEM((routes.shape[1], slots), jnp.int32),
             pltpu.VMEM((routes.shape[1], slots), F32),
-            pltpu.SemaphoreType.DMA((5,)),
+            pltpu.VMEM((count, model), BF16),
+            pltpu.SemaphoreType.DMA((6,)),
         ],
-    )(*in_hbm(plan, lengths, finished, routes.T, route_score.T))
+    )(*in_hbm(plan, lengths, finished, routes.T, route_score.T, tokens))
     outgoing = call(
         dispatch_kernel,
         [(lanes, width)],
@@ -325,8 +327,10 @@
         (2 * 10**8, 2 * 10**6),
         [pltpu.VMEM((lanes, width), BF16), pltpu.SemaphoreType.DMA((lanes // 256,))],
         in_hbm=True,
-    )(scatter, tokens, arrived)
-    queries, outgoing = lax.optimization_barrier((queries, outgoing))
+    )(scatter, flat, arrived)
+    held = (queries, latent_cache, new_latent, lengths, finished, plan, outgoing)
+    held = lax.optimization_barrier(held)
+    queries, latent_cache, new_latent, lengths, finished, plan, outgoing = held
     incoming = exchange(outgoing)
 
     own_length = jnp.where(finished == 0, lengths, 0)
@@ -345,11 +349,12 @@
         [VMEM] + [HBM] * 3,
         (6 * devices * CAP * model * hidden, 6 * model * hidden),
         [
-            pltpu.VMEM((4, model, hidden // 4), BF16),
-            pltpu.VMEM((4, model, hidden // 4), BF16),
-            pltpu.VMEM((PARTS, hidden, width), BF16),
-            pltpu.VMEM((devices * CAP, model), BF16),
+            pltpu.VMEM((PARTS, width, hidden), BF16),
+            pltpu.VMEM((PARTS, width, hidden), BF16),
+            pltpu.VMEM((2, hidden // 2, model), BF16),
+            pltpu.VMEM((PARTS, devices * CAP, width), BF16),
             pltpu.VMEM((devices * CAP, hidden), BF16),
+            pltpu.VMEM((PARTS, devices * CAP, width), F32),
             pltpu.VMEM((lanes // 256, 256, width), BF16),
             pltpu.VMEM((lanes, width), BF16),
             pltpu.SemaphoreType.DMA((3, 4)),

time: 106 us -> 102 us (0.962)
  Pallas kernels: 20.8 us -> 17.9 us
  local copies, waits for them, and re-layouts: 3.78 us -> 6.3 us
  waiting for transfers between devices: 48.1 us -> 45.8 us
  other arithmetic: 4.14 us -> 2.66 us
    all_to_all x2, waiting for transfers between devices: 46.4 us -> 41.3 us  [exchange(): lax.all_to_all(values, BOTH, split_axis=0, concat_axis=0, tiled=True)]
    pallas_call x1, Pallas kernels: 15.1 us -> 12 us  [on_device(): call(expert_kernel, [(lanes, width)], [VMEM] + [HBM] * 3, (6 * devices *...]
    all_to_all x1, waiting for transfers between devices: 1.74 us -> 4.44 us  [on_device(): lax.all_to_all(send.reshape(replicas, 8, width), 'replica', split_axis=0,...]
    reshape x1, local copies, waits for them, and re-layouts: 0.8 us -> 2.69 us  [attend(): per_head = query_rows.reshape(row_count, HEADS, LAT)]
    optimization_barrier x0 -> x1, local copies, waits for them, and re-layouts: none -> 1.45 us  [on_device(): held = lax.optimization_barrier(held)]
    dot_general x1, matrix products: 1.35 us -> 2.46 us  [attend(): jnp.einsum('nht,ntv->nhv', weights.astype(BF16), latent_rows[:, :, :VDIM]...]
    unnamed x13 -> x15, local copies, waits for them, and re-layouts: 2.4 us -> 1.59 us
  transfers between devices with their start and end apart: 4 -> 4, of which waited for: 3 -> 3; matrix products, arithmetic and copies ran while one was open for 10% -> 13% of each run, Pallas kernels for 16% -> 13%
where the time goes in v3:
time: 102 us
  waiting for transfers between devices  45.8 us (45%)
  starting transfers between devices  23.7 us (23%)
  Pallas kernels  17.9 us (18%)
  local copies, waits for them, and re-layouts  6.3 us (6%)
  matrix products  4.36 us (4%)
  other arithmetic  2.66 us (3%)
    all_to_all x2, waiting for transfers between devices, exchange(): lax.all_to_all(values, BOTH, split_axis=0, concat_axis=0, tiled=True)  41.3 us
    all_to_all x2, starting transfers between devices, exchange(): lax.all_to_all(values, BOTH, split_axis=0, concat_axis=0, tiled=True)  15.8 us
    pallas_call x1, Pallas kernels, on_device(): call(expert_kernel, [(lanes, width)], [VMEM] + [HBM] * 3, (6 * devices *...  12 us
    all_to_all x1, waiting for transfers between devices, on_device(): lax.all_to_all(send.reshape(replicas, 8, width), 'replica', split_axis=0,...  4.44 us
    all_to_all x1, starting transfers between devices, on_device(): lax.all_to_all(send.reshape(replicas, 8, width), 'replica', split_axis=0,...  4.4 us
    all_to_all x1, starting transfers between devices, on_device(): lax.all_to_all(leave, 'replica', split_axis=0, concat_axis=0, tiled=True)  3.49 us
    reshape x1, local copies, waits for them, and re-layouts, attend(): per_head = query_rows.reshape(row_count, HEADS, LAT)  2.69 us
    dot_general x1, matrix products, attend(): jnp.einsum('nht,ntv->nhv', weights.astype(BF16), latent_rows[:, :, :VDIM]...  2.46 us
  transfers between devices with their start and end apart: 4, of which 3 were waited for; matrix products, arithmetic and copies ran while one was open for 13% of the time, Pallas kernels for 13%

profile of v3, /device:TPU:0, one launch (start us, length us, event | category | flops | bytes accessed | tf_op | source)
XLA Modules:
  0.0 101.5 jit_solution(16586793859648350604)
XLA Ops:
  0.6 0.0 copy-start.5
  0.6 0.0 copy-start.4
  0.7 0.0 copy-start.6
  0.7 1.7 %shard_map.132 = bf16[64,896]{1,0:T(8,128)(2,1)} custom-call(s32[8]{0:T(128)} %bitcast.28, s32[8]{0:T(128)} %length_hbm.3, s32[8]{0:T(128)} %finished_hbm.3, bf16[8,3584]{1,0:T(8,128)(2,1)} %tokens_hbm.3), custom_call_target="tpu_custom_call" | custom-call | flops 1000000 | bytes 100000 | tf_op jit(solution)/shard_map/pallas_call | solution.py:294
  2.4 4.4 %all-to-all-start = ((bf16[8,8,896]{2,1,0:T(8,128)(2,1)}), bf16[8,8,896]{2,1,0:T(8,128)(2,1)S(1)}, u32[]{:S(2)}, u32[]{:S(2)}) async-start(bf16[8,8,896]{2,1,0:T(8,128)(2,1)} %bitcast.24), calls=%async_computation | async-start | bytes 229376 | tf_op jit(solution)/shard_map/all_to_all | solution.py:307
  6.8 1.5 %shard_map.131 = (bf16[1024,128]{1,0:T(8,128)(2,1)S(1)}, bf16[128,1024]{1,0:T(8,128)(2,1)S(1)}, bf16[32,896]{1,0:T(8,128)(2,1)S(1)}) custom-call(s32[8]{0:T(128)} %bitcast.29, s32[8]{0:T(128)} %length_hbm.3, s32[8]{0:T(128)} %finished_hbm.3, s32[8,16]{1,0:T(8,128)} %bitcast.33, f32[8,16]{1,0:T(8,128)} %bitcast.34, bf16[8,3584]{1,0:T(8,128)(2,1)} %tokens_hbm.3), custom_call_target="tpu_custom_call" | custom-call | flops 10000000 | bytes 1000000 | tf_op jit(solution)/shard_map/pallas_call | solution.py:310
  8.3 4.4 %all-to-all-done = bf16[8,8,896]{2,1,0:T(8,128)(2,1)S(1)} async-done(((bf16[8,8,896]{2,1,0:T(8,128)(2,1)}), bf16[8,8,896]{2,1,0:T(8,128)(2,1)S(1)}, u32[]{:S(2)}, u32[]{:S(2)}) %all-to-all-start) | async-done | bytes 114720 | tf_op jit(solution)/shard_map/all_to_all | solution.py:307
  12.7 1.6 %shard_map.133 = bf16[1024,896]{1,0:T(8,128)(2,1)} custom-call(bf16[1024,128]{1,0:T(8,128)(2,1)S(1)} %get-tuple-element.14.scatter, bf16[32,896]{1,0:T(8,128)(2,1)S(1)} %get-tuple-element.15.tokens, bf16[64,896]{1,0:T(8,128)(2,1)S(1)} %bitcast.19), custom_call_target="tpu_custom_call" | custom-call | flops 200000000 | bytes 2000000 | tf_op jit(solution)/shard_map/pallas_call | solution.py:323
  14.3 0.0 copy-done.5
  14.3 0.5 compare_convert_fusion
  14.8 0.1 iota_compare_fusion
  14.9 9.2 %all-to-all-start.1 = ((bf16[128,8,896]{2,1,0:T(8,128)(2,1)}), bf16[128,8,896]{2,1,0:T(8,128)(2,1)S(1)}, u32[]{:S(2)}, u32[]{:S(2)}) async-start(bf16[128,8,896]{2,1,0:T(8,128)(2,1)} %bitcast.21), calls=%async_computation.1 | async-start | bytes 3670016 | tf_op jit(solution)/shard_map/all_to_all | solution.py:283
  24.1 2.7 %reshape.64 = bf16[8,64,576]{2,1,0:T(8,128)(2,1)} reshape(bf16[8,36864]{1,0:T(8,128)(2,1)} %param.13) | data formatting | bytes 1179648 | tf_op jit(solution)/shard_map/reshape | solution.py:31
  26.8 1.6 %fusion.14 = (f32[8,64]{1,0:T(8,128)S(1)}, f32[8,64,128]{2,1,0:T(8,128)S(1)}) fusion(bf16[8,64,576]{2,1,0:T(8,128)(2,1)} %reshape.64, bf16[8,128,576]{1,2,0:T(8,128)(2,1)S(1)} %copy-done, pred[8,128]{1,0:T(8,128)(4,1)S(1)} %iota_compare_fusion), kind=kOutput, calls=%fused_computation.30 | convolution fusion | flops 75693568 | bytes 2034688 | tf_op jit(solution)/shard_map/nhl,ntl->nht/dot_general | solution.py:33
  28.4 0.3 fusion.9
  28.7 1.5 %copy.15 = bf16[8,128,576]{2,1,0:T(8,128)(2,1)} copy(bf16[8,128,576]{1,2,0:T(8,128)(2,1)S(1)} %copy-done) | data formatting | bytes 2359296 | tf_op jit(solution)/shard_map/optimization_barrier | solution.py:332
  30.2 0.3 fusion.5
  30.5 0.1 fusion.11
  30.6 0.7 slice_convert_fusion
  31.3 2.5 %broadcast_select_fusion.1 = (bf16[8,64,512]{2,1,0:T(8,128)(2,1)}, bf16[8,64,512]{2,1,0:T(8,128)(2,1)S(1)}) fusion(pred[8]{0:T(512)(128)(4,1)S(1)} %fusion.11, f32[8]{0:T(128)} %get-tuple-element.26, f32[8,64]{1,0:T(8,128)S(1)} %get-tuple-element.29, f32[8,512]{1,0:T(8,128)S(1)} %slice_convert_fusion, f32[8,64]{1,0:T(8,128)S(1)} %convert_element_type.21, ...), kind=kOutput, calls=%fused_computation.10 | convolution fusion | flops 68812800 | bytes 2382344 | tf_op jit(solution)/shard_map/nht,ntv->nhv/dot_general | solution.py:43
  33.8 0.6 gather_fusion
  34.4 0.9 broadcast_select_fusion
  35.3 15.9 %all-to-all-done.1 = bf16[128,8,896]{2,1,0:T(8,128)(2,1)S(1)} async-done(((bf16[128,8,896]{2,1,0:T(8,128)(2,1)}), bf16[128,8,896]{2,1,0:T(8,128)(2,1)S(1)}, u32[]{:S(2)}, u32[]{:S(2)}) %all-to-all-start.1) | async-done | bytes 1835040 | tf_op jit(solution)/shard_map/all_to_all | solution.py:283
  51.2 3.5 %all-to-all-start.2 = ((bf16[8,64,512]{2,1,0:T(8,128)(2,1)}), bf16[8,64,512]{2,1,0:T(8,128)(2,1)S(1)}, u32[]{:S(2)}, u32[]{:S(2)}) async-start(bf16[8,64,512]{2,1,0:T(8,128)(2,1)} %broadcast_select_fusion), calls=%async_computation.2 | async-start | bytes 1048576 | tf_op jit(solution)/shard_map/all_to_all | solution.py:342
  54.7 12.0 %shard_map.134 = bf16[1024,896]{1,0:T(8,128)(2,1)} custom-call(bf16[1024,896]{1,0:T(8,128)(2,1)S(1)} %bitcast.17, bf16[1,3584,1024]{2,1,0:T(8,128)(2,1)} %w_gate.1, bf16[1,3584,1024]{2,1,0:T(8,128)(2,1)} %w_up.1, bf16[1,1024,3584]{2,1,0:T(8,128)(2,1)} %w_down.1), custom_call_target="tpu_custom_call" | custom-call | flops 5637144576 | bytes 22020096 | tf_op jit(solution)/shard_map/pallas_call | solution.py:346
  66.7 0.0 all-to-all-done.2
  66.8 0.0 copy-start.2
  66.8 6.6 %all-to-all-start.3 = ((bf16[128,8,896]{2,1,0:T(8,128)(2,1)}), bf16[128,8,896]{2,1,0:T(8,128)(2,1)S(1)}, u32[]{:S(2)}, u32[]{:S(2)}) async-start(bf16[128,8,896]{2,1,0:T(8,128)(2,1)} %bitcast.20), calls=%async_computation.3 | async-start | bytes 3670016 | tf_op jit(solution)/shard_map/all_to_all | solution.py:283
  73.4 0.1 pad_maximum_fusion
  73.5 1.5 %copy.18 = bf16[2,8,64,512]{3,1,2,0:T(8,128)(2,1)} copy(bf16[2,8,64,512]{3,2,1,0:T(8,128)(2,1)S(1)} %bitcast.22) | data formatting | bytes 2097152
  75.0 25.4 %all-to-all-done.3 = bf16[128,8,896]{2,1,0:T(8,128)(2,1)S(1)} async-done(((bf16[128,8,896]{2,1,0:T(8,128)(2,1)}), bf16[128,8,896]{2,1,0:T(8,128)(2,1)S(1)}, u32[]{:S(2)}, u32[]{:S(2)}) %all-to-all-start.3) | async-done | bytes 1835040 | tf_op jit(solution)/shard_map/all_to_all | solution.py:283
  100.4 1.1 %shard_map.135 = bf16[16,3584]{1,0:T(8,128)(2,1)} custom-call(bf16[128,1024]{1,0:T(8,128)(2,1)S(1)} %get-tuple-element.24.gather, bf16[1024,896]{1,0:T(8,128)(2,1)S(1)} %bitcast.18), custom_call_target="tpu_custom_call" | custom-call | flops 200000000 | bytes 2000000 | tf_op jit(solution)/shard_map/pallas_call | solution.py:366
  (14 shorter events, 0.0 us)
Async XLA Ops:
  0.6 13.7 %copy-start.5 = (s32[8]{0:T(128)S(1)}, s32[8]{0:T(128)}, u32[]{:S(2)}) copy-start(s32[8]{0:T(128)} %finished_hbm.3) | copy-start | bytes 100
  0.6 13.7 %copy-start.4 = (s32[8]{0:T(128)S(1)}, s32[8]{0:T(128)}, u32[]{:S(2)}) copy-start(s32[8]{0:T(128)} %length_hbm.3) | copy-start | bytes 100
  0.7 13.7 %copy-start.6 = (s32[1,8,1]{1,2,0:T(1,128)S(1)}, s32[1,8,1]{1,2,0:T(1,128)}, u32[]{:S(2)}) copy-start(s32[1,8,1]{1,2,0:T(1,128)} %param.18) | copy-start | bytes 100
  2.4 10.4 %all-to-all-start = ((bf16[8,8,896]{2,1,0:T(8,128)(2,1)}), bf16[8,8,896]{2,1,0:T(8,128)(2,1)S(1)}, u32[]{:S(2)}, u32[]{:S(2)}) async-start(bf16[8,8,896]{2,1,0:T(8,128)(2,1)} %bitcast.24), calls=%async_computation | async-start | bytes 229376 | tf_op jit(solution)/shard_map/all_to_all | solution.py:307
  14.9 11.9 %copy-start = (bf16[8,128,576]{1,2,0:T(8,128)(2,1)S(1)}, bf16[8,128,576]{1,2,0:T(8,128)(2,1)}, u32[]{:S(2)}) copy-start(bf16[8,128,576]{1,2,0:T(8,128)(2,1)} %param.14) | copy-start | bytes 3538948
  14.9 36.3 %all-to-all-start.1 = ((bf16[128,8,896]{2,1,0:T(8,128)(2,1)}), bf16[128,8,896]{2,1,0:T(8,128)(2,1)S(1)}, u32[]{:S(2)}, u32[]{:S(2)}) async-start(bf16[128,8,896]{2,1,0:T(8,128)(2,1)} %bitcast.21), calls=%async_computation.1 | async-start | bytes 3670016 | tf_op jit(solution)/shard_map/all_to_all | solution.py:283
  26.8 1.6 %copy-start.1 = (bf16[8,64,576]{2,1,0:T(8,128)(2,1)S(1)}, bf16[8,64,576]{2,1,0:T(8,128)(2,1)}, u32[]{:S(2)}) copy-start(bf16[8,64,576]{2,1,0:T(8,128)(2,1)} %reshape.64) | copy-start | bytes 1769476
  26.8 1.6 %copy-start.3 = (bf16[8,576]{1,0:T(8,128)(2,1)S(1)}, bf16[8,576]{1,0:T(8,128)(2,1)}, u32[]{:S(2)}) copy-start(bf16[8,576]{1,0:T(8,128)(2,1)} %param.15) | copy-start | bytes 27652
  51.2 15.5 %all-to-all-start.2 = ((bf16[8,64,512]{2,1,0:T(8,128)(2,1)}), bf16[8,64,512]{2,1,0:T(8,128)(2,1)S(1)}, u32[]{:S(2)}, u32[]{:S(2)}) async-start(bf16[8,64,512]{2,1,0:T(8,128)(2,1)} %broadcast_select_fusion), calls=%async_computation.2 | async-start | bytes 1048576 | tf_op jit(solution)/shard_map/all_to_all | solution.py:342
  66.8 6.6 %copy-start.2 = (bf16[8,64,512]{2,1,0:T(8,128)(2,1)S(1)}, bf16[8,64,512]{2,1,0:T(8,128)(2,1)}, u32[]{:S(2)}) copy-start(bf16[8,64,512]{2,1,0:T(8,128)(2,1)} %get-tuple-element.32) | copy-start | bytes 1572868
  66.8 33.7 %all-to-all-start.3 = ((bf16[128,8,896]{2,1,0:T(8,128)(2,1)}), bf16[128,8,896]{2,1,0:T(8,128)(2,1)S(1)}, u32[]{:S(2)}, u32[]{:S(2)}) async-start(bf16[128,8,896]{2,1,0:T(8,128)(2,1)} %bitcast.20), calls=%async_computation.3 | async-start | bytes 3670016 | tf_op jit(solution)/shard_map/all_to_all | solution.py:283

commit v4 on v3

--- a/solution.py
+++ b/solution.py
@@ -174,53 +174,84 @@
     wait_all(copies)
 
 
+def one_hot(hit):
+    return jnp.where(hit, 1.0, 0.0).astype(BF16)
+
+
 def expert_kernel(recv, w_gate, w_up, w_down, out, *scratch):
-    gates, ups, downs, rows, hidden, partial, results, sent, sems = scratch
-    width = recv.shape[1]
-    blocks = recv.shape[0] // 256
-    half = downs.shape[1]
+    gates, ups, downs, rows, results, sent, sems = scratch
+    lanes, width = recv.shape
+    blocks = lanes // 256
+    total = lanes // PARTS
     gate_copies, up_copies, down_copies = [], [], []
     for q in range(PARTS):
         part = pl.ds(q * width, width)
         gate_copies.append(pltpu.make_async_copy(w_gate.at[0, part, :], gates.at[q], sems.at[0, q]))
         up_copies.append(pltpu.make_async_copy(w_up.at[0, part, :], ups.at[q], sems.at[1, q]))
+        down_copies.append(
+            pltpu.make_async_copy(w_down.at[0, :, part], downs.at[q], sems.at[2, q])
+        )
         start_all([gate_copies[q], up_copies[q]])
-    for n in range(downs.shape[0]):
-        part = pl.ds(n * half, half)
-        down_copies.append(pltpu.make_async_copy(w_down.at[0, part, :], downs.at[n], sems.at[2, n]))
     start_all(down_copies)
 
     one, two = iota((256, 256), 0), iota((256, 256), 1)
-    apart = ((one & 63) * PARTS + (one >> 6)) == two
-    together = ((two & 63) * PARTS + (two >> 6)) == one
-    apart = jnp.where(apart, 1.0, 0.0).astype(BF16)
-    together = jnp.where(together, 1.0, 0.0).astype(BF16)
+    apart = one_hot(((one & 63) * PARTS + (one >> 6)) == two)
+    together = one_hot(((two & 63) * PARTS + (two >> 6)) == one)
+    used = jnp.zeros((8, total), F32)
     for b in range(blocks):
-        got = jnp.dot(apart, recv[b * 256 : (b + 1) * 256, :], preferred_element_type=F32)
-        got = got.astype(BF16)
+        part = recv[b * 256 : (b + 1) * 256, :]
+        nonzero = jnp.where(part.astype(F32) != 0, 1.0, 0.0).astype(BF16)
+        found = lax.dot_general(
+            jnp.ones((8, width), BF16),
+            nonzero,
+            (((1,), (1,)), ((), ())),
+            preferred_element_type=F32,
+        )
+        found = jnp.where(found > 0, 1.0, 0.0).astype(BF16)
+        pool = one_hot((iota((256, total), 0) >> 2) + b * 64 == iota((256, total), 1))
+        used = used + jnp.dot(found, pool, preferred_element_type=F32)
+        got = jnp.dot(apart, part, preferred_element_type=F32).astype(BF16)
         for q in range(PARTS):
             rows[q, b * 64 : (b + 1) * 64, :] = got[q * 64 : (q + 1) * 64, :]
-
-    gate = up = None
-    for q in range(PARTS):
-        gate_copies[q].wait()
-        more = jnp.dot(rows[q], gates[q], preferred_element_type=F32)
-        gate = more if gate is None else gate + more
-        up_copies[q].wait()
-        more = jnp.dot(rows[q], ups[q], preferred_element_type=F32)
-        up = more if up is None else up + more
-    hidden[...] = (gate / (1.0 + jnp.exp(-gate)) * up).astype(BF16)
-    down_copies[0].wait()
-    for q in range(PARTS):
-        part = slice(q * width, (q + 1) * width)
-        partial[q] = jnp.dot(hidden[:, :half], downs[0, :, part], preferred_element_type=F32)
-    down_copies[1].wait()
-    for q in range(PARTS):
-        part = slice(q * width, (q + 1) * width)
-        result = jnp.dot(hidden[:, half:], downs[1, :, part], preferred_element_type=F32)
-        result = (partial[q] + result).astype(BF16)
-        for b in range(blocks):
-            results[b, q * 64 : (q + 1) * 64, :] = result[b * 64 : (b + 1) * 64, :]
+    used = jnp.where(used > 0, 1.0, 0.0)
+    before = one_hot(iota((total, total), 0) < iota((total, total), 1))
+    place = jnp.dot(used.astype(BF16), before, preferred_element_type=F32)
+    count = jnp.sum(used[:1, :]).astype(jnp.int32)
+
+    def body(size):
+        pick = (iota((size, total), 0).astype(F32) == place[:1, :]) & (used[:1, :] > 0)
+        pick = jnp.where(pick, 1.0, 0.0)
+        spread = jnp.transpose(pick).astype(BF16)
+        pick = pick.astype(BF16)
+        packed = [
+            jnp.dot(pick, rows[q], preferred_element_type=F32).astype(BF16) for q in range(PARTS)
+        ]
+        gate = up = None
+        for q in range(PARTS):
+            gate_copies[q].wait()
+            more = jnp.dot(packed[q], gates[q], preferred_element_type=F32)
+            gate = more if gate is None else gate + more
+            up_copies[q].wait()
+            more = jnp.dot(packed[q], ups[q], preferred_element_type=F32)
+            up = more if up is None else up + more
+        hidden = (gate / (1.0 + jnp.exp(-gate)) * up).astype(BF16)
+        for q in range(PARTS):
+            down_copies[q].wait()
+            result = jnp.dot(hidden, downs[q], preferred_element_type=F32).astype(BF16)
+            result = jnp.dot(spread, result, preferred_element_type=F32).astype(BF16)
+            for b in range(blocks):
+                results[b, q * 64 : (q + 1) * 64, :] = result[b * 64 : (b + 1) * 64, :]
+
+    small = 160
+
+    @pl.when(count <= small)
+    def _():
+        body(small)
+
+    @pl.when(count > small)
+    def _():
+        body(total)
+
     copies = []
     for b in range(blocks):
         part = pl.ds(b * 256, 256)
@@ -328,12 +359,11 @@
         [pltpu.VMEM((lanes, width), BF16), pltpu.SemaphoreType.DMA((lanes // 256,))],
         in_hbm=True,
     )(scatter, flat, arrived)
-    held = (queries, latent_cache, new_latent, lengths, finished, plan, outgoing)
-    held = lax.optimization_barrier(held)
-    queries, latent_cache, new_latent, lengths, finished, plan, outgoing = held
+    own_length = jnp.where(finished == 0, lengths, 0)
+    held = lax.optimization_barrier((queries, latent_cache, new_latent, plan, outgoing))
+    queries, latent_cache, new_latent, plan, outgoing = held
     incoming = exchange(outgoing)
 
-    own_length = jnp.where(finished == 0, lengths, 0)
     attended = attend(queries, latent_cache, new_latent, own_length)
     sending = plan >= 0
     moved_out = jnp.any((plan[:, None] == jnp.arange(count)[None, :]), axis=0)
@@ -351,10 +381,8 @@
         [
             pltpu.VMEM((PARTS, width, hidden), BF16),
             pltpu.VMEM((PARTS, width, hidden), BF16),
-            pltpu.VMEM((2, hidden // 2, model), BF16),
+            pltpu.VMEM((PARTS, hidden, width), BF16),
             pltpu.VMEM((PARTS, devices * CAP, width), BF16),
-            pltpu.VMEM((devices * CAP, hidden), BF16),
-            pltpu.VMEM((PARTS, devices * CAP, width), F32),
             pltpu.VMEM((lanes // 256, 256, width), BF16),
             pltpu.VMEM((lanes, width), BF16),
             pltpu.SemaphoreType.DMA((3, 4)),

time: 102 us -> 101 us (level)
  waiting for transfers between devices: 45.8 us -> 43.3 us
  matrix products: 4.36 us -> 5.39 us
    all_to_all x1, waiting for transfers between devices: 4.44 us -> 3.16 us  [on_device(): lax.all_to_all(send.reshape(replicas, 8, width), 'replica', split_axis=0,...]
    all_to_all x2, waiting for transfers between devices: 41.3 us -> 40.2 us  [exchange(): lax.all_to_all(values, BOTH, split_axis=0, concat_axis=0, tiled=True)]
    dot_general x1, matrix products: 0.3 us -> 1.38 us  [attend(): jnp.einsum('nhl,nl->nh', per_head, own_latent, preferred_element_type=F32)]
  transfers between devices with their start and end apart: 4 -> 4, of which waited for: 3 -> 3; matrix products, arithmetic and copies ran while one was open for 13% -> 15% of each run, Pallas kernels for 13% -> 13%
where the time goes in v4:
time: 101 us
  waiting for transfers between devices  43.3 us (43%)
  starting transfers between devices  23.7 us (23%)
  Pallas kernels  17.7 us (18%)
  local copies, waits for them, and re-layouts  6.38 us (6%)
  matrix products  5.39 us (5%)
  other arithmetic  3.37 us (3%)
    all_to_all x2, waiting for transfers between devices, exchange(): lax.all_to_all(values, BOTH, split_axis=0, concat_axis=0, tiled=True)  40.2 us
    all_to_all x2, starting transfers between devices, exchange(): lax.all_to_all(values, BOTH, split_axis=0, concat_axis=0, tiled=True)  15.8 us
    pallas_call x1, Pallas kernels, on_device(): call(expert_kernel, [(lanes, width)], [VMEM] + [HBM] * 3, (6 * devices *...  11.8 us
    all_to_all x1, starting transfers between devices, on_device(): lax.all_to_all(send.reshape(replicas, 8, width), 'replica', split_axis=0,...  4.4 us
    all_to_all x1, starting transfers between devices, on_device(): lax.all_to_all(leave, 'replica', split_axis=0, concat_axis=0, tiled=True)  3.49 us
    all_to_all x1, waiting for transfers between devices, on_device(): lax.all_to_all(send.reshape(replicas, 8, width), 'replica', split_axis=0,...  3.16 us
    reshape x1, local copies, waits for them, and re-layouts, attend(): per_head = query_rows.reshape(row_count, HEADS, LAT)  2.78 us
    dot_general x1, matrix products, attend(): jnp.einsum('nht,ntv->nhv', weights.astype(BF16), latent_rows[:, :, :VDIM]...  2.46 us
  transfers between devices with their start and end apart: 4, of which 3 were waited for; matrix products, arithmetic and copies ran while one was open for 15% of the time, Pallas kernels for 13%

profile of v4, /device:TPU:0, one launch (start us, length us, event | category | flops | bytes accessed | tf_op | source)
XLA Modules:
  0.0 100.7 jit_solution(16506540926987814411)
XLA Ops:
  0.6 1.7 %shard_map.132 = bf16[64,896]{1,0:T(8,128)(2,1)} custom-call(s32[8]{0:T(128)} %bitcast.30, s32[8]{0:T(128)} %length_hbm.3, s32[8]{0:T(128)} %finished_hbm.3, bf16[8,3584]{1,0:T(8,128)(2,1)} %tokens_hbm.3), custom_call_target="tpu_custom_call" | custom-call | flops 1000000 | bytes 100000 | tf_op jit(solution)/shard_map/pallas_call | solution.py:325
  2.3 4.4 %all-to-all-start = ((bf16[8,8,896]{2,1,0:T(8,128)(2,1)}), bf16[8,8,896]{2,1,0:T(8,128)(2,1)S(1)}, u32[]{:S(2)}, u32[]{:S(2)}) async-start(bf16[8,8,896]{2,1,0:T(8,128)(2,1)} %bitcast.24), calls=%async_computation | async-start | bytes 229376 | tf_op jit(solution)/shard_map/all_to_all | solution.py:338
  6.7 1.2 %compare_convert_fusion = (f32[8]{0:T(128)}, s32[8]{0:T(128)S(1)}) fusion(s32[8]{0:T(128)} %length_hbm.3, s32[8]{0:T(128)} %finished_hbm.3), kind=kLoop, calls=%fused_computation.24 | loop fusion | flops 32 | bytes 128 | tf_op jit(solution)/shard_map/convert_element_type | solution.py:51
  7.9 0.1 iota_compare_fusion
  8.0 1.5 %shard_map.131 = (bf16[1024,128]{1,0:T(8,128)(2,1)S(1)}, bf16[128,1024]{1,0:T(8,128)(2,1)S(1)}, bf16[32,896]{1,0:T(8,128)(2,1)S(1)}) custom-call(s32[8]{0:T(128)} %bitcast.31, s32[8]{0:T(128)} %length_hbm.3, s32[8]{0:T(128)} %finished_hbm.3, s32[8,16]{1,0:T(8,128)} %bitcast.28, f32[8,16]{1,0:T(8,128)} %bitcast.29, bf16[8,3584]{1,0:T(8,128)(2,1)} %tokens_hbm.3), custom_call_target="tpu_custom_call" | custom-call | flops 10000000 | bytes 1000000 | tf_op jit(solution)/shard_map/pallas_call | solution.py:341
  9.5 3.2 %all-to-all-done = bf16[8,8,896]{2,1,0:T(8,128)(2,1)S(1)} async-done(((bf16[8,8,896]{2,1,0:T(8,128)(2,1)}), bf16[8,8,896]{2,1,0:T(8,128)(2,1)S(1)}, u32[]{:S(2)}, u32[]{:S(2)}) %all-to-all-start) | async-done | bytes 114720 | tf_op jit(solution)/shard_map/all_to_all | solution.py:338
  12.7 1.5 %shard_map.133 = bf16[1024,896]{1,0:T(8,128)(2,1)} custom-call(bf16[1024,128]{1,0:T(8,128)(2,1)S(1)} %get-tuple-element.12.scatter, bf16[32,896]{1,0:T(8,128)(2,1)S(1)} %get-tuple-element.13.tokens, bf16[64,896]{1,0:T(8,128)(2,1)S(1)} %bitcast.19), custom_call_target="tpu_custom_call" | custom-call | flops 200000000 | bytes 2000000 | tf_op jit(solution)/shard_map/pallas_call | solution.py:354
  14.2 0.0 copy-start.2
  14.2 9.2 %all-to-all-start.1 = ((bf16[128,8,896]{2,1,0:T(8,128)(2,1)}), bf16[128,8,896]{2,1,0:T(8,128)(2,1)S(1)}, u32[]{:S(2)}, u32[]{:S(2)}) async-start(bf16[128,8,896]{2,1,0:T(8,128)(2,1)} %bitcast.21), calls=%async_computation.1 | async-start | bytes 3670016 | tf_op jit(solution)/shard_map/all_to_all | solution.py:314
  23.5 0.0 copy-start
  23.5 2.8 %reshape.64 = bf16[8,64,576]{2,1,0:T(8,128)(2,1)} reshape(bf16[8,36864]{1,0:T(8,128)(2,1)} %param.13) | data formatting | bytes 1179648 | tf_op jit(solution)/shard_map/reshape | solution.py:31
  26.3 1.4 %fusion.9 = f32[8,1,64]{2,1,0:T(1,128)S(1)} fusion(bf16[8,64,576]{2,1,0:T(8,128)(2,1)} %reshape.64, bf16[8,576,1]{1,0,2:T(8,128)(2,1)S(1)} %bitcast.27), kind=kOutput, calls=%fused_computation.15 | convolution fusion | flops 589824 | bytes 601088 | tf_op jit(solution)/shard_map/nhl,nl->nh/dot_general | solution.py:35
  27.6 0.0 copy-done
  27.6 1.5 %fusion.14 = (f32[8,64]{1,0:T(8,128)S(1)}, f32[8,64,128]{2,1,0:T(8,128)S(1)}) fusion(bf16[8,64,576]{2,1,0:T(8,128)(2,1)} %reshape.64, bf16[8,128,576]{1,2,0:T(8,128)(2,1)S(1)} %copy-done, pred[8,128]{1,0:T(8,128)(4,1)S(1)} %iota_compare_fusion), kind=kOutput, calls=%fused_computation.30 | convolution fusion | flops 75693568 | bytes 2034688 | tf_op jit(solution)/shard_map/nhl,ntl->nht/dot_general | solution.py:33
  29.2 0.0 copy-start.3
  29.2 1.4 %copy.15 = bf16[8,128,576]{2,1,0:T(8,128)(2,1)} copy(bf16[8,128,576]{1,2,0:T(8,128)(2,1)S(1)} %copy-done) | data formatting | bytes 2359296 | tf_op jit(solution)/shard_map/optimization_barrier | solution.py:363
  30.7 0.3 fusion.5
  31.0 0.1 fusion.11
  31.1 0.7 slice_convert_fusion
  31.8 2.5 %broadcast_select_fusion.1 = (bf16[8,64,512]{2,1,0:T(8,128)(2,1)}, bf16[8,64,512]{2,1,0:T(8,128)(2,1)S(1)}) fusion(pred[8]{0:T(512)(128)(4,1)S(1)} %fusion.11, f32[8]{0:T(128)} %get-tuple-element.22, f32[8,64]{1,0:T(8,128)S(1)} %get-tuple-element.25, f32[8,512]{1,0:T(8,128)S(1)} %slice_convert_fusion, f32[8,64]{1,0:T(8,128)S(1)} %convert_element_type.21, ...), kind=kOutput, calls=%fused_computation.10 | convolution fusion | flops 68812800 | bytes 2382344 | tf_op jit(solution)/shard_map/nht,ntv->nhv/dot_general | solution.py:43
  34.2 0.6 gather_fusion
  34.8 0.9 broadcast_select_fusion
  35.8 14.8 %all-to-all-done.1 = bf16[128,8,896]{2,1,0:T(8,128)(2,1)S(1)} async-done(((bf16[128,8,896]{2,1,0:T(8,128)(2,1)}), bf16[128,8,896]{2,1,0:T(8,128)(2,1)S(1)}, u32[]{:S(2)}, u32[]{:S(2)}) %all-to-all-start.1) | async-done | bytes 1835040 | tf_op jit(solution)/shard_map/all_to_all | solution.py:314
  50.5 3.5 %all-to-all-start.2 = ((bf16[8,64,512]{2,1,0:T(8,128)(2,1)}), bf16[8,64,512]{2,1,0:T(8,128)(2,1)S(1)}, u32[]{:S(2)}, u32[]{:S(2)}) async-start(bf16[8,64,512]{2,1,0:T(8,128)(2,1)} %broadcast_select_fusion), calls=%async_computation.2 | async-start | bytes 1048576 | tf_op jit(solution)/shard_map/all_to_all | solution.py:372
  54.0 11.8 %shard_map.134 = bf16[1024,896]{1,0:T(8,128)(2,1)} custom-call(bf16[1024,896]{1,0:T(8,128)(2,1)S(1)} %bitcast.17, bf16[1,3584,1024]{2,1,0:T(8,128)(2,1)} %w_gate.1, bf16[1,3584,1024]{2,1,0:T(8,128)(2,1)} %w_up.1, bf16[1,1024,3584]{2,1,0:T(8,128)(2,1)} %w_down.1), custom_call_target="tpu_custom_call" | custom-call | flops 5637144576 | bytes 22020096 | tf_op jit(solution)/shard_map/pallas_call | solution.py:376
  65.9 0.0 all-to-all-done.2
  65.9 0.0 copy-start.1
  65.9 6.6 %all-to-all-start.3 = ((bf16[128,8,896]{2,1,0:T(8,128)(2,1)}), bf16[128,8,896]{2,1,0:T(8,128)(2,1)S(1)}, u32[]{:S(2)}, u32[]{:S(2)}) async-start(bf16[128,8,896]{2,1,0:T(8,128)(2,1)} %bitcast.20), calls=%async_computation.3 | async-start | bytes 3670016 | tf_op jit(solution)/shard_map/all_to_all | solution.py:314
  72.5 0.1 pad_maximum_fusion
  72.6 1.5 %copy.18 = bf16[2,8,64,512]{3,1,2,0:T(8,128)(2,1)} copy(bf16[2,8,64,512]{3,2,1,0:T(8,128)(2,1)S(1)} %bitcast.22) | data formatting | bytes 2097152
  74.1 25.4 %all-to-all-done.3 = bf16[128,8,896]{2,1,0:T(8,128)(2,1)S(1)} async-done(((bf16[128,8,896]{2,1,0:T(8,128)(2,1)}), bf16[128,8,896]{2,1,0:T(8,128)(2,1)S(1)}, u32[]{:S(2)}, u32[]{:S(2)}) %all-to-all-start.3) | async-done | bytes 1835040 | tf_op jit(solution)/shard_map/all_to_all | solution.py:314
  99.6 1.1 %shard_map.135 = bf16[16,3584]{1,0:T(8,128)(2,1)} custom-call(bf16[128,1024]{1,0:T(8,128)(2,1)S(1)} %get-tuple-element.20.gather, bf16[1024,896]{1,0:T(8,128)(2,1)S(1)} %bitcast.18), custom_call_target="tpu_custom_call" | custom-call | flops 200000000 | bytes 2000000 | tf_op jit(solution)/shard_map/pallas_call | solution.py:394
  (9 shorter events, 0.0 us)
Async XLA Ops:
  2.3 10.4 %all-to-all-start = ((bf16[8,8,896]{2,1,0:T(8,128)(2,1)}), bf16[8,8,896]{2,1,0:T(8,128)(2,1)S(1)}, u32[]{:S(2)}, u32[]{:S(2)}) async-start(bf16[8,8,896]{2,1,0:T(8,128)(2,1)} %bitcast.24), calls=%async_computation | async-start | bytes 229376 | tf_op jit(solution)/shard_map/all_to_all | solution.py:338
  14.2 12.0 %copy-start.2 = (bf16[8,576]{1,0:T(8,128)(2,1)S(1)}, bf16[8,576]{1,0:T(8,128)(2,1)}, u32[]{:S(2)}) copy-start(bf16[8,576]{1,0:T(8,128)(2,1)} %param.15) | copy-start | bytes 27652
  14.2 36.3 %all-to-all-start.1 = ((bf16[128,8,896]{2,1,0:T(8,128)(2,1)}), bf16[128,8,896]{2,1,0:T(8,128)(2,1)S(1)}, u32[]{:S(2)}, u32[]{:S(2)}) async-start(bf16[128,8,896]{2,1,0:T(8,128)(2,1)} %bitcast.21), calls=%async_computation.1 | async-start | bytes 3670016 | tf_op jit(solution)/shard_map/all_to_all | solution.py:314
  23.5 4.2 %copy-start = (bf16[8,128,576]{1,2,0:T(8,128)(2,1)S(1)}, bf16[8,128,576]{1,2,0:T(8,128)(2,1)}, u32[]{:S(2)}) copy-start(bf16[8,128,576]{1,2,0:T(8,128)(2,1)} %param.14) | copy-start | bytes 3538948
  29.2 1.8 %copy-start.3 = (s32[1,8,1]{1,2,0:T(1,128)S(1)}, s32[1,8,1]{1,2,0:T(1,128)}, u32[]{:S(2)}) copy-start(s32[1,8,1]{1,2,0:T(1,128)} %param.18) | copy-start | bytes 100
  50.5 15.4 %all-to-all-start.2 = ((bf16[8,64,512]{2,1,0:T(8,128)(2,1)}), bf16[8,64,512]{2,1,0:T(8,128)(2,1)S(1)}, u32[]{:S(2)}, u32[]{:S(2)}) async-start(bf16[8,64,512]{2,1,0:T(8,128)(2,1)} %broadcast_select_fusion), calls=%async_computation.2 | async-start | bytes 1048576 | tf_op jit(solution)/shard_map/all_to_all | solution.py:372
  65.9 6.6 %copy-start.1 = (bf16[8,64,512]{2,1,0:T(8,128)(2,1)S(1)}, bf16[8,64,512]{2,1,0:T(8,128)(2,1)}, u32[]{:S(2)}) copy-start(bf16[8,64,512]{2,1,0:T(8,128)(2,1)} %get-tuple-element.28) | copy-start | bytes 1572868
  65.9 33.6 %all-to-all-start.3 = ((bf16[128,8,896]{2,1,0:T(8,128)(2,1)}), bf16[128,8,896]{2,1,0:T(8,128)(2,1)S(1)}, u32[]{:S(2)}, u32[]{:S(2)}) async-start(bf16[128,8,896]{2,1,0:T(8,128)(2,1)} %bitcast.20), calls=%async_computation.3 | async-start | bytes 3670016 | tf_op jit(solution)/shard_map/all_to_all | solution.py:314

commit v5 on v4

--- a/solution.py
+++ b/solution.py
@@ -178,6 +178,20 @@
     return jnp.where(hit, 1.0, 0.0).astype(BF16)
 
 
+def halves(source, target, sems):
+    half = source.shape[0] // 2
+    parts = [pl.ds(n * half, half) for n in range(2)]
+    return [
+        pltpu.make_async_copy(source.at[part, :], target.at[part, :], sems.at[n])
+        for n, part in enumerate(parts)
+    ]
+
+
+def start_halves(copies):
+    for n, copy in enumerate(copies):
+        copy.start(priority=n % 2)
+
+
 def expert_kernel(recv, w_gate, w_up, w_down, out, *scratch):
     gates, ups, downs, rows, results, sent, sems = scratch
     lanes, width = recv.shape
@@ -185,14 +199,14 @@
     total = lanes // PARTS
     gate_copies, up_copies, down_copies = [], [], []
     for q in range(PARTS):
-        part = pl.ds(q * width, width)
-        gate_copies.append(pltpu.make_async_copy(w_gate.at[0, part, :], gates.at[q], sems.at[0, q]))
-        up_copies.append(pltpu.make_async_copy(w_up.at[0, part, :], ups.at[q], sems.at[1, q]))
-        down_copies.append(
-            pltpu.make_async_copy(w_down.at[0, :, part], downs.at[q], sems.at[2, q])
-        )
-        start_all([gate_copies[q], up_copies[q]])
-    start_all(down_copies)
+        part = slice(q * width, (q + 1) * width)
+        gate_copies.append(halves(w_gate.at[0, part, :], gates.at[q], sems.at[0, q]))
+        up_copies.append(halves(w_up.at[0, part, :], ups.at[q], sems.at[1, q]))
+        down_copies.append(halves(w_down.at[0, :, part], downs.at[q], sems.at[2, q]))
+    for q in range(PARTS):
+        start_halves(gate_copies[q] + up_copies[q])
+    for q in range(PARTS):
+        start_halves(down_copies[q])
 
     one, two = iota((256, 256), 0), iota((256, 256), 1)
     apart = one_hot(((one & 63) * PARTS + (one >> 6)) == two)
@@ -228,15 +242,15 @@
         ]
         gate = up = None
         for q in range(PARTS):
-            gate_copies[q].wait()
+            wait_all(gate_copies[q])
             more = jnp.dot(packed[q], gates[q], preferred_element_type=F32)
             gate = more if gate is None else gate + more
-            up_copies[q].wait()
+            wait_all(up_copies[q])
             more = jnp.dot(packed[q], ups[q], preferred_element_type=F32)
             up = more if up is None else up + more
         hidden = (gate / (1.0 + jnp.exp(-gate)) * up).astype(BF16)
         for q in range(PARTS):
-            down_copies[q].wait()
+            wait_all(down_copies[q])
             result = jnp.dot(hidden, downs[q], preferred_element_type=F32).astype(BF16)
             result = jnp.dot(spread, result, preferred_element_type=F32).astype(BF16)
             for b in range(blocks):
@@ -257,7 +271,7 @@
         part = pl.ds(b * 256, 256)
         value = jnp.dot(together, results[b], preferred_element_type=F32).astype(BF16)
         sent[part, :] = value
-        copies += start_all([pltpu.make_async_copy(sent.at[part], out.at[part], sems.at[0, b])])
+        copies += start_all([pltpu.make_async_copy(sent.at[part], out.at[part], sems.at[0, b, 0])])
     wait_all(copies)
 
 
@@ -385,7 +399,7 @@
             pltpu.VMEM((PARTS, devices * CAP, width), BF16),
             pltpu.VMEM((lanes // 256, 256, width), BF16),
             pltpu.VMEM((lanes, width), BF16),
-            pltpu.SemaphoreType.DMA((3, 4)),
+            pltpu.SemaphoreType.DMA((3, PARTS, 2)),
         ],
         46,
         True,

time: 101 us -> 104 us (1.030)
  Pallas kernels: 17.7 us -> 20.2 us
    pallas_call x1, Pallas kernels: 11.8 us -> 14.3 us  [on_device(): call(expert_kernel, [(lanes, width)], [VMEM] + [HBM] * 3, (6 * devices *...]
  transfers between devices with their start and end apart: 4 -> 4, of which waited for: 3 -> 3; matrix products, arithmetic and copies ran while one was open for 15% -> 15% of each run, Pallas kernels for 13% -> 15%
where the time goes in v5:
time: 104 us; the launch traced here: 103 us
  waiting for transfers between devices  43.3 us (42%)
  starting transfers between devices  23.7 us (23%)
  Pallas kernels  20.2 us (19%)
  local copies, waits for them, and re-layouts  6.38 us (6%)
  matrix products  5.39 us (5%)
  other arithmetic  3.37 us (3%)
    all_to_all x2, waiting for transfers between devices, exchange(): lax.all_to_all(values, BOTH, split_axis=0, concat_axis=0, tiled=True)  40.2 us
    all_to_all x2, starting transfers between devices, exchange(): lax.all_to_all(values, BOTH, split_axis=0, concat_axis=0, tiled=True)  15.8 us
    pallas_call x1, Pallas kernels, on_device(): call(expert_kernel, [(lanes, width)], [VMEM] + [HBM] * 3, (6 * devices *...  14.3 us
    all_to_all x1, starting transfers between devices, on_device(): lax.all_to_all(send.reshape(replicas, 8, width), 'replica', split_axis=0,...  4.4 us
    all_to_all x1, starting transfers between devices, on_device(): lax.all_to_all(leave, 'replica', split_axis=0, concat_axis=0, tiled=True)  3.49 us
    all_to_all x1, waiting for transfers between devices, on_device(): lax.all_to_all(send.reshape(replicas, 8, width), 'replica', split_axis=0,...  3.16 us
    reshape x1, local copies, waits for them, and re-layouts, attend(): per_head = query_rows.reshape(row_count, HEADS, LAT)  2.78 us
    dot_general x1, matrix products, attend(): jnp.einsum('nht,ntv->nhv', weights.astype(BF16), latent_rows[:, :, :VDIM]...  2.46 us
  transfers between devices with their start and end apart: 4, of which 3 were waited for; matrix products, arithmetic and copies ran while one was open for 15% of the time, Pallas kernels for 15%

profile of v5, /device:TPU:0, one launch (start us, length us, event | category | flops | bytes accessed | tf_op | source)
XLA Modules:
  0.0 103.1 jit_solution(908562195211409874)
XLA Ops:
  0.6 1.7 %shard_map.132 = bf16[64,896]{1,0:T(8,128)(2,1)} custom-call(s32[8]{0:T(128)} %bitcast.30, s32[8]{0:T(128)} %length_hbm.3, s32[8]{0:T(128)} %finished_hbm.3, bf16[8,3584]{1,0:T(8,128)(2,1)} %tokens_hbm.3), custom_call_target="tpu_custom_call" | custom-call | flops 1000000 | bytes 100000 | tf_op jit(solution)/shard_map/pallas_call | solution.py:339
  2.3 4.4 %all-to-all-start = ((bf16[8,8,896]{2,1,0:T(8,128)(2,1)}), bf16[8,8,896]{2,1,0:T(8,128)(2,1)S(1)}, u32[]{:S(2)}, u32[]{:S(2)}) async-start(bf16[8,8,896]{2,1,0:T(8,128)(2,1)} %bitcast.24), calls=%async_computation | async-start | bytes 229376 | tf_op jit(solution)/shard_map/all_to_all | solution.py:352
  6.7 1.2 %compare_convert_fusion = (f32[8]{0:T(128)}, s32[8]{0:T(128)S(1)}) fusion(s32[8]{0:T(128)} %length_hbm.3, s32[8]{0:T(128)} %finished_hbm.3), kind=kLoop, calls=%fused_computation.24 | loop fusion | flops 32 | bytes 128 | tf_op jit(solution)/shard_map/convert_element_type | solution.py:51
  7.9 0.1 iota_compare_fusion
  8.0 1.5 %shard_map.131 = (bf16[1024,128]{1,0:T(8,128)(2,1)S(1)}, bf16[128,1024]{1,0:T(8,128)(2,1)S(1)}, bf16[32,896]{1,0:T(8,128)(2,1)S(1)}) custom-call(s32[8]{0:T(128)} %bitcast.31, s32[8]{0:T(128)} %length_hbm.3, s32[8]{0:T(128)} %finished_hbm.3, s32[8,16]{1,0:T(8,128)} %bitcast.28, f32[8,16]{1,0:T(8,128)} %bitcast.29, bf16[8,3584]{1,0:T(8,128)(2,1)} %tokens_hbm.3), custom_call_target="tpu_custom_call" | custom-call | flops 10000000 | bytes 1000000 | tf_op jit(solution)/shard_map/pallas_call | solution.py:355
  9.5 3.2 %all-to-all-done = bf16[8,8,896]{2,1,0:T(8,128)(2,1)S(1)} async-done(((bf16[8,8,896]{2,1,0:T(8,128)(2,1)}), bf16[8,8,896]{2,1,0:T(8,128)(2,1)S(1)}, u32[]{:S(2)}, u32[]{:S(2)}) %all-to-all-start) | async-done | bytes 114720 | tf_op jit(solution)/shard_map/all_to_all | solution.py:352
  12.7 1.5 %shard_map.133 = bf16[1024,896]{1,0:T(8,128)(2,1)} custom-call(bf16[1024,128]{1,0:T(8,128)(2,1)S(1)} %get-tuple-element.12.scatter, bf16[32,896]{1,0:T(8,128)(2,1)S(1)} %get-tuple-element.13.tokens, bf16[64,896]{1,0:T(8,128)(2,1)S(1)} %bitcast.19), custom_call_target="tpu_custom_call" | custom-call | flops 200000000 | bytes 2000000 | tf_op jit(solution)/shard_map/pallas_call | solution.py:368
  14.2 0.0 copy-start.2
  14.2 9.2 %all-to-all-start.1 = ((bf16[128,8,896]{2,1,0:T(8,128)(2,1)}), bf16[128,8,896]{2,1,0:T(8,128)(2,1)S(1)}, u32[]{:S(2)}, u32[]{:S(2)}) async-start(bf16[128,8,896]{2,1,0:T(8,128)(2,1)} %bitcast.21), calls=%async_computation.1 | async-start | bytes 3670016 | tf_op jit(solution)/shard_map/all_to_all | solution.py:328
  23.5 0.0 copy-start
  23.5 2.8 %reshape.64 = bf16[8,64,576]{2,1,0:T(8,128)(2,1)} reshape(bf16[8,36864]{1,0:T(8,128)(2,1)} %param.13) | data formatting | bytes 1179648 | tf_op jit(solution)/shard_map/reshape | solution.py:31
  26.3 1.4 %fusion.9 = f32[8,1,64]{2,1,0:T(1,128)S(1)} fusion(bf16[8,64,576]{2,1,0:T(8,128)(2,1)} %reshape.64, bf16[8,576,1]{1,0,2:T(8,128)(2,1)S(1)} %bitcast.27), kind=kOutput, calls=%fused_computation.15 | convolution fusion | flops 589824 | bytes 601088 | tf_op jit(solution)/shard_map/nhl,nl->nh/dot_general | solution.py:35
  27.6 0.0 copy-done
  27.6 1.5 %fusion.14 = (f32[8,64]{1,0:T(8,128)S(1)}, f32[8,64,128]{2,1,0:T(8,128)S(1)}) fusion(bf16[8,64,576]{2,1,0:T(8,128)(2,1)} %reshape.64, bf16[8,128,576]{1,2,0:T(8,128)(2,1)S(1)} %copy-done, pred[8,128]{1,0:T(8,128)(4,1)S(1)} %iota_compare_fusion), kind=kOutput, calls=%fused_computation.30 | convolution fusion | flops 75693568 | bytes 2034688 | tf_op jit(solution)/shard_map/nhl,ntl->nht/dot_general | solution.py:33
  29.2 0.0 copy-start.3
  29.2 1.4 %copy.15 = bf16[8,128,576]{2,1,0:T(8,128)(2,1)} copy(bf16[8,128,576]{1,2,0:T(8,128)(2,1)S(1)} %copy-done) | data formatting | bytes 2359296 | tf_op jit(solution)/shard_map/optimization_barrier | solution.py:377
  30.7 0.3 fusion.5
  31.0 0.1 fusion.11
  31.1 0.7 slice_convert_fusion
  31.8 2.5 %broadcast_select_fusion.1 = (bf16[8,64,512]{2,1,0:T(8,128)(2,1)}, bf16[8,64,512]{2,1,0:T(8,128)(2,1)S(1)}) fusion(pred[8]{0:T(512)(128)(4,1)S(1)} %fusion.11, f32[8]{0:T(128)} %get-tuple-element.22, f32[8,64]{1,0:T(8,128)S(1)} %get-tuple-element.25, f32[8,512]{1,0:T(8,128)S(1)} %slice_convert_fusion, f32[8,64]{1,0:T(8,128)S(1)} %convert_element_type.21, ...), kind=kOutput, calls=%fused_computation.10 | convolution fusion | flops 68812800 | bytes 2382344 | tf_op jit(solution)/shard_map/nht,ntv->nhv/dot_general | solution.py:43
  34.2 0.6 gather_fusion
  34.8 0.9 broadcast_select_fusion
  35.8 14.8 %all-to-all-done.1 = bf16[128,8,896]{2,1,0:T(8,128)(2,1)S(1)} async-done(((bf16[128,8,896]{2,1,0:T(8,128)(2,1)}), bf16[128,8,896]{2,1,0:T(8,128)(2,1)S(1)}, u32[]{:S(2)}, u32[]{:S(2)}) %all-to-all-start.1) | async-done | bytes 1835040 | tf_op jit(solution)/shard_map/all_to_all | solution.py:328
  50.5 3.5 %all-to-all-start.2 = ((bf16[8,64,512]{2,1,0:T(8,128)(2,1)}), bf16[8,64,512]{2,1,0:T(8,128)(2,1)S(1)}, u32[]{:S(2)}, u32[]{:S(2)}) async-start(bf16[8,64,512]{2,1,0:T(8,128)(2,1)} %broadcast_select_fusion), calls=%async_computation.2 | async-start | bytes 1048576 | tf_op jit(solution)/shard_map/all_to_all | solution.py:386
  54.0 14.3 %shard_map.134 = bf16[1024,896]{1,0:T(8,128)(2,1)} custom-call(bf16[1024,896]{1,0:T(8,128)(2,1)S(1)} %bitcast.17, bf16[1,3584,1024]{2,1,0:T(8,128)(2,1)} %w_gate.1, bf16[1,3584,1024]{2,1,0:T(8,128)(2,1)} %w_up.1, bf16[1,1024,3584]{2,1,0:T(8,128)(2,1)} %w_down.1), custom_call_target="tpu_custom_call" | custom-call | flops 5637144576 | bytes 22020096 | tf_op jit(solution)/shard_map/pallas_call | solution.py:390
  68.4 0.0 all-to-all-done.2
  68.4 0.0 copy-start.1
  68.4 6.6 %all-to-all-start.3 = ((bf16[128,8,896]{2,1,0:T(8,128)(2,1)}), bf16[128,8,896]{2,1,0:T(8,128)(2,1)S(1)}, u32[]{:S(2)}, u32[]{:S(2)}) async-start(bf16[128,8,896]{2,1,0:T(8,128)(2,1)} %bitcast.20), calls=%async_computation.3 | async-start | bytes 3670016 | tf_op jit(solution)/shard_map/all_to_all | solution.py:328
  75.0 0.1 pad_maximum_fusion
  75.1 1.5 %copy.18 = bf16[2,8,64,512]{3,1,2,0:T(8,128)(2,1)} copy(bf16[2,8,64,512]{3,2,1,0:T(8,128)(2,1)S(1)} %bitcast.22) | data formatting | bytes 2097152
  76.6 25.4 %all-to-all-done.3 = bf16[128,8,896]{2,1,0:T(8,128)(2,1)S(1)} async-done(((bf16[128,8,896]{2,1,0:T(8,128)(2,1)}), bf16[128,8,896]{2,1,0:T(8,128)(2,1)S(1)}, u32[]{:S(2)}, u32[]{:S(2)}) %all-to-all-start.3) | async-done | bytes 1835040 | tf_op jit(solution)/shard_map/all_to_all | solution.py:328
  102.0 1.1 %shard_map.135 = bf16[16,3584]{1,0:T(8,128)(2,1)} custom-call(bf16[128,1024]{1,0:T(8,128)(2,1)S(1)} %get-tuple-element.20.gather, bf16[1024,896]{1,0:T(8,128)(2,1)S(1)} %bitcast.18), custom_call_target="tpu_custom_call" | custom-call | flops 200000000 | bytes 2000000 | tf_op jit(solution)/shard_map/pallas_call | solution.py:408
  (9 shorter events, 0.0 us)
Async XLA Ops:
  2.3 10.4 %all-to-all-start = ((bf16[8,8,896]{2,1,0:T(8,128)(2,1)}), bf16[8,8,896]{2,1,0:T(8,128)(2,1)S(1)}, u32[]{:S(2)}, u32[]{:S(2)}) async-start(bf16[8,8,896]{2,1,0:T(8,128)(2,1)} %bitcast.24), calls=%async_computation | async-start | bytes 229376 | tf_op jit(solution)/shard_map/all_to_all | solution.py:352
  14.2 12.0 %copy-start.2 = (bf16[8,576]{1,0:T(8,128)(2,1)S(1)}, bf16[8,576]{1,0:T(8,128)(2,1)}, u32[]{:S(2)}) copy-start(bf16[8,576]{1,0:T(8,128)(2,1)} %param.15) | copy-start | bytes 27652
  14.2 36.3 %all-to-all-start.1 = ((bf16[128,8,896]{2,1,0:T(8,128)(2,1)}), bf16[128,8,896]{2,1,0:T(8,128)(2,1)S(1)}, u32[]{:S(2)}, u32[]{:S(2)}) async-start(bf16[128,8,896]{2,1,0:T(8,128)(2,1)} %bitcast.21), calls=%async_computation.1 | async-start | bytes 3670016 | tf_op jit(solution)/shard_map/all_to_all | solution.py:328
  23.5 4.2 %copy-start = (bf16[8,128,576]{1,2,0:T(8,128)(2,1)S(1)}, bf16[8,128,576]{1,2,0:T(8,128)(2,1)}, u32[]{:S(2)}) copy-start(bf16[8,128,576]{1,2,0:T(8,128)(2,1)} %param.14) | copy-start | bytes 3538948
  29.2 1.8 %copy-start.3 = (s32[1,8,1]{1,2,0:T(1,128)S(1)}, s32[1,8,1]{1,2,0:T(1,128)}, u32[]{:S(2)}) copy-start(s32[1,8,1]{1,2,0:T(1,128)} %param.18) | copy-start | bytes 100
  50.5 17.8 %all-to-all-start.2 = ((bf16[8,64,512]{2,1,0:T(8,128)(2,1)}), bf16[8,64,512]{2,1,0:T(8,128)(2,1)S(1)}, u32[]{:S(2)}, u32[]{:S(2)}) async-start(bf16[8,64,512]{2,1,0:T(8,128)(2,1)} %broadcast_select_fusion), calls=%async_computation.2 | async-start | bytes 1048576 | tf_op jit(solution)/shard_map/all_to_all | solution.py:386
  68.4 6.6 %copy-start.1 = (bf16[8,64,512]{2,1,0:T(8,128)(2,1)S(1)}, bf16[8,64,512]{2,1,0:T(8,128)(2,1)}, u32[]{:S(2)}) copy-start(bf16[8,64,512]{2,1,0:T(8,128)(2,1)} %get-tuple-element.28) | copy-start | bytes 1572868
  68.4 33.6 %all-to-all-start.3 = ((bf16[128,8,896]{2,1,0:T(8,128)(2,1)}), bf16[128,8,896]{2,1,0:T(8,128)(2,1)S(1)}, u32[]{:S(2)}, u32[]{:S(2)}) async-start(bf16[128,8,896]{2,1,0:T(8,128)(2,1)} %bitcast.20), calls=%async_computation.3 | async-start | bytes 3670016 | tf_op jit(solution)/shard_map/all_to_all | solution.py:328

commit v6 on v4

--- a/solution.py
+++ b/solution.py
@@ -14,6 +14,7 @@
 
 PARTS = 4
 CAP = 2
+IN_FLIGHT = 3
 
 score_scale = 192.0 ** (-0.5)
 
@@ -183,16 +184,19 @@
     lanes, width = recv.shape
     blocks = lanes // 256
     total = lanes // PARTS
-    gate_copies, up_copies, down_copies = [], [], []
+    queue = []
     for q in range(PARTS):
         part = pl.ds(q * width, width)
-        gate_copies.append(pltpu.make_async_copy(w_gate.at[0, part, :], gates.at[q], sems.at[0, q]))
-        up_copies.append(pltpu.make_async_copy(w_up.at[0, part, :], ups.at[q], sems.at[1, q]))
-        down_copies.append(
-            pltpu.make_async_copy(w_down.at[0, :, part], downs.at[q], sems.at[2, q])
-        )
-        start_all([gate_copies[q], up_copies[q]])
-    start_all(down_copies)
+        queue.append(pltpu.make_async_copy(w_gate.at[0, part, :], gates.at[q], sems.at[0, q]))
+        queue.append(pltpu.make_async_copy(w_up.at[0, part, :], ups.at[q], sems.at[1, q]))
+    for q in range(PARTS):
+        part = pl.ds(q * width, width)
+        queue.append(pltpu.make_async_copy(w_down.at[0, :, part], downs.at[q], sems.at[2, q]))
+    start_all(queue[:IN_FLIGHT])
+
+    def arrive(n):
+        queue[n].wait()
+        start_all(queue[n + IN_FLIGHT : n + IN_FLIGHT + 1])
 
     one, two = iota((256, 256), 0), iota((256, 256), 1)
     apart = one_hot(((one & 63) * PARTS + (one >> 6)) == two)
@@ -228,15 +232,15 @@
         ]
         gate = up = None
         for q in range(PARTS):
-            gate_copies[q].wait()
+            arrive(2 * q)
             more = jnp.dot(packed[q], gates[q], preferred_element_type=F32)
             gate = more if gate is None else gate + more
-            up_copies[q].wait()
+            arrive(2 * q + 1)
             more = jnp.dot(packed[q], ups[q], preferred_element_type=F32)
             up = more if up is None else up + more
         hidden = (gate / (1.0 + jnp.exp(-gate)) * up).astype(BF16)
         for q in range(PARTS):
-            down_copies[q].wait()
+            arrive(2 * PARTS + q)
             result = jnp.dot(hidden, downs[q], preferred_element_type=F32).astype(BF16)
             result = jnp.dot(spread, result, preferred_element_type=F32).astype(BF16)
             for b in range(blocks):

time: 101 us -> 102 us (level)
  transfers between devices with their start and end apart: 4 -> 4, of which waited for: 3 -> 3; matrix products, arithmetic and copies ran while one was open for 15% -> 15% of each run, Pallas kernels for 13% -> 14%
where the time goes in v6:
time: 102 us; the launch traced here: 101 us
  waiting for transfers between devices  43.3 us (42%)
  starting transfers between devices  23.7 us (23%)
  Pallas kernels  18.1 us (18%)
  local copies, waits for them, and re-layouts  6.38 us (6%)
  matrix products  5.39 us (5%)
  other arithmetic  3.37 us (3%)
    all_to_all x2, waiting for transfers between devices, exchange(): lax.all_to_all(values, BOTH, split_axis=0, concat_axis=0, tiled=True)  40.2 us
    all_to_all x2, starting transfers between devices, exchange(): lax.all_to_all(values, BOTH, split_axis=0, concat_axis=0, tiled=True)  15.8 us
    pallas_call x1, Pallas kernels, on_device(): call(expert_kernel, [(lanes, width)], [VMEM] + [HBM] * 3, (6 * devices *...  12.3 us
    all_to_all x1, starting transfers between devices, on_device(): lax.all_to_all(send.reshape(replicas, 8, width), 'replica', split_axis=0,...  4.4 us
    all_to_all x1, starting transfers between devices, on_device(): lax.all_to_all(leave, 'replica', split_axis=0, concat_axis=0, tiled=True)  3.49 us
    all_to_all x1, waiting for transfers between devices, on_device(): lax.all_to_all(send.reshape(replicas, 8, width), 'replica', split_axis=0,...  3.16 us
    reshape x1, local copies, waits for them, and re-layouts, attend(): per_head = query_rows.reshape(row_count, HEADS, LAT)  2.78 us
    dot_general x1, matrix products, attend(): jnp.einsum('nht,ntv->nhv', weights.astype(BF16), latent_rows[:, :, :VDIM]...  2.46 us
  transfers between devices with their start and end apart: 4, of which 3 were waited for; matrix products, arithmetic and copies ran while one was open for 15% of the time, Pallas kernels for 14%

profile of v6, /device:TPU:0, one launch (start us, length us, event | category | flops | bytes accessed | tf_op | source)
XLA Modules:
  0.0 101.1 jit_solution(8780061589287260894)
XLA Ops:
  0.6 1.7 %shard_map.132 = bf16[64,896]{1,0:T(8,128)(2,1)} custom-call(s32[8]{0:T(128)} %bitcast.30, s32[8]{0:T(128)} %length_hbm.3, s32[8]{0:T(128)} %finished_hbm.3, bf16[8,3584]{1,0:T(8,128)(2,1)} %tokens_hbm.3), custom_call_target="tpu_custom_call" | custom-call | flops 1000000 | bytes 100000 | tf_op jit(solution)/shard_map/pallas_call | solution.py:329
  2.3 4.4 %all-to-all-start = ((bf16[8,8,896]{2,1,0:T(8,128)(2,1)}), bf16[8,8,896]{2,1,0:T(8,128)(2,1)S(1)}, u32[]{:S(2)}, u32[]{:S(2)}) async-start(bf16[8,8,896]{2,1,0:T(8,128)(2,1)} %bitcast.24), calls=%async_computation | async-start | bytes 229376 | tf_op jit(solution)/shard_map/all_to_all | solution.py:342
  6.7 1.2 %compare_convert_fusion = (f32[8]{0:T(128)}, s32[8]{0:T(128)S(1)}) fusion(s32[8]{0:T(128)} %length_hbm.3, s32[8]{0:T(128)} %finished_hbm.3), kind=kLoop, calls=%fused_computation.24 | loop fusion | flops 32 | bytes 128 | tf_op jit(solution)/shard_map/convert_element_type | solution.py:52
  7.9 0.1 iota_compare_fusion
  8.0 1.5 %shard_map.131 = (bf16[1024,128]{1,0:T(8,128)(2,1)S(1)}, bf16[128,1024]{1,0:T(8,128)(2,1)S(1)}, bf16[32,896]{1,0:T(8,128)(2,1)S(1)}) custom-call(s32[8]{0:T(128)} %bitcast.31, s32[8]{0:T(128)} %length_hbm.3, s32[8]{0:T(128)} %finished_hbm.3, s32[8,16]{1,0:T(8,128)} %bitcast.28, f32[8,16]{1,0:T(8,128)} %bitcast.29, bf16[8,3584]{1,0:T(8,128)(2,1)} %tokens_hbm.3), custom_call_target="tpu_custom_call" | custom-call | flops 10000000 | bytes 1000000 | tf_op jit(solution)/shard_map/pallas_call | solution.py:345
  9.5 3.2 %all-to-all-done = bf16[8,8,896]{2,1,0:T(8,128)(2,1)S(1)} async-done(((bf16[8,8,896]{2,1,0:T(8,128)(2,1)}), bf16[8,8,896]{2,1,0:T(8,128)(2,1)S(1)}, u32[]{:S(2)}, u32[]{:S(2)}) %all-to-all-start) | async-done | bytes 114720 | tf_op jit(solution)/shard_map/all_to_all | solution.py:342
  12.7 1.5 %shard_map.133 = bf16[1024,896]{1,0:T(8,128)(2,1)} custom-call(bf16[1024,128]{1,0:T(8,128)(2,1)S(1)} %get-tuple-element.12.scatter, bf16[32,896]{1,0:T(8,128)(2,1)S(1)} %get-tuple-element.13.tokens, bf16[64,896]{1,0:T(8,128)(2,1)S(1)} %bitcast.19), custom_call_target="tpu_custom_call" | custom-call | flops 200000000 | bytes 2000000 | tf_op jit(solution)/shard_map/pallas_call | solution.py:358
  14.2 0.0 copy-start.2
  14.2 9.2 %all-to-all-start.1 = ((bf16[128,8,896]{2,1,0:T(8,128)(2,1)}), bf16[128,8,896]{2,1,0:T(8,128)(2,1)S(1)}, u32[]{:S(2)}, u32[]{:S(2)}) async-start(bf16[128,8,896]{2,1,0:T(8,128)(2,1)} %bitcast.21), calls=%async_computation.1 | async-start | bytes 3670016 | tf_op jit(solution)/shard_map/all_to_all | solution.py:318
  23.5 0.0 copy-start
  23.5 2.8 %reshape.64 = bf16[8,64,576]{2,1,0:T(8,128)(2,1)} reshape(bf16[8,36864]{1,0:T(8,128)(2,1)} %param.13) | data formatting | bytes 1179648 | tf_op jit(solution)/shard_map/reshape | solution.py:32
  26.3 1.4 %fusion.9 = f32[8,1,64]{2,1,0:T(1,128)S(1)} fusion(bf16[8,64,576]{2,1,0:T(8,128)(2,1)} %reshape.64, bf16[8,576,1]{1,0,2:T(8,128)(2,1)S(1)} %bitcast.27), kind=kOutput, calls=%fused_computation.15 | convolution fusion | flops 589824 | bytes 601088 | tf_op jit(solution)/shard_map/nhl,nl->nh/dot_general | solution.py:36
  27.6 0.0 copy-done
  27.6 1.5 %fusion.14 = (f32[8,64]{1,0:T(8,128)S(1)}, f32[8,64,128]{2,1,0:T(8,128)S(1)}) fusion(bf16[8,64,576]{2,1,0:T(8,128)(2,1)} %reshape.64, bf16[8,128,576]{1,2,0:T(8,128)(2,1)S(1)} %copy-done, pred[8,128]{1,0:T(8,128)(4,1)S(1)} %iota_compare_fusion), kind=kOutput, calls=%fused_computation.30 | convolution fusion | flops 75693568 | bytes 2034688 | tf_op jit(solution)/shard_map/nhl,ntl->nht/dot_general | solution.py:34
  29.2 0.0 copy-start.3
  29.2 1.4 %copy.15 = bf16[8,128,576]{2,1,0:T(8,128)(2,1)} copy(bf16[8,128,576]{1,2,0:T(8,128)(2,1)S(1)} %copy-done) | data formatting | bytes 2359296 | tf_op jit(solution)/shard_map/optimization_barrier | solution.py:367
  30.7 0.3 fusion.5
  31.0 0.1 fusion.11
  31.1 0.7 slice_convert_fusion
  31.8 2.5 %broadcast_select_fusion.1 = (bf16[8,64,512]{2,1,0:T(8,128)(2,1)}, bf16[8,64,512]{2,1,0:T(8,128)(2,1)S(1)}) fusion(pred[8]{0:T(512)(128)(4,1)S(1)} %fusion.11, f32[8]{0:T(128)} %get-tuple-element.22, f32[8,64]{1,0:T(8,128)S(1)} %get-tuple-element.25, f32[8,512]{1,0:T(8,128)S(1)} %slice_convert_fusion, f32[8,64]{1,0:T(8,128)S(1)} %convert_element_type.21, ...), kind=kOutput, calls=%fused_computation.10 | convolution fusion | flops 68812800 | bytes 2382344 | tf_op jit(solution)/shard_map/nht,ntv->nhv/dot_general | solution.py:44
  34.2 0.6 gather_fusion
  34.8 0.9 broadcast_select_fusion
  35.8 14.8 %all-to-all-done.1 = bf16[128,8,896]{2,1,0:T(8,128)(2,1)S(1)} async-done(((bf16[128,8,896]{2,1,0:T(8,128)(2,1)}), bf16[128,8,896]{2,1,0:T(8,128)(2,1)S(1)}, u32[]{:S(2)}, u32[]{:S(2)}) %all-to-all-start.1) | async-done | bytes 1835040 | tf_op jit(solution)/shard_map/all_to_all | solution.py:318
  50.5 3.5 %all-to-all-start.2 = ((bf16[8,64,512]{2,1,0:T(8,128)(2,1)}), bf16[8,64,512]{2,1,0:T(8,128)(2,1)S(1)}, u32[]{:S(2)}, u32[]{:S(2)}) async-start(bf16[8,64,512]{2,1,0:T(8,128)(2,1)} %broadcast_select_fusion), calls=%async_computation.2 | async-start | bytes 1048576 | tf_op jit(solution)/shard_map/all_to_all | solution.py:376
  54.0 12.3 %shard_map.134 = bf16[1024,896]{1,0:T(8,128)(2,1)} custom-call(bf16[1024,896]{1,0:T(8,128)(2,1)S(1)} %bitcast.17, bf16[1,3584,1024]{2,1,0:T(8,128)(2,1)} %w_gate.1, bf16[1,3584,1024]{2,1,0:T(8,128)(2,1)} %w_up.1, bf16[1,1024,3584]{2,1,0:T(8,128)(2,1)} %w_down.1), custom_call_target="tpu_custom_call" | custom-call | flops 5637144576 | bytes 22020096 | tf_op jit(solution)/shard_map/pallas_call | solution.py:380
  66.3 0.0 all-to-all-done.2
  66.3 0.0 copy-start.1
  66.3 6.6 %all-to-all-start.3 = ((bf16[128,8,896]{2,1,0:T(8,128)(2,1)}), bf16[128,8,896]{2,1,0:T(8,128)(2,1)S(1)}, u32[]{:S(2)}, u32[]{:S(2)}) async-start(bf16[128,8,896]{2,1,0:T(8,128)(2,1)} %bitcast.20), calls=%async_computation.3 | async-start | bytes 3670016 | tf_op jit(solution)/shard_map/all_to_all | solution.py:318
  72.9 0.1 pad_maximum_fusion
  73.0 1.5 %copy.18 = bf16[2,8,64,512]{3,1,2,0:T(8,128)(2,1)} copy(bf16[2,8,64,512]{3,2,1,0:T(8,128)(2,1)S(1)} %bitcast.22) | data formatting | bytes 2097152
  74.6 25.4 %all-to-all-done.3 = bf16[128,8,896]{2,1,0:T(8,128)(2,1)S(1)} async-done(((bf16[128,8,896]{2,1,0:T(8,128)(2,1)}), bf16[128,8,896]{2,1,0:T(8,128)(2,1)S(1)}, u32[]{:S(2)}, u32[]{:S(2)}) %all-to-all-start.3) | async-done | bytes 1835040 | tf_op jit(solution)/shard_map/all_to_all | solution.py:318
  100.0 1.1 %shard_map.135 = bf16[16,3584]{1,0:T(8,128)(2,1)} custom-call(bf16[128,1024]{1,0:T(8,128)(2,1)S(1)} %get-tuple-element.20.gather, bf16[1024,896]{1,0:T(8,128)(2,1)S(1)} %bitcast.18), custom_call_target="tpu_custom_call" | custom-call | flops 200000000 | bytes 2000000 | tf_op jit(solution)/shard_map/pallas_call | solution.py:398
  (9 shorter events, 0.0 us)
Async XLA Ops:
  2.3 10.4 %all-to-all-start = ((bf16[8,8,896]{2,1,0:T(8,128)(2,1)}), bf16[8,8,896]{2,1,0:T(8,128)(2,1)S(1)}, u32[]{:S(2)}, u32[]{:S(2)}) async-start(bf16[8,8,896]{2,1,0:T(8,128)(2,1)} %bitcast.24), calls=%async_computation | async-start | bytes 229376 | tf_op jit(solution)/shard_map/all_to_all | solution.py:342
  14.2 12.0 %copy-start.2 = (bf16[8,576]{1,0:T(8,128)(2,1)S(1)}, bf16[8,576]{1,0:T(8,128)(2,1)}, u32[]{:S(2)}) copy-start(bf16[8,576]{1,0:T(8,128)(2,1)} %param.15) | copy-start | bytes 27652
  14.2 36.3 %all-to-all-start.1 = ((bf16[128,8,896]{2,1,0:T(8,128)(2,1)}), bf16[128,8,896]{2,1,0:T(8,128)(2,1)S(1)}, u32[]{:S(2)}, u32[]{:S(2)}) async-start(bf16[128,8,896]{2,1,0:T(8,128)(2,1)} %bitcast.21), calls=%async_computation.1 | async-start | bytes 3670016 | tf_op jit(solution)/shard_map/all_to_all | solution.py:318
  23.5 4.2 %copy-start = (bf16[8,128,576]{1,2,0:T(8,128)(2,1)S(1)}, bf16[8,128,576]{1,2,0:T(8,128)(2,1)}, u32[]{:S(2)}) copy-start(bf16[8,128,576]{1,2,0:T(8,128)(2,1)} %param.14) | copy-start | bytes 3538948
  29.2 1.8 %copy-start.3 = (s32[1,8,1]{1,2,0:T(1,128)S(1)}, s32[1,8,1]{1,2,0:T(1,128)}, u32[]{:S(2)}) copy-start(s32[1,8,1]{1,2,0:T(1,128)} %param.18) | copy-start | bytes 100
  50.5 15.8 %all-to-all-start.2 = ((bf16[8,64,512]{2,1,0:T(8,128)(2,1)}), bf16[8,64,512]{2,1,0:T(8,128)(2,1)S(1)}, u32[]{:S(2)}, u32[]{:S(2)}) async-start(bf16[8,64,512]{2,1,0:T(8,128)(2,1)} %broadcast_select_fusion), calls=%async_computation.2 | async-start | bytes 1048576 | tf_op jit(solution)/shard_map/all_to_all | solution.py:376
  66.3 6.6 %copy-start.1 = (bf16[8,64,512]{2,1,0:T(8,128)(2,1)S(1)}, bf16[8,64,512]{2,1,0:T(8,128)(2,1)}, u32[]{:S(2)}) copy-start(bf16[8,64,512]{2,1,0:T(8,128)(2,1)} %get-tuple-element.28) | copy-start | bytes 1572868
  66.3 33.7 %all-to-all-start.3 = ((bf16[128,8,896]{2,1,0:T(8,128)(2,1)}), bf16[128,8,896]{2,1,0:T(8,128)(2,1)S(1)}, u32[]{:S(2)}, u32[]{:S(2)}) async-start(bf16[128,8,896]{2,1,0:T(8,128)(2,1)} %bitcast.20), calls=%async_computation.3 | async-start | bytes 3670016 | tf_op jit(solution)/shard_map/all_to_all | solution.py:318

commit v7 on v4

--- a/solution.py
+++ b/solution.py
@@ -61,6 +61,10 @@
 
 def alive_of(length, finished):
     return lambda s: jnp.where(finished[s] == 0, length[s], 0)
+
+
+def my_replica():
+    return lax.axis_index("replica")
 
 
 def start_all(copies):
@@ -259,6 +263,27 @@
         sent[part, :] = value
         copies += start_all([pltpu.make_async_copy(sent.at[part], out.at[part], sems.at[0, b])])
     wait_all(copies)
+
+
+def leave_kernel(plan, attended, *outs):
+    for k, out in enumerate(outs, 1):
+        row = plan[my_replica() ^ k]
+        kept = jnp.where(row >= 0, 1.0, 0.0)
+        out[...] = (attended[jnp.maximum(row, 0)].astype(F32) * kept).astype(BF16)
+
+
+def land_kernel(plan, attended, *rest):
+    arrived, out = rest[:-1], rest[-1]
+    count = attended.shape[0]
+    for s in range(count):
+        moved = jnp.int32(0)
+        for d in range(count):
+            moved = jnp.where(plan[d] == s, 1, moved)
+        kept = jnp.where(moved == 0, 1.0, 0.0)
+        out[s] = (attended[s].astype(F32) * kept).astype(BF16)
+    out[count + my_replica()] = jnp.zeros(out.shape[1:], BF16)
+    for k, value in enumerate(arrived, 1):
+        out[count + (my_replica() ^ k)] = value[...]
 
 
 def combine_kernel(gather, recv, out):
@@ -360,18 +385,27 @@
         in_hbm=True,
     )(scatter, flat, arrived)
     own_length = jnp.where(finished == 0, lengths, 0)
-    held = lax.optimization_barrier((queries, latent_cache, new_latent, plan, outgoing))
-    queries, latent_cache, new_latent, plan, outgoing = held
+    held = lax.optimization_barrier((queries, new_latent, outgoing))
+    queries, new_latent, outgoing = held
     incoming = exchange(outgoing)
 
     attended = attend(queries, latent_cache, new_latent, own_length)
-    sending = plan >= 0
-    moved_out = jnp.any((plan[:, None] == jnp.arange(count)[None, :]), axis=0)
-    leave = jnp.where(sending[:, None, None], attended[jnp.maximum(plan, 0)], jnp.zeros((), BF16))
-    leave, incoming = lax.optimization_barrier((leave, incoming))
-    landed = lax.all_to_all(leave, "replica", split_axis=0, concat_axis=0, tiled=True)
-    stay = jnp.where(moved_out[:, None, None], jnp.zeros((), BF16), attended)
-    attended_out = jnp.concatenate([stay, landed], axis=0).reshape(slots, HEADS * VDIM)
+    leave = call(
+        leave_kernel,
+        [(HEADS, VDIM)] * (replicas - 1),
+        [SMEM, VMEM],
+        (10**6, 10**6),
+    )(plan, attended)
+    landed = []
+    for k, value in enumerate(leave, 1):
+        landed.append(lax.ppermute(value, "replica", [(i, i ^ k) for i in range(replicas)]))
+    *landed, incoming = lax.optimization_barrier((*landed, incoming))
+    attended_out = call(
+        land_kernel,
+        [(slots, HEADS, VDIM)],
+        [SMEM] + [VMEM] * replicas,
+        (10**6, 4 * 10**6),
+    )(plan, attended, *landed).reshape(slots, HEADS * VDIM)
 
     results = call(
         expert_kernel,

time: 101 us -> 102 us (level)
  starting transfers between devices: 23.7 us -> 30.3 us
  local copies, waits for them, and re-layouts: 6.38 us -> 2.48 us
  matrix products: 5.39 us -> 2.59 us
  other arithmetic: 3.37 us -> 1.04 us
  waiting for transfers between devices: 43.3 us -> 45.2 us
  Pallas kernels: 17.7 us -> 19.1 us
    ppermute x0 -> x7, waiting for transfers between devices: none -> 16.6 us  [on_device(): lax.ppermute(value, 'replica', [(i, i ^ k) for i in range(replicas)])]
    all_to_all x2, waiting for transfers between devices: 40.2 us -> 24.8 us  [exchange(): lax.all_to_all(values, BOTH, split_axis=0, concat_axis=0, tiled=True)]
    ppermute x0 -> x7, starting transfers between devices: none -> 8.23 us  [on_device(): lax.ppermute(value, 'replica', [(i, i ^ k) for i in range(replicas)])]
    all_to_all x1 -> x0, starting transfers between devices: 3.49 us -> none  [on_device(): lax.all_to_all(leave, 'replica', split_axis=0, concat_axis=0, tiled=True)]
    reshape x1, local copies, waits for them, and re-layouts: 2.78 us -> 0.8 us  [attend(): per_head = query_rows.reshape(row_count, HEADS, LAT)]
    dot_general x1, matrix products: 2.46 us -> 0.53 us  [attend(): jnp.einsum('nht,ntv->nhv', weights.astype(BF16), latent_rows[:, :, :VDIM]...]
    all_to_all x2, starting transfers between devices: 15.8 us -> 17.7 us  [exchange(): lax.all_to_all(values, BOTH, split_axis=0, concat_axis=0, tiled=True)]
    optimization_barrier x1 -> x0, local copies, waits for them, and re-layouts: 1.44 us -> none  [on_device(): lax.optimization_barrier((queries, latent_cache, new_latent, plan, outgoi...]
  transfers between devices with their start and end apart: 4 -> 10, of which waited for: 3 -> 6; matrix products, arithmetic and copies ran while one was open for 15% -> 6% of each run, Pallas kernels for 13% -> 3%
where the time goes in v7:
time: 102 us
  waiting for transfers between devices  45.2 us (44%)
  starting transfers between devices  30.3 us (30%)
  Pallas kernels  19.1 us (19%)
  matrix products  2.59 us (3%)
  local copies, waits for them, and re-layouts  2.48 us (2%)
  other arithmetic  1.04 us (1%)
    all_to_all x2, waiting for transfers between devices, exchange(): lax.all_to_all(values, BOTH, split_axis=0, concat_axis=0, tiled=True)  24.8 us
    all_to_all x2, starting transfers between devices, exchange(): lax.all_to_all(values, BOTH, split_axis=0, concat_axis=0, tiled=True)  17.7 us
    ppermute x7, waiting for transfers between devices, on_device(): lax.ppermute(value, 'replica', [(i, i ^ k) for i in range(replicas)])  16.6 us
    pallas_call x1, Pallas kernels, on_device(): call(expert_kernel, [(lanes, width)], [VMEM] + [HBM] * 3, (6 * devices *...  11.9 us
    ppermute x7, starting transfers between devices, on_device(): lax.ppermute(value, 'replica', [(i, i ^ k) for i in range(replicas)])  8.23 us
    all_to_all x1, starting transfers between devices, on_device(): lax.all_to_all(send.reshape(replicas, 8, width), 'replica', split_axis=0,...  4.4 us
    all_to_all x1, waiting for transfers between devices, on_device(): lax.all_to_all(send.reshape(replicas, 8, width), 'replica', split_axis=0,...  3.77 us
  transfers between devices with their start and end apart: 10, of which 6 were waited for; matrix products, arithmetic and copies ran while one was open for 6% of the time, Pallas kernels for 3%

profile of v7, /device:TPU:0, one launch (start us, length us, event | category | flops | bytes accessed | tf_op | source)
XLA Modules:
  0.0 101.5 jit_solution(18336832168984685466)
XLA Ops:
  0.6 1.7 %shard_map.132 = bf16[64,896]{1,0:T(8,128)(2,1)} custom-call(s32[8]{0:T(128)} %bitcast.21, s32[8]{0:T(128)} %length_hbm.3, s32[8]{0:T(128)} %finished_hbm.3, bf16[8,3584]{1,0:T(8,128)(2,1)} %tokens_hbm.3), custom_call_target="tpu_custom_call" | custom-call | flops 1000000 | bytes 100000 | tf_op jit(solution)/shard_map/pallas_call | solution.py:350
  2.3 4.4 %all-to-all-start = ((bf16[8,8,896]{2,1,0:T(8,128)(2,1)}), bf16[8,8,896]{2,1,0:T(8,128)(2,1)S(1)}, u32[]{:S(2)}, u32[]{:S(2)}) async-start(bf16[8,8,896]{2,1,0:T(8,128)(2,1)} %bitcast.28), calls=%async_computation | async-start | bytes 229376 | tf_op jit(solution)/shard_map/all_to_all | solution.py:363
  6.7 0.7 compare_convert_fusion
  7.4 1.5 %shard_map.131 = (bf16[1024,128]{1,0:T(8,128)(2,1)S(1)}, bf16[128,1024]{1,0:T(8,128)(2,1)S(1)}, bf16[32,896]{1,0:T(8,128)(2,1)S(1)}) custom-call(s32[8]{0:T(128)} %bitcast.22, s32[8]{0:T(128)} %length_hbm.3, s32[8]{0:T(128)} %finished_hbm.3, s32[8,16]{1,0:T(8,128)} %bitcast.32, f32[8,16]{1,0:T(8,128)} %bitcast.33, bf16[8,3584]{1,0:T(8,128)(2,1)} %tokens_hbm.3), custom_call_target="tpu_custom_call" | custom-call | flops 10000000 | bytes 1000000 | tf_op jit(solution)/shard_map/pallas_call | solution.py:366
  8.9 3.8 %all-to-all-done = bf16[8,8,896]{2,1,0:T(8,128)(2,1)S(1)} async-done(((bf16[8,8,896]{2,1,0:T(8,128)(2,1)}), bf16[8,8,896]{2,1,0:T(8,128)(2,1)S(1)}, u32[]{:S(2)}, u32[]{:S(2)}) %all-to-all-start) | async-done | bytes 114720 | tf_op jit(solution)/shard_map/all_to_all | solution.py:363
  12.7 1.6 %shard_map.133 = bf16[1024,896]{1,0:T(8,128)(2,1)} custom-call(bf16[1024,128]{1,0:T(8,128)(2,1)S(1)} %get-tuple-element.23.scatter, bf16[32,896]{1,0:T(8,128)(2,1)S(1)} %get-tuple-element.24.tokens, bf16[64,896]{1,0:T(8,128)(2,1)S(1)} %bitcast.20), custom_call_target="tpu_custom_call" | custom-call | flops 200000000 | bytes 2000000 | tf_op jit(solution)/shard_map/pallas_call | solution.py:379
  14.3 9.2 %all-to-all-start.1 = ((bf16[128,8,896]{2,1,0:T(8,128)(2,1)}), bf16[128,8,896]{2,1,0:T(8,128)(2,1)S(1)}, u32[]{:S(2)}, u32[]{:S(2)}) async-start(bf16[128,8,896]{2,1,0:T(8,128)(2,1)} %bitcast.26), calls=%async_computation.1 | async-start | bytes 3670016 | tf_op jit(solution)/shard_map/all_to_all | solution.py:339
  23.5 0.1 iota_compare_fusion
  23.6 0.8 reshape.61
  24.4 0.3 fusion.9
  24.7 1.8 %fusion.13 = (f32[8,64]{1,0:T(8,128)S(1)}, f32[8,64,128]{2,1,0:T(8,128)S(1)}) fusion(bf16[8,64,576]{2,1,0:T(8,128)(2,1)S(1)} %reshape.61, bf16[8,128,576]{1,2,0:T(8,128)(2,1)} %param.14, pred[8,128]{1,0:T(8,128)(4,1)S(1)} %iota_compare_fusion), kind=kOutput, calls=%fused_computation.21 | convolution fusion | flops 75693568 | bytes 2034688 | tf_op jit(solution)/shard_map/nhl,ntl->nht/dot_general | solution.py:33
  26.5 0.3 fusion.5
  26.8 0.5 fusion.2.attended
  27.4 0.1 copy-done
  27.5 0.6 shard_map.134
  28.1 0.1 collective-permute-start
  28.2 1.1 %collective-permute-start.1 = (bf16[64,512]{1,0:T(8,128)(2,1)S(1)}, bf16[64,512]{1,0:T(8,128)(2,1)S(1)}, u32[]{:S(2)}, u32[]{:S(2)}) collective-permute-start(bf16[64,512]{1,0:T(8,128)(2,1)S(1)} %get-tuple-element.28), channel_id=1, source_target_pairs={{0,32},{16,48},{32,0},{48,16},{64,96},{80,112},{96,64},{112,80},{1... | collective-permute-start | bytes 196616 | tf_op jit(solution)/shard_map/ppermute | solution.py:401
  29.3 0.8 collective-permute-start.2
  30.1 2.4 %collective-permute-start.3 = (bf16[64,512]{1,0:T(8,128)(2,1)S(1)}, bf16[64,512]{1,0:T(8,128)(2,1)S(1)}, u32[]{:S(2)}, u32[]{:S(2)}) collective-permute-start(bf16[64,512]{1,0:T(8,128)(2,1)S(1)} %get-tuple-element.30), channel_id=1, source_target_pairs={{0,64},{16,80},{32,96},{48,112},{64,0},{80,16},{96,32},{112,48},{1... | collective-permute-start | bytes 196616 | tf_op jit(solution)/shard_map/ppermute | solution.py:401
  32.5 0.8 collective-permute-start.4
  33.3 2.2 %collective-permute-start.5 = (bf16[64,512]{1,0:T(8,128)(2,1)S(1)}, bf16[64,512]{1,0:T(8,128)(2,1)S(1)}, u32[]{:S(2)}, u32[]{:S(2)}) collective-permute-start(bf16[64,512]{1,0:T(8,128)(2,1)S(1)} %get-tuple-element.32), channel_id=1, source_target_pairs={{0,96},{16,112},{32,64},{48,80},{64,32},{80,48},{96,0},{112,16},{1... | collective-permute-start | bytes 196616 | tf_op jit(solution)/shard_map/ppermute | solution.py:401
  35.5 10.8 %collective-permute-done.1.rest_1_ = bf16[64,512]{1,0:T(8,128)(2,1)S(1)} collective-permute-done((bf16[64,512]{1,0:T(8,128)(2,1)S(1)}, bf16[64,512]{1,0:T(8,128)(2,1)S(1)}, u32[]{:S(2)}, u32[]{:S(2)}) %collective-permute-start.1) | collective-permute-done | bytes 65568 | tf_op jit(solution)/shard_map/ppermute | solution.py:401
  46.3 0.8 collective-permute-start.6
  47.2 3.5 %collective-permute-done.3.rest_3_ = bf16[64,512]{1,0:T(8,128)(2,1)S(1)} collective-permute-done((bf16[64,512]{1,0:T(8,128)(2,1)S(1)}, bf16[64,512]{1,0:T(8,128)(2,1)S(1)}, u32[]{:S(2)}, u32[]{:S(2)}) %collective-permute-start.3) | collective-permute-done | bytes 65568 | tf_op jit(solution)/shard_map/ppermute | solution.py:401
  50.7 0.5 collective-permute-done.4.rest_4_
  51.2 1.8 %collective-permute-done.6.rest_6_ = bf16[64,512]{1,0:T(8,128)(2,1)S(1)} collective-permute-done((bf16[64,512]{1,0:T(8,128)(2,1)S(1)}, bf16[64,512]{1,0:T(8,128)(2,1)S(1)}, u32[]{:S(2)}, u32[]{:S(2)}) %collective-permute-start.6) | collective-permute-done | bytes 65568 | tf_op jit(solution)/shard_map/ppermute | solution.py:401
  53.0 11.9 %shard_map.136 = bf16[1024,896]{1,0:T(8,128)(2,1)} custom-call(bf16[1024,896]{1,0:T(8,128)(2,1)S(1)} %bitcast.17, bf16[1,3584,1024]{2,1,0:T(8,128)(2,1)} %w_gate.1, bf16[1,3584,1024]{2,1,0:T(8,128)(2,1)} %w_up.1, bf16[1,1024,3584]{2,1,0:T(8,128)(2,1)} %w_down.1), custom_call_target="tpu_custom_call" | custom-call | flops 5637144576 | bytes 22020096 | tf_op jit(solution)/shard_map/pallas_call | solution.py:410
  64.9 8.5 %all-to-all-start.2 = ((bf16[128,8,896]{2,1,0:T(8,128)(2,1)}), bf16[128,8,896]{2,1,0:T(8,128)(2,1)S(1)}, u32[]{:S(2)}, u32[]{:S(2)}) async-start(bf16[128,8,896]{2,1,0:T(8,128)(2,1)} %bitcast.25), calls=%async_computation.2 | async-start | bytes 3670016 | tf_op jit(solution)/shard_map/all_to_all | solution.py:339
  73.4 0.7 shard_map.135
  74.1 1.5 %copy.18 = bf16[2,8,64,512]{3,1,2,0:T(8,128)(2,1)} copy(bf16[2,8,64,512]{3,2,1,0:T(8,128)(2,1)S(1)} %bitcast.19) | data formatting | bytes 2097152
  75.6 24.8 %all-to-all-done.2 = bf16[128,8,896]{2,1,0:T(8,128)(2,1)S(1)} async-done(((bf16[128,8,896]{2,1,0:T(8,128)(2,1)}), bf16[128,8,896]{2,1,0:T(8,128)(2,1)S(1)}, u32[]{:S(2)}, u32[]{:S(2)}) %all-to-all-start.2) | async-done | bytes 1835040 | tf_op jit(solution)/shard_map/all_to_all | solution.py:339
  100.4 1.1 %shard_map.137 = bf16[16,3584]{1,0:T(8,128)(2,1)} custom-call(bf16[128,1024]{1,0:T(8,128)(2,1)S(1)} %get-tuple-element.42.gather, bf16[1024,896]{1,0:T(8,128)(2,1)S(1)} %bitcast.18), custom_call_target="tpu_custom_call" | custom-call | flops 200000000 | bytes 2000000 | tf_op jit(solution)/shard_map/pallas_call | solution.py:428
  (15 shorter events, 0.1 us)
Async XLA Ops:
  2.3 10.4 %all-to-all-start = ((bf16[8,8,896]{2,1,0:T(8,128)(2,1)}), bf16[8,8,896]{2,1,0:T(8,128)(2,1)S(1)}, u32[]{:S(2)}, u32[]{:S(2)}) async-start(bf16[8,8,896]{2,1,0:T(8,128)(2,1)} %bitcast.28), calls=%async_computation | async-start | bytes 229376 | tf_op jit(solution)/shard_map/all_to_all | solution.py:363
  14.3 9.3 %copy-start.2 = (bf16[8,36864]{1,0:T(8,128)(2,1)S(1)}, bf16[8,36864]{1,0:T(8,128)(2,1)}, u32[]{:S(2)}) copy-start(bf16[8,36864]{1,0:T(8,128)(2,1)} %param.13) | copy-start | bytes 1769476
  14.3 10.1 %copy-start.3 = (bf16[8,576]{1,0:T(8,128)(2,1)S(1)}, bf16[8,576]{1,0:T(8,128)(2,1)}, u32[]{:S(2)}) copy-start(bf16[8,576]{1,0:T(8,128)(2,1)} %param.15) | copy-start | bytes 27652
  14.3 38.7 %all-to-all-start.1 = ((bf16[128,8,896]{2,1,0:T(8,128)(2,1)}), bf16[128,8,896]{2,1,0:T(8,128)(2,1)S(1)}, u32[]{:S(2)}, u32[]{:S(2)}) async-start(bf16[128,8,896]{2,1,0:T(8,128)(2,1)} %bitcast.26), calls=%async_computation.1 | async-start | bytes 3670016 | tf_op jit(solution)/shard_map/all_to_all | solution.py:339
  24.4 2.4 %copy-start.1 = (bf16[8,128,576]{1,2,0:T(8,128)(2,1)S(1)}, bf16[8,128,576]{1,2,0:T(8,128)(2,1)}, u32[]{:S(2)}) copy-start(bf16[8,128,576]{1,2,0:T(8,128)(2,1)} %param.14) | copy-start | bytes 3538948
  26.8 0.7 copy-start
  28.1 5.2 %collective-permute-start = (bf16[64,512]{1,0:T(8,128)(2,1)S(1)}, bf16[64,512]{1,0:T(8,128)(2,1)S(1)}, u32[]{:S(2)}, u32[]{:S(2)}) collective-permute-start(bf16[64,512]{1,0:T(8,128)(2,1)S(1)} %get-tuple-element.27), channel_id=1, source_target_pairs={{0,16},{16,0},{32,48},{48,32},{64,80},{80,64},{96,112},{112,96},{1... | collective-permute-start | bytes 196616 | tf_op jit(solution)/shard_map/ppermute | solution.py:401
  28.2 18.1 %collective-permute-start.1 = (bf16[64,512]{1,0:T(8,128)(2,1)S(1)}, bf16[64,512]{1,0:T(8,128)(2,1)S(1)}, u32[]{:S(2)}, u32[]{:S(2)}) collective-permute-start(bf16[64,512]{1,0:T(8,128)(2,1)S(1)} %get-tuple-element.28), channel_id=1, source_target_pairs={{0,32},{16,48},{32,0},{48,16},{64,96},{80,112},{96,64},{112,80},{1... | collective-permute-start | bytes 196616 | tf_op jit(solution)/shard_map/ppermute | solution.py:401
  29.3 17.9 %collective-permute-start.2 = (bf16[64,512]{1,0:T(8,128)(2,1)S(1)}, bf16[64,512]{1,0:T(8,128)(2,1)S(1)}, u32[]{:S(2)}, u32[]{:S(2)}) collective-permute-start(bf16[64,512]{1,0:T(8,128)(2,1)S(1)} %get-tuple-element.29), channel_id=1, source_target_pairs={{0,48},{16,32},{32,16},{48,0},{64,112},{80,96},{96,80},{112,64},{1... | collective-permute-start | bytes 196616 | tf_op jit(solution)/shard_map/ppermute | solution.py:401
  30.1 20.7 %collective-permute-start.3 = (bf16[64,512]{1,0:T(8,128)(2,1)S(1)}, bf16[64,512]{1,0:T(8,128)(2,1)S(1)}, u32[]{:S(2)}, u32[]{:S(2)}) collective-permute-start(bf16[64,512]{1,0:T(8,128)(2,1)S(1)} %get-tuple-element.30), channel_id=1, source_target_pairs={{0,64},{16,80},{32,96},{48,112},{64,0},{80,16},{96,32},{112,48},{1... | collective-permute-start | bytes 196616 | tf_op jit(solution)/shard_map/ppermute | solution.py:401
  32.5 18.7 %collective-permute-start.4 = (bf16[64,512]{1,0:T(8,128)(2,1)S(1)}, bf16[64,512]{1,0:T(8,128)(2,1)S(1)}, u32[]{:S(2)}, u32[]{:S(2)}) collective-permute-start(bf16[64,512]{1,0:T(8,128)(2,1)S(1)} %get-tuple-element.31), channel_id=1, source_target_pairs={{0,80},{16,64},{32,112},{48,96},{64,16},{80,0},{96,48},{112,32},{1... | collective-permute-start | bytes 196616 | tf_op jit(solution)/shard_map/ppermute | solution.py:401
  33.3 17.9 %collective-permute-start.5 = (bf16[64,512]{1,0:T(8,128)(2,1)S(1)}, bf16[64,512]{1,0:T(8,128)(2,1)S(1)}, u32[]{:S(2)}, u32[]{:S(2)}) collective-permute-start(bf16[64,512]{1,0:T(8,128)(2,1)S(1)} %get-tuple-element.32), channel_id=1, source_target_pairs={{0,96},{16,112},{32,64},{48,80},{64,32},{80,48},{96,0},{112,16},{1... | collective-permute-start | bytes 196616 | tf_op jit(solution)/shard_map/ppermute | solution.py:401
  46.3 6.7 %collective-permute-start.6 = (bf16[64,512]{1,0:T(8,128)(2,1)S(1)}, bf16[64,512]{1,0:T(8,128)(2,1)S(1)}, u32[]{:S(2)}, u32[]{:S(2)}) collective-permute-start(bf16[64,512]{1,0:T(8,128)(2,1)S(1)} %get-tuple-element.33), channel_id=1, source_target_pairs={{0,112},{16,96},{32,80},{48,64},{64,48},{80,32},{96,16},{112,0},{1... | collective-permute-start | bytes 196616 | tf_op jit(solution)/shard_map/ppermute | solution.py:401
  64.9 35.5 %all-to-all-start.2 = ((bf16[128,8,896]{2,1,0:T(8,128)(2,1)}), bf16[128,8,896]{2,1,0:T(8,128)(2,1)S(1)}, u32[]{:S(2)}, u32[]{:S(2)}) async-start(bf16[128,8,896]{2,1,0:T(8,128)(2,1)} %bitcast.25), calls=%async_computation.2 | async-start | bytes 3670016 | tf_op jit(solution)/shard_map/all_to_all | solution.py:339

commit v8 on v7

--- a/solution.py
+++ b/solution.py
@@ -265,25 +265,35 @@
     wait_all(copies)
 
 
-def leave_kernel(plan, attended, *outs):
-    for k, out in enumerate(outs, 1):
-        row = plan[my_replica() ^ k]
-        kept = jnp.where(row >= 0, 1.0, 0.0)
-        out[...] = (attended[jnp.maximum(row, 0)].astype(F32) * kept).astype(BF16)
-
-
-def land_kernel(plan, attended, *rest):
-    arrived, out = rest[:-1], rest[-1]
+def leave_kernel(plan, attended, own, beside):
+    for n in range(own.shape[0]):
+        for core, out in enumerate((own, beside)):
+            row = plan[my_replica() ^ (2 * n + core)]
+            kept = jnp.where(row >= 0, 1.0, 0.0)
+            out[n] = (attended[jnp.maximum(row, 0)].astype(F32) * kept).astype(BF16)
+
+
+def pair_kernel(own, handed, *outs):
+    for n, out in enumerate(outs, 1):
+        out[0] = own[n]
+        out[1] = handed[n]
+
+
+def land_kernel(plan, attended, handed, *rest):
+    arrived, out = rest[:-2], rest[-1]
     count = attended.shape[0]
+    me = my_replica()
     for s in range(count):
         moved = jnp.int32(0)
         for d in range(count):
             moved = jnp.where(plan[d] == s, 1, moved)
         kept = jnp.where(moved == 0, 1.0, 0.0)
         out[s] = (attended[s].astype(F32) * kept).astype(BF16)
-    out[count + my_replica()] = jnp.zeros(out.shape[1:], BF16)
-    for k, value in enumerate(arrived, 1):
-        out[count + (my_replica() ^ k)] = value[...]
+    out[count + me] = jnp.zeros(out.shape[1:], BF16)
+    out[count + (me ^ 1)] = handed[0]
+    for n, rows in enumerate(arrived, 1):
+        for core in range(2):
+            out[count + (me ^ (2 * n + core))] = rows[core]
 
 
 def combine_kernel(gather, recv, out):
@@ -390,23 +400,25 @@
     incoming = exchange(outgoing)
 
     attended = attend(queries, latent_cache, new_latent, own_length)
-    leave = call(
+    def swap(values, k):
+        return lax.ppermute(values, "replica", [(i, i ^ k) for i in range(replicas)])
+
+    chips = replicas // 2
+    own, beside = call(
         leave_kernel,
-        [(HEADS, VDIM)] * (replicas - 1),
+        [(chips, HEADS, VDIM)] * 2,
         [SMEM, VMEM],
         (10**6, 10**6),
     )(plan, attended)
-    landed = []
-    for k, value in enumerate(leave, 1):
-        landed.append(lax.ppermute(value, "replica", [(i, i ^ k) for i in range(replicas)]))
+    handed = swap(beside, 1)
+    pairs = call(
+        pair_kernel,
+        [(2, HEADS, VDIM)] * (chips - 1),
+        [VMEM] * 2,
+        (10**6, 10**6),
+    )(own, handed)
+    landed = [swap(pair, 2 * n) for n, pair in enumerate(pairs, 1)]
     *landed, incoming = lax.optimization_barrier((*landed, incoming))
-    attended_out = call(
-        land_kernel,
-        [(slots, HEADS, VDIM)],
-        [SMEM] + [VMEM] * replicas,
-        (10**6, 4 * 10**6),
-    )(plan, attended, *landed).reshape(slots, HEADS * VDIM)
-
     results = call(
         expert_kernel,
         [(lanes, width)],
@@ -425,6 +437,12 @@
         True,
     )(incoming, *in_hbm(w_gate, w_up, w_down))
     returned = exchange(results)
+    attended_out = call(
+        land_kernel,
+        [(slots, HEADS, VDIM)],
+        [SMEM] + [VMEM] * (1 + chips) + [HBM],
+        (10**6, 4 * 10**6),
+    )(plan, attended, handed, *landed, *in_hbm(results)).reshape(slots, HEADS * VDIM)
     expert_out = call(combine_kernel, [(slots, model)], [VMEM] * 2, (2 * 10**8, 2 * 10**6))(
         gather, returned
     )

time: 102 us -> 101 us (level)
  starting transfers between devices: 30.3 us -> 26.9 us
  waiting for transfers between devices: 45.2 us -> 47.1 us
    ppermute x7 -> x4, starting transfers between devices: 8.23 us -> 4.86 us  [swap(): lax.ppermute(values, 'replica', [(i, i ^ k) for i in range(replicas)])]
    ppermute x7 -> x4, waiting for transfers between devices: 16.6 us -> 18.6 us  [swap(): lax.ppermute(values, 'replica', [(i, i ^ k) for i in range(replicas)])]
  transfers between devices with their start and end apart: 10 -> 7, of which waited for: 6 -> 5; matrix products, arithmetic and copies ran while one was open for 6% -> 6% of each run, Pallas kernels for 3% -> 3%
where the time goes in v8:
time: 101 us; the launch traced here: 100 us
  waiting for transfers between devices  47.1 us (47%)
  starting transfers between devices  26.9 us (27%)
  Pallas kernels  19.1 us (19%)
  matrix products  2.6 us (3%)
  local copies, waits for them, and re-layouts  2.47 us (2%)
  other arithmetic  1.04 us (1%)
    all_to_all x2, waiting for transfers between devices, exchange(): lax.all_to_all(values, BOTH, split_axis=0, concat_axis=0, tiled=True)  24.8 us
    ppermute x4, waiting for transfers between devices, swap(): lax.ppermute(values, 'replica', [(i, i ^ k) for i in range(replicas)])  18.6 us
    all_to_all x2, starting transfers between devices, exchange(): lax.all_to_all(values, BOTH, split_axis=0, concat_axis=0, tiled=True)  17.7 us
    pallas_call x1, Pallas kernels, on_device(): call(expert_kernel, [(lanes, width)], [VMEM] + [HBM] * 3, (6 * devices *...  11.9 us
    ppermute x4, starting transfers between devices, swap(): lax.ppermute(values, 'replica', [(i, i ^ k) for i in range(replicas)])  4.86 us
    all_to_all x1, starting transfers between devices, on_device(): lax.all_to_all(send.reshape(replicas, 8, width), 'replica', split_axis=0,...  4.4 us
    all_to_all x1, waiting for transfers between devices, on_device(): lax.all_to_all(send.reshape(replicas, 8, width), 'replica', split_axis=0,...  3.69 us
  transfers between devices with their start and end apart: 7, of which 5 were waited for; matrix products, arithmetic and copies ran while one was open for 6% of the time, Pallas kernels for 3%

profile of v8, /device:TPU:0, one launch (start us, length us, event | category | flops | bytes accessed | tf_op | source)
XLA Modules:
  0.0 100.1 jit_solution(11209761391066426891)
XLA Ops:
  0.6 1.7 %shard_map.132 = bf16[64,896]{1,0:T(8,128)(2,1)} custom-call(s32[8]{0:T(128)} %bitcast.21, s32[8]{0:T(128)} %length_hbm.3, s32[8]{0:T(128)} %finished_hbm.3, bf16[8,3584]{1,0:T(8,128)(2,1)} %tokens_hbm.3), custom_call_target="tpu_custom_call" | custom-call | flops 1000000 | bytes 100000 | tf_op jit(solution)/shard_map/pallas_call | solution.py:360
  2.3 4.4 %all-to-all-start = ((bf16[8,8,896]{2,1,0:T(8,128)(2,1)}), bf16[8,8,896]{2,1,0:T(8,128)(2,1)S(1)}, u32[]{:S(2)}, u32[]{:S(2)}) async-start(bf16[8,8,896]{2,1,0:T(8,128)(2,1)} %bitcast.28), calls=%async_computation | async-start | bytes 229376 | tf_op jit(solution)/shard_map/all_to_all | solution.py:373
  6.7 0.7 compare_convert_fusion
  7.4 0.1 iota_compare_fusion
  7.5 1.5 %shard_map.131 = (bf16[1024,128]{1,0:T(8,128)(2,1)S(1)}, bf16[128,1024]{1,0:T(8,128)(2,1)S(1)}, bf16[32,896]{1,0:T(8,128)(2,1)S(1)}) custom-call(s32[8]{0:T(128)} %bitcast.22, s32[8]{0:T(128)} %length_hbm.3, s32[8]{0:T(128)} %finished_hbm.3, s32[8,16]{1,0:T(8,128)} %bitcast.32, f32[8,16]{1,0:T(8,128)} %bitcast.33, bf16[8,3584]{1,0:T(8,128)(2,1)} %tokens_hbm.3), custom_call_target="tpu_custom_call" | custom-call | flops 10000000 | bytes 1000000 | tf_op jit(solution)/shard_map/pallas_call | solution.py:376
  9.0 3.7 %all-to-all-done = bf16[8,8,896]{2,1,0:T(8,128)(2,1)S(1)} async-done(((bf16[8,8,896]{2,1,0:T(8,128)(2,1)}), bf16[8,8,896]{2,1,0:T(8,128)(2,1)S(1)}, u32[]{:S(2)}, u32[]{:S(2)}) %all-to-all-start) | async-done | bytes 114720 | tf_op jit(solution)/shard_map/all_to_all | solution.py:373
  12.7 1.6 %shard_map.133 = bf16[1024,896]{1,0:T(8,128)(2,1)} custom-call(bf16[1024,128]{1,0:T(8,128)(2,1)S(1)} %get-tuple-element.17.scatter, bf16[32,896]{1,0:T(8,128)(2,1)S(1)} %get-tuple-element.18.tokens, bf16[64,896]{1,0:T(8,128)(2,1)S(1)} %bitcast.20), custom_call_target="tpu_custom_call" | custom-call | flops 200000000 | bytes 2000000 | tf_op jit(solution)/shard_map/pallas_call | solution.py:389
  14.3 0.0 copy-start.2
  14.3 0.0 copy-start.3
  14.3 9.2 %all-to-all-start.1 = ((bf16[128,8,896]{2,1,0:T(8,128)(2,1)}), bf16[128,8,896]{2,1,0:T(8,128)(2,1)S(1)}, u32[]{:S(2)}, u32[]{:S(2)}) async-start(bf16[128,8,896]{2,1,0:T(8,128)(2,1)} %bitcast.26), calls=%async_computation.1 | async-start | bytes 3670016 | tf_op jit(solution)/shard_map/all_to_all | solution.py:349
  23.5 0.8 reshape.61
  24.3 0.0 copy-start.1
  24.3 0.3 fusion.9
  24.6 1.8 %fusion.13 = (f32[8,64]{1,0:T(8,128)S(1)}, f32[8,64,128]{2,1,0:T(8,128)S(1)}) fusion(bf16[8,64,576]{2,1,0:T(8,128)(2,1)S(1)} %reshape.61, bf16[8,128,576]{1,2,0:T(8,128)(2,1)} %param.14, pred[8,128]{1,0:T(8,128)(4,1)S(1)} %iota_compare_fusion), kind=kOutput, calls=%fused_computation.21 | convolution fusion | flops 75693568 | bytes 2034688 | tf_op jit(solution)/shard_map/nhl,ntl->nht/dot_general | solution.py:33
  26.4 0.3 fusion.5
  26.8 0.0 copy-start
  26.8 0.5 fusion.2.attended
  27.3 0.1 copy-done
  27.4 0.6 shard_map.134
  28.1 0.1 collective-permute-start
  28.2 1.5 %collective-permute-done.handed = bf16[4,64,512]{2,1,0:T(8,128)(2,1)S(1)} collective-permute-done((bf16[4,64,512]{2,1,0:T(8,128)(2,1)S(1)}, bf16[4,64,512]{2,1,0:T(8,128)(2,1)S(1)}, u32[]{:S(2)}, u32[]{:S(2)}) %collective-permute-start) | collective-permute-done | bytes 262176 | tf_op jit(solution)/shard_map/ppermute | solution.py:404
  29.7 1.0 %collective-permute-start.1 = (bf16[2,64,512]{2,1,0:T(8,128)(2,1)S(1)}, bf16[2,64,512]{2,1,0:T(8,128)(2,1)S(1)}, u32[]{:S(2)}, u32[]{:S(2)}) collective-permute-start(bf16[2,64,512]{2,1,0:T(8,128)(2,1)S(1)} %get-tuple-element.23), channel_id=1, source_target_pairs={{0,32},{16,48},{32,0},{48,16},{64,96},{80,112},{96,64},{112,80},{1... | collective-permute-start | bytes 393224 | tf_op jit(solution)/shard_map/ppermute | solution.py:404
  30.8 2.7 %collective-permute-start.2 = (bf16[2,64,512]{2,1,0:T(8,128)(2,1)S(1)}, bf16[2,64,512]{2,1,0:T(8,128)(2,1)S(1)}, u32[]{:S(2)}, u32[]{:S(2)}) collective-permute-start(bf16[2,64,512]{2,1,0:T(8,128)(2,1)S(1)} %get-tuple-element.24), channel_id=1, source_target_pairs={{0,64},{16,80},{32,96},{48,112},{64,0},{80,16},{96,32},{112,48},{1... | collective-permute-start | bytes 393224 | tf_op jit(solution)/shard_map/ppermute | solution.py:404
  33.4 1.1 %collective-permute-start.3 = (bf16[2,64,512]{2,1,0:T(8,128)(2,1)S(1)}, bf16[2,64,512]{2,1,0:T(8,128)(2,1)S(1)}, u32[]{:S(2)}, u32[]{:S(2)}) collective-permute-start(bf16[2,64,512]{2,1,0:T(8,128)(2,1)S(1)} %get-tuple-element.25), channel_id=1, source_target_pairs={{0,96},{16,112},{32,64},{48,80},{64,32},{80,48},{96,0},{112,16},{1... | collective-permute-start | bytes 393224 | tf_op jit(solution)/shard_map/ppermute | solution.py:404
  34.5 13.3 %collective-permute-done.1.rest_0_ = bf16[2,64,512]{2,1,0:T(8,128)(2,1)S(1)} collective-permute-done((bf16[2,64,512]{2,1,0:T(8,128)(2,1)S(1)}, bf16[2,64,512]{2,1,0:T(8,128)(2,1)S(1)}, u32[]{:S(2)}, u32[]{:S(2)}) %collective-permute-start.1) | collective-permute-done | bytes 131104 | tf_op jit(solution)/shard_map/ppermute | solution.py:404
  47.7 3.8 %collective-permute-done.2.rest_1_ = bf16[2,64,512]{2,1,0:T(8,128)(2,1)S(1)} collective-permute-done((bf16[2,64,512]{2,1,0:T(8,128)(2,1)S(1)}, bf16[2,64,512]{2,1,0:T(8,128)(2,1)S(1)}, u32[]{:S(2)}, u32[]{:S(2)}) %collective-permute-start.2) | collective-permute-done | bytes 131104 | tf_op jit(solution)/shard_map/ppermute | solution.py:404
  51.6 11.9 %shard_map.136.rest_3_ = bf16[1024,896]{1,0:T(8,128)(2,1)} custom-call(bf16[1024,896]{1,0:T(8,128)(2,1)S(1)} %bitcast.17, bf16[1,3584,1024]{2,1,0:T(8,128)(2,1)} %w_gate.1, bf16[1,3584,1024]{2,1,0:T(8,128)(2,1)} %w_up.1, bf16[1,1024,3584]{2,1,0:T(8,128)(2,1)} %w_down.1), custom_call_target="tpu_custom_call" | custom-call | flops 5637144576 | bytes 22020096 | tf_op jit(solution)/shard_map/pallas_call | solution.py:422
  63.5 8.5 %all-to-all-start.2 = ((bf16[128,8,896]{2,1,0:T(8,128)(2,1)}), bf16[128,8,896]{2,1,0:T(8,128)(2,1)S(1)}, u32[]{:S(2)}, u32[]{:S(2)}) async-start(bf16[128,8,896]{2,1,0:T(8,128)(2,1)} %bitcast.25), calls=%async_computation.2 | async-start | bytes 3670016 | tf_op jit(solution)/shard_map/all_to_all | solution.py:349
  72.0 0.7 shard_map.137
  72.7 1.5 %copy.18 = bf16[2,8,64,512]{3,1,2,0:T(8,128)(2,1)} copy(bf16[2,8,64,512]{3,2,1,0:T(8,128)(2,1)S(1)} %bitcast.19) | data formatting | bytes 2097152
  74.2 24.8 %all-to-all-done.2 = bf16[128,8,896]{2,1,0:T(8,128)(2,1)S(1)} async-done(((bf16[128,8,896]{2,1,0:T(8,128)(2,1)}), bf16[128,8,896]{2,1,0:T(8,128)(2,1)S(1)}, u32[]{:S(2)}, u32[]{:S(2)}) %all-to-all-start.2) | async-done | bytes 1835040 | tf_op jit(solution)/shard_map/all_to_all | solution.py:349
  99.0 1.1 %shard_map.138 = bf16[16,3584]{1,0:T(8,128)(2,1)} custom-call(bf16[128,1024]{1,0:T(8,128)(2,1)S(1)} %get-tuple-element.31.gather, bf16[1024,896]{1,0:T(8,128)(2,1)S(1)} %bitcast.18), custom_call_target="tpu_custom_call" | custom-call | flops 200000000 | bytes 2000000 | tf_op jit(solution)/shard_map/pallas_call | solution.py:446
  (10 shorter events, 0.1 us)
Async XLA Ops:
  2.3 10.4 %all-to-all-start = ((bf16[8,8,896]{2,1,0:T(8,128)(2,1)}), bf16[8,8,896]{2,1,0:T(8,128)(2,1)S(1)}, u32[]{:S(2)}, u32[]{:S(2)}) async-start(bf16[8,8,896]{2,1,0:T(8,128)(2,1)} %bitcast.28), calls=%async_computation | async-start | bytes 229376 | tf_op jit(solution)/shard_map/all_to_all | solution.py:373
  14.3 9.2 %copy-start.2 = (bf16[8,36864]{1,0:T(8,128)(2,1)S(1)}, bf16[8,36864]{1,0:T(8,128)(2,1)}, u32[]{:S(2)}) copy-start(bf16[8,36864]{1,0:T(8,128)(2,1)} %param.13) | copy-start | bytes 1769476
  14.3 10.1 %copy-start.3 = (bf16[8,576]{1,0:T(8,128)(2,1)S(1)}, bf16[8,576]{1,0:T(8,128)(2,1)}, u32[]{:S(2)}) copy-start(bf16[8,576]{1,0:T(8,128)(2,1)} %param.15) | copy-start | bytes 27652
  14.3 37.3 %all-to-all-start.1 = ((bf16[128,8,896]{2,1,0:T(8,128)(2,1)}), bf16[128,8,896]{2,1,0:T(8,128)(2,1)S(1)}, u32[]{:S(2)}, u32[]{:S(2)}) async-start(bf16[128,8,896]{2,1,0:T(8,128)(2,1)} %bitcast.26), calls=%async_computation.1 | async-start | bytes 3670016 | tf_op jit(solution)/shard_map/all_to_all | solution.py:349
  24.3 2.4 %copy-start.1 = (bf16[8,128,576]{1,2,0:T(8,128)(2,1)S(1)}, bf16[8,128,576]{1,2,0:T(8,128)(2,1)}, u32[]{:S(2)}) copy-start(bf16[8,128,576]{1,2,0:T(8,128)(2,1)} %param.14) | copy-start | bytes 3538948
  26.8 0.7 copy-start
  28.1 1.6 %collective-permute-start = (bf16[4,64,512]{2,1,0:T(8,128)(2,1)S(1)}, bf16[4,64,512]{2,1,0:T(8,128)(2,1)S(1)}, u32[]{:S(2)}, u32[]{:S(2)}) collective-permute-start(bf16[4,64,512]{2,1,0:T(8,128)(2,1)S(1)} %get-tuple-element.21), channel_id=1, source_target_pairs={{0,16},{16,0},{32,48},{48,32},{64,80},{80,64},{96,112},{112,96},{1... | collective-permute-start | bytes 786440 | tf_op jit(solution)/shard_map/ppermute | solution.py:404
  29.7 18.0 %collective-permute-start.1 = (bf16[2,64,512]{2,1,0:T(8,128)(2,1)S(1)}, bf16[2,64,512]{2,1,0:T(8,128)(2,1)S(1)}, u32[]{:S(2)}, u32[]{:S(2)}) collective-permute-start(bf16[2,64,512]{2,1,0:T(8,128)(2,1)S(1)} %get-tuple-element.23), channel_id=1, source_target_pairs={{0,32},{16,48},{32,0},{48,16},{64,96},{80,112},{96,64},{112,80},{1... | collective-permute-start | bytes 393224 | tf_op jit(solution)/shard_map/ppermute | solution.py:404
  30.8 20.8 %collective-permute-start.2 = (bf16[2,64,512]{2,1,0:T(8,128)(2,1)S(1)}, bf16[2,64,512]{2,1,0:T(8,128)(2,1)S(1)}, u32[]{:S(2)}, u32[]{:S(2)}) collective-permute-start(bf16[2,64,512]{2,1,0:T(8,128)(2,1)S(1)} %get-tuple-element.24), channel_id=1, source_target_pairs={{0,64},{16,80},{32,96},{48,112},{64,0},{80,16},{96,32},{112,48},{1... | collective-permute-start | bytes 393224 | tf_op jit(solution)/shard_map/ppermute | solution.py:404
  33.4 18.2 %collective-permute-start.3 = (bf16[2,64,512]{2,1,0:T(8,128)(2,1)S(1)}, bf16[2,64,512]{2,1,0:T(8,128)(2,1)S(1)}, u32[]{:S(2)}, u32[]{:S(2)}) collective-permute-start(bf16[2,64,512]{2,1,0:T(8,128)(2,1)S(1)} %get-tuple-element.25), channel_id=1, source_target_pairs={{0,96},{16,112},{32,64},{48,80},{64,32},{80,48},{96,0},{112,16},{1... | collective-permute-start | bytes 393224 | tf_op jit(solution)/shard_map/ppermute | solution.py:404
  63.5 35.5 %all-to-all-start.2 = ((bf16[128,8,896]{2,1,0:T(8,128)(2,1)}), bf16[128,8,896]{2,1,0:T(8,128)(2,1)S(1)}, u32[]{:S(2)}, u32[]{:S(2)}) async-start(bf16[128,8,896]{2,1,0:T(8,128)(2,1)} %bitcast.25), calls=%async_computation.2 | async-start | bytes 3670016 | tf_op jit(solution)/shard_map/all_to_all | solution.py:349

commit v9 on v8

--- a/solution.py
+++ b/solution.py
@@ -280,7 +280,7 @@
 
 
 def land_kernel(plan, attended, handed, *rest):
-    arrived, out = rest[:-2], rest[-1]
+    arrived, out = rest[:-1], rest[-1]
     count = attended.shape[0]
     me = my_replica()
     for s in range(count):
@@ -418,12 +418,11 @@
         (10**6, 10**6),
     )(own, handed)
     landed = [swap(pair, 2 * n) for n, pair in enumerate(pairs, 1)]
-    *landed, incoming = lax.optimization_barrier((*landed, incoming))
     results = call(
         expert_kernel,
         [(lanes, width)],
         [VMEM] + [HBM] * 3,
-        (6 * devices * CAP * model * hidden, 6 * model * hidden),
+        (10**5, 10**5),
         [
             pltpu.VMEM((PARTS, width, hidden), BF16),
             pltpu.VMEM((PARTS, width, hidden), BF16),
@@ -436,13 +435,14 @@
         46,
         True,
     )(incoming, *in_hbm(w_gate, w_up, w_down))
+    *landed, results = lax.optimization_barrier((*landed, results))
     returned = exchange(results)
     attended_out = call(
         land_kernel,
         [(slots, HEADS, VDIM)],
-        [SMEM] + [VMEM] * (1 + chips) + [HBM],
+        [SMEM] + [VMEM] * (1 + chips),
         (10**6, 4 * 10**6),
-    )(plan, attended, handed, *landed, *in_hbm(results)).reshape(slots, HEADS * VDIM)
+    )(plan, attended, handed, *landed).reshape(slots, HEADS * VDIM)
     expert_out = call(combine_kernel, [(slots, model)], [VMEM] * 2, (2 * 10**8, 2 * 10**6))(
         gather, returned
     )

time: 101 us -> 95.8 us (0.949)
  starting transfers between devices: 26.9 us -> 23.1 us
  waiting for transfers between devices: 47.1 us -> 45.6 us
    ppermute x4, waiting for transfers between devices: 18.6 us -> 1.53 us  [swap(): lax.ppermute(values, 'replica', [(i, i ^ k) for i in range(replicas)])]
    all_to_all x2, waiting for transfers between devices: 24.8 us -> 40.4 us  [exchange(): lax.all_to_all(values, BOTH, split_axis=0, concat_axis=0, tiled=True)]
    all_to_all x2, starting transfers between devices: 17.7 us -> 13.9 us  [exchange(): lax.all_to_all(values, BOTH, split_axis=0, concat_axis=0, tiled=True)]
  transfers between devices with their start and end apart: 7 -> 7, of which waited for: 5 -> 4; matrix products, arithmetic and copies ran while one was open for 6% -> 6% of each run, Pallas kernels for 3% -> 16%
where the time goes in v9:
time: 95.8 us; the launch traced here: 95.4 us
  waiting for transfers between devices  45.6 us (48%)
  starting transfers between devices  23.1 us (24%)
  Pallas kernels  19.8 us (21%)
  matrix products  2.6 us (3%)
  local copies, waits for them, and re-layouts  2.47 us (3%)
  other arithmetic  1.04 us (1%)
    all_to_all x2, waiting for transfers between devices, exchange(): lax.all_to_all(values, BOTH, split_axis=0, concat_axis=0, tiled=True)  40.4 us
    all_to_all x2, starting transfers between devices, exchange(): lax.all_to_all(values, BOTH, split_axis=0, concat_axis=0, tiled=True)  13.9 us
    pallas_call x1, Pallas kernels, on_device(): call(expert_kernel, [(lanes, width)], [VMEM] + [HBM] * 3, (10 ** 5, 10 **...  11.9 us
    ppermute x4, starting transfers between devices, swap(): lax.ppermute(values, 'replica', [(i, i ^ k) for i in range(replicas)])  4.78 us
    all_to_all x1, starting transfers between devices, on_device(): lax.all_to_all(send.reshape(replicas, 8, width), 'replica', split_axis=0,...  4.4 us
    all_to_all x1, waiting for transfers between devices, on_device(): lax.all_to_all(send.reshape(replicas, 8, width), 'replica', split_axis=0,...  3.69 us
  transfers between devices with their start and end apart: 7, of which 4 were waited for; matrix products, arithmetic and copies ran while one was open for 6% of the time, Pallas kernels for 16%

profile of v9, /device:TPU:0, one launch (start us, length us, event | category | flops | bytes accessed | tf_op | source)
XLA Modules:
  0.0 95.4 jit_solution(11046524576276449758)
XLA Ops:
  0.6 1.7 %shard_map.132 = bf16[64,896]{1,0:T(8,128)(2,1)} custom-call(s32[8]{0:T(128)} %bitcast.21, s32[8]{0:T(128)} %length_hbm.3, s32[8]{0:T(128)} %finished_hbm.3, bf16[8,3584]{1,0:T(8,128)(2,1)} %tokens_hbm.3), custom_call_target="tpu_custom_call" | custom-call | flops 1000000 | bytes 100000 | tf_op jit(solution)/shard_map/pallas_call | solution.py:360
  2.3 4.4 %all-to-all-start = ((bf16[8,8,896]{2,1,0:T(8,128)(2,1)}), bf16[8,8,896]{2,1,0:T(8,128)(2,1)S(1)}, u32[]{:S(2)}, u32[]{:S(2)}) async-start(bf16[8,8,896]{2,1,0:T(8,128)(2,1)} %bitcast.28), calls=%async_computation | async-start | bytes 229376 | tf_op jit(solution)/shard_map/all_to_all | solution.py:373
  6.7 0.7 compare_convert_fusion
  7.4 0.1 iota_compare_fusion
  7.5 1.5 %shard_map.131 = (bf16[1024,128]{1,0:T(8,128)(2,1)S(1)}, bf16[128,1024]{1,0:T(8,128)(2,1)S(1)}, bf16[32,896]{1,0:T(8,128)(2,1)S(1)}) custom-call(s32[8]{0:T(128)} %bitcast.22, s32[8]{0:T(128)} %length_hbm.3, s32[8]{0:T(128)} %finished_hbm.3, s32[8,16]{1,0:T(8,128)} %bitcast.32, f32[8,16]{1,0:T(8,128)} %bitcast.33, bf16[8,3584]{1,0:T(8,128)(2,1)} %tokens_hbm.3), custom_call_target="tpu_custom_call" | custom-call | flops 10000000 | bytes 1000000 | tf_op jit(solution)/shard_map/pallas_call | solution.py:376
  9.0 3.7 %all-to-all-done = bf16[8,8,896]{2,1,0:T(8,128)(2,1)S(1)} async-done(((bf16[8,8,896]{2,1,0:T(8,128)(2,1)}), bf16[8,8,896]{2,1,0:T(8,128)(2,1)S(1)}, u32[]{:S(2)}, u32[]{:S(2)}) %all-to-all-start) | async-done | bytes 114720 | tf_op jit(solution)/shard_map/all_to_all | solution.py:373
  12.7 1.6 %shard_map.133 = bf16[1024,896]{1,0:T(8,128)(2,1)} custom-call(bf16[1024,128]{1,0:T(8,128)(2,1)S(1)} %get-tuple-element.17.scatter, bf16[32,896]{1,0:T(8,128)(2,1)S(1)} %get-tuple-element.18.tokens, bf16[64,896]{1,0:T(8,128)(2,1)S(1)} %bitcast.20), custom_call_target="tpu_custom_call" | custom-call | flops 200000000 | bytes 2000000 | tf_op jit(solution)/shard_map/pallas_call | solution.py:389
  14.3 0.0 copy-start.2
  14.3 0.0 copy-start.3
  14.3 9.2 %all-to-all-start.1 = ((bf16[128,8,896]{2,1,0:T(8,128)(2,1)}), bf16[128,8,896]{2,1,0:T(8,128)(2,1)S(1)}, u32[]{:S(2)}, u32[]{:S(2)}) async-start(bf16[128,8,896]{2,1,0:T(8,128)(2,1)} %bitcast.26), calls=%async_computation.1 | async-start | bytes 3670016 | tf_op jit(solution)/shard_map/all_to_all | solution.py:349
  23.5 0.8 reshape.61
  24.3 0.0 copy-start.1
  24.3 0.3 fusion.9
  24.6 1.8 %fusion.13 = (f32[8,64]{1,0:T(8,128)S(1)}, f32[8,64,128]{2,1,0:T(8,128)S(1)}) fusion(bf16[8,64,576]{2,1,0:T(8,128)(2,1)S(1)} %reshape.61, bf16[8,128,576]{1,2,0:T(8,128)(2,1)} %param.14, pred[8,128]{1,0:T(8,128)(4,1)S(1)} %iota_compare_fusion), kind=kOutput, calls=%fused_computation.21 | convolution fusion | flops 75693568 | bytes 2034688 | tf_op jit(solution)/shard_map/nhl,ntl->nht/dot_general | solution.py:33
  26.4 0.3 fusion.5
  26.8 0.0 copy-start
  26.8 0.5 fusion.2.attended
  27.3 0.1 copy-done
  27.4 0.6 shard_map.134
  28.1 0.1 collective-permute-start
  28.2 1.5 %collective-permute-done.handed = bf16[4,64,512]{2,1,0:T(8,128)(2,1)S(1)} collective-permute-done((bf16[4,64,512]{2,1,0:T(8,128)(2,1)S(1)}, bf16[4,64,512]{2,1,0:T(8,128)(2,1)S(1)}, u32[]{:S(2)}, u32[]{:S(2)}) %collective-permute-start) | collective-permute-done | bytes 262176 | tf_op jit(solution)/shard_map/ppermute | solution.py:404
  29.7 0.7 shard_map.135
  30.4 1.0 %collective-permute-start.1 = (bf16[2,64,512]{2,1,0:T(8,128)(2,1)}, bf16[2,64,512]{2,1,0:T(8,128)(2,1)S(1)}, u32[]{:S(2)}, u32[]{:S(2)}) collective-permute-start(bf16[2,64,512]{2,1,0:T(8,128)(2,1)} %get-tuple-element.23), channel_id=1, source_target_pairs={{0,32},{16,48},{32,0},{48,16},{64,96},{80,112},{96,64},{112,80},{1... | collective-permute-start | bytes 393224 | tf_op jit(solution)/shard_map/ppermute | solution.py:404
  31.3 2.7 %collective-permute-start.2 = (bf16[2,64,512]{2,1,0:T(8,128)(2,1)S(1)}, bf16[2,64,512]{2,1,0:T(8,128)(2,1)S(1)}, u32[]{:S(2)}, u32[]{:S(2)}) collective-permute-start(bf16[2,64,512]{2,1,0:T(8,128)(2,1)S(1)} %get-tuple-element.24), channel_id=1, source_target_pairs={{0,64},{16,80},{32,96},{48,112},{64,0},{80,16},{96,32},{112,48},{1... | collective-permute-start | bytes 393224 | tf_op jit(solution)/shard_map/ppermute | solution.py:404
  34.0 1.1 %collective-permute-start.3 = (bf16[2,64,512]{2,1,0:T(8,128)(2,1)S(1)}, bf16[2,64,512]{2,1,0:T(8,128)(2,1)S(1)}, u32[]{:S(2)}, u32[]{:S(2)}) collective-permute-start(bf16[2,64,512]{2,1,0:T(8,128)(2,1)S(1)} %get-tuple-element.25), channel_id=1, source_target_pairs={{0,96},{16,112},{32,64},{48,80},{64,32},{80,48},{96,0},{112,16},{1... | collective-permute-start | bytes 393224 | tf_op jit(solution)/shard_map/ppermute | solution.py:404
  35.1 15.5 %all-to-all-done.1 = bf16[128,8,896]{2,1,0:T(8,128)(2,1)S(1)} async-done(((bf16[128,8,896]{2,1,0:T(8,128)(2,1)}), bf16[128,8,896]{2,1,0:T(8,128)(2,1)S(1)}, u32[]{:S(2)}, u32[]{:S(2)}) %all-to-all-start.1) | async-done | bytes 1835040 | tf_op jit(solution)/shard_map/all_to_all | solution.py:349
  50.6 11.9 %shard_map.136 = bf16[1024,896]{1,0:T(8,128)(2,1)} custom-call(bf16[1024,896]{1,0:T(8,128)(2,1)S(1)} %bitcast.17, bf16[1,3584,1024]{2,1,0:T(8,128)(2,1)} %w_gate.1, bf16[1,3584,1024]{2,1,0:T(8,128)(2,1)} %w_up.1, bf16[1,1024,3584]{2,1,0:T(8,128)(2,1)} %w_down.1), custom_call_target="tpu_custom_call" | custom-call | flops 100000 | bytes 100000 | tf_op jit(solution)/shard_map/pallas_call | solution.py:421
  62.5 4.7 %all-to-all-start.2 = ((bf16[128,8,896]{2,1,0:T(8,128)(2,1)}), bf16[128,8,896]{2,1,0:T(8,128)(2,1)S(1)}, u32[]{:S(2)}, u32[]{:S(2)}) async-start(bf16[128,8,896]{2,1,0:T(8,128)(2,1)} %bitcast.25), calls=%async_computation.2 | async-start | bytes 3670016 | tf_op jit(solution)/shard_map/all_to_all | solution.py:349
  67.2 0.7 shard_map.137
  67.9 1.5 %copy.18 = bf16[2,8,64,512]{3,1,2,0:T(8,128)(2,1)} copy(bf16[2,8,64,512]{3,2,1,0:T(8,128)(2,1)S(1)} %bitcast.19) | data formatting | bytes 2097152
  69.4 24.8 %all-to-all-done.2 = bf16[128,8,896]{2,1,0:T(8,128)(2,1)S(1)} async-done(((bf16[128,8,896]{2,1,0:T(8,128)(2,1)}), bf16[128,8,896]{2,1,0:T(8,128)(2,1)S(1)}, u32[]{:S(2)}, u32[]{:S(2)}) %all-to-all-start.2) | async-done | bytes 1835040 | tf_op jit(solution)/shard_map/all_to_all | solution.py:349
  94.3 1.1 %shard_map.138 = bf16[16,3584]{1,0:T(8,128)(2,1)} custom-call(bf16[128,1024]{1,0:T(8,128)(2,1)S(1)} %get-tuple-element.30.gather, bf16[1024,896]{1,0:T(8,128)(2,1)S(1)} %bitcast.18), custom_call_target="tpu_custom_call" | custom-call | flops 200000000 | bytes 2000000 | tf_op jit(solution)/shard_map/pallas_call | solution.py:446
  (10 shorter events, 0.0 us)
Async XLA Ops:
  2.3 10.4 %all-to-all-start = ((bf16[8,8,896]{2,1,0:T(8,128)(2,1)}), bf16[8,8,896]{2,1,0:T(8,128)(2,1)S(1)}, u32[]{:S(2)}, u32[]{:S(2)}) async-start(bf16[8,8,896]{2,1,0:T(8,128)(2,1)} %bitcast.28), calls=%async_computation | async-start | bytes 229376 | tf_op jit(solution)/shard_map/all_to_all | solution.py:373
  14.3 9.2 %copy-start.2 = (bf16[8,36864]{1,0:T(8,128)(2,1)S(1)}, bf16[8,36864]{1,0:T(8,128)(2,1)}, u32[]{:S(2)}) copy-start(bf16[8,36864]{1,0:T(8,128)(2,1)} %param.13) | copy-start | bytes 1769476
  14.3 10.1 %copy-start.3 = (bf16[8,576]{1,0:T(8,128)(2,1)S(1)}, bf16[8,576]{1,0:T(8,128)(2,1)}, u32[]{:S(2)}) copy-start(bf16[8,576]{1,0:T(8,128)(2,1)} %param.15) | copy-start | bytes 27652
  14.3 36.3 %all-to-all-start.1 = ((bf16[128,8,896]{2,1,0:T(8,128)(2,1)}), bf16[128,8,896]{2,1,0:T(8,128)(2,1)S(1)}, u32[]{:S(2)}, u32[]{:S(2)}) async-start(bf16[128,8,896]{2,1,0:T(8,128)(2,1)} %bitcast.26), calls=%async_computation.1 | async-start | bytes 3670016 | tf_op jit(solution)/shard_map/all_to_all | solution.py:349
  24.3 2.4 %copy-start.1 = (bf16[8,128,576]{1,2,0:T(8,128)(2,1)S(1)}, bf16[8,128,576]{1,2,0:T(8,128)(2,1)}, u32[]{:S(2)}) copy-start(bf16[8,128,576]{1,2,0:T(8,128)(2,1)} %param.14) | copy-start | bytes 3538948
  26.8 0.7 copy-start
  28.1 1.6 %collective-permute-start = (bf16[4,64,512]{2,1,0:T(8,128)(2,1)S(1)}, bf16[4,64,512]{2,1,0:T(8,128)(2,1)S(1)}, u32[]{:S(2)}, u32[]{:S(2)}) collective-permute-start(bf16[4,64,512]{2,1,0:T(8,128)(2,1)S(1)} %get-tuple-element.21), channel_id=1, source_target_pairs={{0,16},{16,0},{32,48},{48,32},{64,80},{80,64},{96,112},{112,96},{1... | collective-permute-start | bytes 786440 | tf_op jit(solution)/shard_map/ppermute | solution.py:404
  30.4 32.1 %collective-permute-start.1 = (bf16[2,64,512]{2,1,0:T(8,128)(2,1)}, bf16[2,64,512]{2,1,0:T(8,128)(2,1)S(1)}, u32[]{:S(2)}, u32[]{:S(2)}) collective-permute-start(bf16[2,64,512]{2,1,0:T(8,128)(2,1)} %get-tuple-element.23), channel_id=1, source_target_pairs={{0,32},{16,48},{32,0},{48,16},{64,96},{80,112},{96,64},{112,80},{1... | collective-permute-start | bytes 393224 | tf_op jit(solution)/shard_map/ppermute | solution.py:404
  31.3 31.2 %collective-permute-start.2 = (bf16[2,64,512]{2,1,0:T(8,128)(2,1)S(1)}, bf16[2,64,512]{2,1,0:T(8,128)(2,1)S(1)}, u32[]{:S(2)}, u32[]{:S(2)}) collective-permute-start(bf16[2,64,512]{2,1,0:T(8,128)(2,1)S(1)} %get-tuple-element.24), channel_id=1, source_target_pairs={{0,64},{16,80},{32,96},{48,112},{64,0},{80,16},{96,32},{112,48},{1... | collective-permute-start | bytes 393224 | tf_op jit(solution)/shard_map/ppermute | solution.py:404
  34.0 28.5 %collective-permute-start.3 = (bf16[2,64,512]{2,1,0:T(8,128)(2,1)S(1)}, bf16[2,64,512]{2,1,0:T(8,128)(2,1)S(1)}, u32[]{:S(2)}, u32[]{:S(2)}) collective-permute-start(bf16[2,64,512]{2,1,0:T(8,128)(2,1)S(1)} %get-tuple-element.25), channel_id=1, source_target_pairs={{0,96},{16,112},{32,64},{48,80},{64,32},{80,48},{96,0},{112,16},{1... | collective-permute-start | bytes 393224 | tf_op jit(solution)/shard_map/ppermute | solution.py:404
  62.5 31.8 %all-to-all-start.2 = ((bf16[128,8,896]{2,1,0:T(8,128)(2,1)}), bf16[128,8,896]{2,1,0:T(8,128)(2,1)S(1)}, u32[]{:S(2)}, u32[]{:S(2)}) async-start(bf16[128,8,896]{2,1,0:T(8,128)(2,1)} %bitcast.25), calls=%async_computation.2 | async-start | bytes 3670016 | tf_op jit(solution)/shard_map/all_to_all | solution.py:349

commit v10 on v9

--- a/solution.py
+++ b/solution.py
@@ -83,8 +83,8 @@
     return jnp.concatenate(pieces, axis=0).astype(BF16)
 
 
-def pick_kernel(plan_hbm, length_hbm, finished_hbm, tokens_hbm, out, *scratch):
-    plan, length, finished, tokens, send, sems = scratch
+def pick_kernel(plan_hbm, length_hbm, finished_hbm, tokens_hbm, own, beside, *scratch):
+    plan, length, finished, tokens, sems = scratch
     pairs = [
         (plan_hbm, plan),
         (length_hbm, length),
@@ -93,16 +93,28 @@
     ]
     wait_all(start_all([pltpu.make_async_copy(*pair, sems.at[n]) for n, pair in enumerate(pairs)]))
     count = tokens.shape[0]
-    shape = (send.shape[0], PARTS * count)
+    height, width = own.shape
+    shape = (2 * height, PARTS * count)
     row, col = iota(shape, 0), iota(shape, 1)
     source = col & (count - 1)
-    wanted = by_index(row >> 3, send.shape[0] // 8, lambda d: plan[d])
+    place = row >> 3
+    chips = height // 8
+    step = (place & (chips - 1)) * 2 + jnp.where(place < chips, 0, 1)
+    wanted = by_index(step ^ my_replica(), 2 * chips, lambda d: plan[d])
     alive = by_index(source, count, alive_of(length, finished))
     chosen = (wanted == source) & ((row & 7) == (col >> 3)) & (alive > 0)
     chosen = jnp.where(chosen, 1.0, 0.0).astype(BF16)
-    flat = sub_rows(tokens[...], send.shape[1])
-    send[...] = jnp.dot(chosen, flat, preferred_element_type=F32).astype(BF16)
-    wait_all(start_all([pltpu.make_async_copy(send, out, sems.at[0])]))
+    flat = sub_rows(tokens[...], width)
+    picked = jnp.dot(chosen, flat, preferred_element_type=F32).astype(BF16)
+    own[...] = picked[:height]
+    beside[...] = picked[height:]
+
+
+def pair_tokens_kernel(own, handed, *outs):
+    mine, other = own[...].astype(F32), handed[...].astype(F32)
+    for n, out in enumerate(outs, 1):
+        part = slice(8 * n, 8 * n + 8)
+        out[...] = jnp.concatenate([mine[part], other[part]], axis=0).astype(BF16)
 
 
 def routing_kernel(plan_hbm, length_hbm, finished_hbm, routes_hbm, score_hbm, tokens_hbm, *rest):
@@ -152,8 +164,11 @@
     stays = (alive > 0) & (moved == 0)
     half = part[:count]
     pieces = [jnp.where(stays & (half == q), taken[:count], 0.0) for q in range(PARTS)]
-    for i in range(count):
-        pieces.append(jnp.where(half == row, taken[count + i : count + i + 1], 0.0))
+    swapped = iota((count, count), 1) == (iota((count, count), 0) ^ my_replica())
+    swapped = jnp.where(swapped, 1.0, 0.0).astype(BF16)
+    landed = jnp.dot(swapped, taken[count:].astype(BF16), preferred_element_type=F32)
+    for k in range(1, count):
+        pieces.append(jnp.where(half == row, landed[k : k + 1], 0.0))
     used = len(pieces) * count
     pieces.append(jnp.zeros((scatter.shape[1] - used, lanes), F32))
     scatter[...] = jnp.transpose(jnp.concatenate(pieces, axis=0)).astype(BF16)
@@ -165,10 +180,14 @@
     gather[...] = jnp.concatenate(pieces, axis=0).astype(BF16)
 
 
-def dispatch_kernel(scatter, tokens, arrived, out, block, sems):
+def dispatch_kernel(scatter, tokens, handed, *rest):
+    arrived, (out, block, sems) = rest[:-3], rest[-3:]
     lanes, width = out.shape
-    pad = scatter.shape[1] - tokens.shape[0] - arrived.shape[0]
-    flat = jnp.concatenate([tokens[...], arrived[...], jnp.zeros((pad, width), BF16)], axis=0)
+    pieces = [tokens[...].astype(F32), handed[...].astype(F32)[:8]]
+    pieces += [rows[...].astype(F32) for rows in arrived]
+    pad = scatter.shape[1] - sum(piece.shape[0] for piece in pieces)
+    pieces.append(jnp.zeros((pad, width), F32))
+    flat = jnp.concatenate(pieces, axis=0).astype(BF16)
     copies = []
     for b in range(lanes // 256):
         part = pl.ds(b * 256, 256)
@@ -357,22 +376,29 @@
         pltpu.SMEM((count,), jnp.int32),
         pltpu.SMEM((count,), jnp.int32),
     ]
-    send = call(
+    def swap(values, k):
+        return lax.ppermute(values, "replica", [(i, i ^ k) for i in range(replicas)])
+
+    chips = replicas // 2
+    tokens_own, tokens_beside = call(
         pick_kernel,
-        [(replicas * 8, width)],
+        [(chips * 8, width)] * 2,
         [HBM] * 4,
         (10**6, 10**5),
         integers
         + [
             pltpu.VMEM((count, model), BF16),
-            pltpu.VMEM((replicas * 8, width), BF16),
             pltpu.SemaphoreType.DMA((4,)),
         ],
-        in_hbm=True,
     )(*in_hbm(plan, lengths, finished, tokens))
-    arrived = lax.all_to_all(
-        send.reshape(replicas, 8, width), "replica", split_axis=0, concat_axis=0, tiled=True
-    ).reshape(replicas * 8, width)
+    tokens_handed = swap(tokens_beside, 1)
+    tokens_paired = call(
+        pair_tokens_kernel,
+        [(16, width)] * (chips - 1),
+        [VMEM] * 2,
+        (10**5, 10**5),
+    )(tokens_own, tokens_handed)
+    arrived = [swap(pair, 2 * n) for n, pair in enumerate(tokens_paired, 1)]
     scatter, gather, flat = call(
         routing_kernel,
         [(lanes, 128), (2 * PARTS * slots, lanes), (PARTS * count, width)],
@@ -389,21 +415,17 @@
     outgoing = call(
         dispatch_kernel,
         [(lanes, width)],
-        [VMEM] * 3,
+        [VMEM] * (2 + chips),
         (2 * 10**8, 2 * 10**6),
         [pltpu.VMEM((lanes, width), BF16), pltpu.SemaphoreType.DMA((lanes // 256,))],
         in_hbm=True,
-    )(scatter, flat, arrived)
+    )(scatter, flat, tokens_handed, *arrived)
     own_length = jnp.where(finished == 0, lengths, 0)
     held = lax.optimization_barrier((queries, new_latent, outgoing))
     queries, new_latent, outgoing = held
     incoming = exchange(outgoing)
 
     attended = attend(queries, latent_cache, new_latent, own_length)
-    def swap(values, k):
-        return lax.ppermute(values, "replica", [(i, i ^ k) for i in range(replicas)])
-
-    chips = replicas // 2
     own, beside = call(
         leave_kernel,
         [(chips, HEADS, VDIM)] * 2,

time: 95.8 us -> 95 us (level)
    ppermute x4 -> x8, starting transfers between devices: 4.78 us -> 9.65 us  [swap(): lax.ppermute(values, 'replica', [(i, i ^ k) for i in range(replicas)])]
    all_to_all x1 -> x0, starting transfers between devices: 4.4 us -> none  [on_device(): lax.all_to_all(send.reshape(replicas, 8, width), 'replica', split_axis=0,...]
    all_to_all x1 -> x0, waiting for transfers between devices: 3.69 us -> none  [on_device(): lax.all_to_all(send.reshape(replicas, 8, width), 'replica', split_axis=0,...]
    ppermute x4 -> x8, waiting for transfers between devices: 1.53 us -> 5.09 us  [swap(): lax.ppermute(values, 'replica', [(i, i ^ k) for i in range(replicas)])]
    pallas_call x2 -> x3, Pallas kernels: 3.27 us -> 2.62 us  [the longest x1 1.57 us: on_device(): call(dispatch_kernel, [(lanes, width)], [VMEM] * (2 + chips), (2 * 10 **...]
  transfers between devices with their start and end apart: 7 -> 10, of which waited for: 4 -> 6; matrix products, arithmetic and copies ran while one was open for 6% -> 6% of each run, Pallas kernels for 16% -> 16%
where the time goes in v10:
time: 95 us; the launch traced here: 94.6 us
  waiting for transfers between devices  45.4 us (48%)
  starting transfers between devices  22.9 us (24%)
  Pallas kernels  19.2 us (20%)
  matrix products  2.59 us (3%)
  local copies, waits for them, and re-layouts  2.48 us (3%)
  other arithmetic  1.04 us (1%)
    all_to_all x2, waiting for transfers between devices, exchange(): lax.all_to_all(values, BOTH, split_axis=0, concat_axis=0, tiled=True)  40.4 us
    all_to_all x2, starting transfers between devices, exchange(): lax.all_to_all(values, BOTH, split_axis=0, concat_axis=0, tiled=True)  13.3 us
    pallas_call x1, Pallas kernels, on_device(): call(expert_kernel, [(lanes, width)], [VMEM] + [HBM] * 3, (10 ** 5, 10 **...  11.9 us
    ppermute x8, starting transfers between devices, swap(): lax.ppermute(values, 'replica', [(i, i ^ k) for i in range(replicas)])  9.65 us
    ppermute x8, waiting for transfers between devices, swap(): lax.ppermute(values, 'replica', [(i, i ^ k) for i in range(replicas)])  5.09 us
  transfers between devices with their start and end apart: 10, of which 6 were waited for; matrix products, arithmetic and copies ran while one was open for 6% of the time, Pallas kernels for 16%

profile of v10, /device:TPU:0, one launch (start us, length us, event | category | flops | bytes accessed | tf_op | source)
XLA Modules:
  0.0 94.6 jit_solution(15163131165508213406)
XLA Ops:
  0.6 1.0 %shard_map.132 = (bf16[32,896]{1,0:T(8,128)(2,1)S(1)}, bf16[32,896]{1,0:T(8,128)(2,1)S(1)}) custom-call(s32[8]{0:T(128)} %bitcast.18, s32[8]{0:T(128)} %length_hbm.3, s32[8]{0:T(128)} %finished_hbm.3, bf16[8,3584]{1,0:T(8,128)(2,1)} %tokens_hbm.3), custom_call_target="tpu_custom_call" | custom-call | flops 1000000 | bytes 100000 | tf_op jit(solution)/shard_map/pallas_call | solution.py:383
  1.7 0.1 collective-permute-start
  1.8 0.7 compare_convert_fusion
  2.4 0.6 collective-permute-done.handed
  3.0 1.7 %collective-permute-start.1 = (bf16[16,896]{1,0:T(8,128)(2,1)S(1)}, bf16[16,896]{1,0:T(8,128)(2,1)S(1)}, u32[]{:S(2)}, u32[]{:S(2)}) collective-permute-start(bf16[16,896]{1,0:T(8,128)(2,1)S(1)} %get-tuple-element.26), channel_id=1, source_target_pairs={{0,32},{16,48},{32,0},{48,16},{64,96},{80,112},{96,64},{112,80},{1... | collective-permute-start | bytes 86024 | tf_op jit(solution)/shard_map/ppermute | solution.py:380
  4.7 2.7 %collective-permute-start.2 = (bf16[16,896]{1,0:T(8,128)(2,1)S(1)}, bf16[16,896]{1,0:T(8,128)(2,1)S(1)}, u32[]{:S(2)}, u32[]{:S(2)}) collective-permute-start(bf16[16,896]{1,0:T(8,128)(2,1)S(1)} %get-tuple-element.27), channel_id=1, source_target_pairs={{0,64},{16,80},{32,96},{48,112},{64,0},{80,16},{96,32},{112,48},{1... | collective-permute-start | bytes 86024 | tf_op jit(solution)/shard_map/ppermute | solution.py:380
  7.4 0.4 collective-permute-start.3
  7.9 1.6 %shard_map.131 = (bf16[1024,128]{1,0:T(8,128)(2,1)S(1)}, bf16[128,1024]{1,0:T(8,128)(2,1)S(1)}, bf16[32,896]{1,0:T(8,128)(2,1)S(1)}) custom-call(s32[8]{0:T(128)} %bitcast.19, s32[8]{0:T(128)} %length_hbm.3, s32[8]{0:T(128)} %finished_hbm.3, s32[8,16]{1,0:T(8,128)} %bitcast.28, f32[8,16]{1,0:T(8,128)} %bitcast.29, bf16[8,3584]{1,0:T(8,128)(2,1)} %tokens_hbm.3), custom_call_target="tpu_custom_call" | custom-call | flops 10000000 | bytes 1000000 | tf_op jit(solution)/shard_map/pallas_call | solution.py:402
  9.5 0.6 collective-permute-done.2.rest_1_
  10.0 2.4 %collective-permute-done.3.rest_2_ = bf16[16,896]{1,0:T(8,128)(2,1)S(1)} collective-permute-done((bf16[16,896]{1,0:T(8,128)(2,1)S(1)}, bf16[16,896]{1,0:T(8,128)(2,1)S(1)}, u32[]{:S(2)}, u32[]{:S(2)}) %collective-permute-start.3) | collective-permute-done | bytes 28704 | tf_op jit(solution)/shard_map/ppermute | solution.py:380
  12.5 1.6 %shard_map.134 = bf16[1024,896]{1,0:T(8,128)(2,1)} custom-call(bf16[1024,128]{1,0:T(8,128)(2,1)S(1)} %get-tuple-element.22.scatter, bf16[32,896]{1,0:T(8,128)(2,1)S(1)} %get-tuple-element.23.tokens, bf16[32,896]{1,0:T(8,128)(2,1)S(1)} %collective-permute-done.handed, bf16[16,896]{1,0:T(8,128)(2,1)S(1)} %collective-permute-done.1.rest_0_, ...), custom_call_target="tpu_custom_call" | custom-call | flops 200000000 | bytes 2000000 | tf_op jit(solution)/shard_map/pallas_call | solution.py:415
  14.1 8.6 %all-to-all-start = ((bf16[128,8,896]{2,1,0:T(8,128)(2,1)}), bf16[128,8,896]{2,1,0:T(8,128)(2,1)S(1)}, u32[]{:S(2)}, u32[]{:S(2)}) async-start(bf16[128,8,896]{2,1,0:T(8,128)(2,1)} %bitcast.23), calls=%async_computation | async-start | bytes 3670016 | tf_op jit(solution)/shard_map/all_to_all | solution.py:368
  22.7 0.8 reshape.53
  23.5 0.3 fusion.9
  23.8 1.8 %fusion.13 = (f32[8,64]{1,0:T(8,128)S(1)}, f32[8,64,128]{2,1,0:T(8,128)S(1)}) fusion(bf16[8,64,576]{2,1,0:T(8,128)(2,1)S(1)} %reshape.53, bf16[8,128,576]{1,2,0:T(8,128)(2,1)} %param.14, pred[8,128]{1,0:T(8,128)(4,1)S(1)} %iota_compare_fusion), kind=kOutput, calls=%fused_computation.21 | convolution fusion | flops 75693568 | bytes 2034688 | tf_op jit(solution)/shard_map/nhl,ntl->nht/dot_general | solution.py:33
  25.6 0.3 fusion.5
  26.0 0.5 fusion.2.attended
  26.5 0.1 copy-done
  26.6 0.6 shard_map.135
  27.2 0.1 collective-permute-start.4
  27.3 1.5 %collective-permute-done.4.handed = bf16[4,64,512]{2,1,0:T(8,128)(2,1)S(1)} collective-permute-done((bf16[4,64,512]{2,1,0:T(8,128)(2,1)S(1)}, bf16[4,64,512]{2,1,0:T(8,128)(2,1)S(1)}, u32[]{:S(2)}, u32[]{:S(2)}) %collective-permute-start.4) | collective-permute-done | bytes 262176 | tf_op jit(solution)/shard_map/ppermute | solution.py:380
  28.9 0.7 shard_map.136
  29.5 1.0 %collective-permute-start.5 = (bf16[2,64,512]{2,1,0:T(8,128)(2,1)}, bf16[2,64,512]{2,1,0:T(8,128)(2,1)S(1)}, u32[]{:S(2)}, u32[]{:S(2)}) collective-permute-start(bf16[2,64,512]{2,1,0:T(8,128)(2,1)} %get-tuple-element.33), channel_id=1, source_target_pairs={{0,32},{16,48},{32,0},{48,16},{64,96},{80,112},{96,64},{112,80},{1... | collective-permute-start | bytes 393224 | tf_op jit(solution)/shard_map/ppermute | solution.py:380
  30.5 2.7 %collective-permute-start.6 = (bf16[2,64,512]{2,1,0:T(8,128)(2,1)S(1)}, bf16[2,64,512]{2,1,0:T(8,128)(2,1)S(1)}, u32[]{:S(2)}, u32[]{:S(2)}) collective-permute-start(bf16[2,64,512]{2,1,0:T(8,128)(2,1)S(1)} %get-tuple-element.34), channel_id=1, source_target_pairs={{0,64},{16,80},{32,96},{48,112},{64,0},{80,16},{96,32},{112,48},{1... | collective-permute-start | bytes 393224 | tf_op jit(solution)/shard_map/ppermute | solution.py:380
  33.2 1.1 %collective-permute-start.7 = (bf16[2,64,512]{2,1,0:T(8,128)(2,1)S(1)}, bf16[2,64,512]{2,1,0:T(8,128)(2,1)S(1)}, u32[]{:S(2)}, u32[]{:S(2)}) collective-permute-start(bf16[2,64,512]{2,1,0:T(8,128)(2,1)S(1)} %get-tuple-element.35), channel_id=1, source_target_pairs={{0,96},{16,112},{32,64},{48,80},{64,32},{80,48},{96,0},{112,16},{1... | collective-permute-start | bytes 393224 | tf_op jit(solution)/shard_map/ppermute | solution.py:380
  34.2 15.5 %all-to-all-done = bf16[128,8,896]{2,1,0:T(8,128)(2,1)S(1)} async-done(((bf16[128,8,896]{2,1,0:T(8,128)(2,1)}), bf16[128,8,896]{2,1,0:T(8,128)(2,1)S(1)}, u32[]{:S(2)}, u32[]{:S(2)}) %all-to-all-start) | async-done | bytes 1835040 | tf_op jit(solution)/shard_map/all_to_all | solution.py:368
  49.8 11.9 %shard_map.137 = bf16[1024,896]{1,0:T(8,128)(2,1)} custom-call(bf16[1024,896]{1,0:T(8,128)(2,1)S(1)} %bitcast.15, bf16[1,3584,1024]{2,1,0:T(8,128)(2,1)} %w_gate.1, bf16[1,3584,1024]{2,1,0:T(8,128)(2,1)} %w_up.1, bf16[1,1024,3584]{2,1,0:T(8,128)(2,1)} %w_down.1), custom_call_target="tpu_custom_call" | custom-call | flops 100000 | bytes 100000 | tf_op jit(solution)/shard_map/pallas_call | solution.py:443
  61.7 4.7 %all-to-all-start.1 = ((bf16[128,8,896]{2,1,0:T(8,128)(2,1)}), bf16[128,8,896]{2,1,0:T(8,128)(2,1)S(1)}, u32[]{:S(2)}, u32[]{:S(2)}) async-start(bf16[128,8,896]{2,1,0:T(8,128)(2,1)} %bitcast.22), calls=%async_computation.1 | async-start | bytes 3670016 | tf_op jit(solution)/shard_map/all_to_all | solution.py:368
  66.4 0.7 shard_map.138
  67.1 1.5 %copy.18 = bf16[2,8,64,512]{3,1,2,0:T(8,128)(2,1)} copy(bf16[2,8,64,512]{3,2,1,0:T(8,128)(2,1)S(1)} %bitcast.17) | data formatting | bytes 2097152
  68.6 24.8 %all-to-all-done.1 = bf16[128,8,896]{2,1,0:T(8,128)(2,1)S(1)} async-done(((bf16[128,8,896]{2,1,0:T(8,128)(2,1)}), bf16[128,8,896]{2,1,0:T(8,128)(2,1)S(1)}, u32[]{:S(2)}, u32[]{:S(2)}) %all-to-all-start.1) | async-done | bytes 1835040 | tf_op jit(solution)/shard_map/all_to_all | solution.py:368
  93.5 1.1 %shard_map.139 = bf16[16,3584]{1,0:T(8,128)(2,1)} custom-call(bf16[128,1024]{1,0:T(8,128)(2,1)S(1)} %get-tuple-element.40.gather, bf16[1024,896]{1,0:T(8,128)(2,1)S(1)} %bitcast.16), custom_call_target="tpu_custom_call" | custom-call | flops 200000000 | bytes 2000000 | tf_op jit(solution)/shard_map/pallas_call | solution.py:468
  (17 shorter events, 0.1 us)
Async XLA Ops:
  1.7 1.3 %collective-permute-start = (bf16[32,896]{1,0:T(8,128)(2,1)S(1)}, bf16[32,896]{1,0:T(8,128)(2,1)S(1)}, u32[]{:S(2)}, u32[]{:S(2)}) collective-permute-start(bf16[32,896]{1,0:T(8,128)(2,1)S(1)} %get-tuple-element.24), channel_id=1, source_target_pairs={{0,16},{16,0},{32,48},{48,32},{64,80},{80,64},{96,112},{112,96},{1... | collective-permute-start | bytes 172040 | tf_op jit(solution)/shard_map/ppermute | solution.py:380
  3.0 6.5 %collective-permute-start.1 = (bf16[16,896]{1,0:T(8,128)(2,1)S(1)}, bf16[16,896]{1,0:T(8,128)(2,1)S(1)}, u32[]{:S(2)}, u32[]{:S(2)}) collective-permute-start(bf16[16,896]{1,0:T(8,128)(2,1)S(1)} %get-tuple-element.26), channel_id=1, source_target_pairs={{0,32},{16,48},{32,0},{48,16},{64,96},{80,112},{96,64},{112,80},{1... | collective-permute-start | bytes 86024 | tf_op jit(solution)/shard_map/ppermute | solution.py:380
  4.7 5.4 %collective-permute-start.2 = (bf16[16,896]{1,0:T(8,128)(2,1)S(1)}, bf16[16,896]{1,0:T(8,128)(2,1)S(1)}, u32[]{:S(2)}, u32[]{:S(2)}) collective-permute-start(bf16[16,896]{1,0:T(8,128)(2,1)S(1)} %get-tuple-element.27), channel_id=1, source_target_pairs={{0,64},{16,80},{32,96},{48,112},{64,0},{80,16},{96,32},{112,48},{1... | collective-permute-start | bytes 86024 | tf_op jit(solution)/shard_map/ppermute | solution.py:380
  7.4 5.1 %collective-permute-start.3 = (bf16[16,896]{1,0:T(8,128)(2,1)S(1)}, bf16[16,896]{1,0:T(8,128)(2,1)S(1)}, u32[]{:S(2)}, u32[]{:S(2)}) collective-permute-start(bf16[16,896]{1,0:T(8,128)(2,1)S(1)} %get-tuple-element.28), channel_id=1, source_target_pairs={{0,96},{16,112},{32,64},{48,80},{64,32},{80,48},{96,0},{112,16},{1... | collective-permute-start | bytes 86024 | tf_op jit(solution)/shard_map/ppermute | solution.py:380
  14.1 8.6 %copy-start.2 = (bf16[8,36864]{1,0:T(8,128)(2,1)S(1)}, bf16[8,36864]{1,0:T(8,128)(2,1)}, u32[]{:S(2)}) copy-start(bf16[8,36864]{1,0:T(8,128)(2,1)} %param.13) | copy-start | bytes 1769476
  14.1 9.5 %copy-start.3 = (bf16[8,576]{1,0:T(8,128)(2,1)S(1)}, bf16[8,576]{1,0:T(8,128)(2,1)}, u32[]{:S(2)}) copy-start(bf16[8,576]{1,0:T(8,128)(2,1)} %param.15) | copy-start | bytes 27652
  14.1 35.7 %all-to-all-start = ((bf16[128,8,896]{2,1,0:T(8,128)(2,1)}), bf16[128,8,896]{2,1,0:T(8,128)(2,1)S(1)}, u32[]{:S(2)}, u32[]{:S(2)}) async-start(bf16[128,8,896]{2,1,0:T(8,128)(2,1)} %bitcast.23), calls=%async_computation | async-start | bytes 3670016 | tf_op jit(solution)/shard_map/all_to_all | solution.py:368
  23.5 2.4 %copy-start.1 = (bf16[8,128,576]{1,2,0:T(8,128)(2,1)S(1)}, bf16[8,128,576]{1,2,0:T(8,128)(2,1)}, u32[]{:S(2)}) copy-start(bf16[8,128,576]{1,2,0:T(8,128)(2,1)} %param.14) | copy-start | bytes 3538948
  25.9 0.7 copy-start
  27.2 1.6 %collective-permute-start.4 = (bf16[4,64,512]{2,1,0:T(8,128)(2,1)S(1)}, bf16[4,64,512]{2,1,0:T(8,128)(2,1)S(1)}, u32[]{:S(2)}, u32[]{:S(2)}) collective-permute-start(bf16[4,64,512]{2,1,0:T(8,128)(2,1)S(1)} %get-tuple-element.31), channel_id=1, source_target_pairs={{0,16},{16,0},{32,48},{48,32},{64,80},{80,64},{96,112},{112,96},{1... | collective-permute-start | bytes 786440 | tf_op jit(solution)/shard_map/ppermute | solution.py:380
  29.5 32.1 %collective-permute-start.5 = (bf16[2,64,512]{2,1,0:T(8,128)(2,1)}, bf16[2,64,512]{2,1,0:T(8,128)(2,1)S(1)}, u32[]{:S(2)}, u32[]{:S(2)}) collective-permute-start(bf16[2,64,512]{2,1,0:T(8,128)(2,1)} %get-tuple-element.33), channel_id=1, source_target_pairs={{0,32},{16,48},{32,0},{48,16},{64,96},{80,112},{96,64},{112,80},{1... | collective-permute-start | bytes 393224 | tf_op jit(solution)/shard_map/ppermute | solution.py:380
  30.5 31.2 %collective-permute-start.6 = (bf16[2,64,512]{2,1,0:T(8,128)(2,1)S(1)}, bf16[2,64,512]{2,1,0:T(8,128)(2,1)S(1)}, u32[]{:S(2)}, u32[]{:S(2)}) collective-permute-start(bf16[2,64,512]{2,1,0:T(8,128)(2,1)S(1)} %get-tuple-element.34), channel_id=1, source_target_pairs={{0,64},{16,80},{32,96},{48,112},{64,0},{80,16},{96,32},{112,48},{1... | collective-permute-start | bytes 393224 | tf_op jit(solution)/shard_map/ppermute | solution.py:380
  33.2 28.5 %collective-permute-start.7 = (bf16[2,64,512]{2,1,0:T(8,128)(2,1)S(1)}, bf16[2,64,512]{2,1,0:T(8,128)(2,1)S(1)}, u32[]{:S(2)}, u32[]{:S(2)}) collective-permute-start(bf16[2,64,512]{2,1,0:T(8,128)(2,1)S(1)} %get-tuple-element.35), channel_id=1, source_target_pairs={{0,96},{16,112},{32,64},{48,80},{64,32},{80,48},{96,0},{112,16},{1... | collective-permute-start | bytes 393224 | tf_op jit(solution)/shard_map/ppermute | solution.py:380
  61.7 31.8 %all-to-all-start.1 = ((bf16[128,8,896]{2,1,0:T(8,128)(2,1)}), bf16[128,8,896]{2,1,0:T(8,128)(2,1)S(1)}, u32[]{:S(2)}, u32[]{:S(2)}) async-start(bf16[128,8,896]{2,1,0:T(8,128)(2,1)} %bitcast.22), calls=%async_computation.1 | async-start | bytes 3670016 | tf_op jit(solution)/shard_map/all_to_all | solution.py:368
